TPU v7x, 32 devices: a whole 2x2x4 slice. The times are simulated.
32 devices in a mesh: dp: 8 (over z, y), fsdp: 4 (over x, core).
Axes of the slice: x: 2, y: 2, z: 4, core: 2. Of those that a mesh axis runs over, the one named last changes fastest.
Arguments:
- inputs: bfloat16 [32768, 512], P(('dp', 'fsdp')), may hold values from -6 to 6
- memory: bfloat16 [65536, 512], P(('dp', 'fsdp')), may hold values from -6 to 6
- seg_lengths: int32 [32, 16], P(('dp', 'fsdp')), may hold values from 1 to 256, 1024 in all within a row
- mem_lengths: int32 [32, 17], P(('dp', 'fsdp')), may hold values from 1 to 256, 2048 in all within a row
- self_query: bfloat16 [262144], P(('dp', 'fsdp')), may hold values from -0.25 to 0.25
- self_key: bfloat16 [262144], P(('dp', 'fsdp')), may hold values from -0.25 to 0.25
- self_value: bfloat16 [262144], P(('dp', 'fsdp')), may hold values from -0.25 to 0.25
- self_out: bfloat16 [262144], P(('dp', 'fsdp')), may hold values from -1 to 1
- cross_query: bfloat16 [262144], P(('dp', 'fsdp')), may hold values from -0.25 to 0.25
- cross_key: bfloat16 [262144], P(('dp', 'fsdp')), may hold values from -0.25 to 0.25
- cross_value: bfloat16 [262144], P(('dp', 'fsdp')), may hold values from -0.25 to 0.25
- cross_out: bfloat16 [262144], P(('dp', 'fsdp')), may hold values from -1 to 1
- ffn_in: bfloat16 [1048576], P(('dp', 'fsdp')), may hold values from -0.25 to 0.25
- ffn_out: bfloat16 [1048576], P(('dp', 'fsdp')), may hold values from -0.125 to 0.125
- norm_params: float32 [3072], P(('dp', 'fsdp')), may hold values from -1.2 to 1.45
- cotangent: bfloat16 [32768, 512], P(('dp', 'fsdp')), may hold values from -6 to 6
Outputs:
- block_output: bfloat16 [32768, 512], P(('dp', 'fsdp'))
- grad_inputs: bfloat16 [32768, 512], P(('dp', 'fsdp'))
- grad_memory: bfloat16 [65536, 512], P(('dp', 'fsdp'))
- grad_self_query: float32 [262144], P(('dp', 'fsdp'))
- grad_self_key: float32 [262144], P(('dp', 'fsdp'))
- grad_self_value: float32 [262144], P(('dp', 'fsdp'))
- grad_self_out: float32 [262144], P(('dp', 'fsdp'))
- grad_cross_query: float32 [262144], P(('dp', 'fsdp'))
- grad_cross_key: float32 [262144], P(('dp', 'fsdp'))
- grad_cross_value: float32 [262144], P(('dp', 'fsdp'))
- grad_cross_out: float32 [262144], P(('dp', 'fsdp'))
- grad_ffn_in: float32 [1048576], P(('dp', 'fsdp'))
- grad_ffn_out: float32 [1048576], P(('dp', 'fsdp'))
- grad_norm_params: float32 [3072], P(('dp', 'fsdp'))
Inputs may be any that keep to these rules, and one draw needn't show every extreme that they name: `seg_lengths`: each row sums to 1024. `mem_lengths`: each row sums to 2048; the last entry counts padding rows at the end of the stream's memory.
All inputs are finite; a program needn't handle non-finite values.
Results may differ from a plain program's by a relative error of at most 0.03.
Values may be sent and summed in bfloat16 or wider, within the bound.
No kernel may reach another device: no remote copies, remote signals or barrier semaphores. Data moves between devices by JAX's collectives and lax.ppermute only.
A program may use at most 256 MiB of HBM per device.

v0:
```python
import jax
import jax.numpy as jnp
from jax import lax
from jax.sharding import PartitionSpec as P

HD = 64


masked_score = -1e30
norm_eps = 1e-05


def layer_norm(source, gain_row, shift_row):
    row_mean = jnp.mean(source, axis=-1, keepdims=True)
    centered = source - row_mean
    variance = jnp.mean(centered * centered, axis=-1, keepdims=True)
    return centered * lax.rsqrt(variance + norm_eps) * gain_row + shift_row


def gelu_tanh(source):
    return (
        0.5
        * source
        * (1.0 + jnp.tanh(0.7978845608028654 * (source + 0.044715 * source * source * source)))
    )


def segment_ids(lengths, row_count):
    ends = jnp.cumsum(lengths)
    places = jnp.arange(row_count, dtype=jnp.int32)
    return jnp.sum((places[:, None] >= ends[None, :]).astype(jnp.int32), axis=1)


def project(left, right):
    return jnp.dot(left, right, preferred_element_type=jnp.float32)


def project_back(grad_rows, weight):
    return lax.dot_general(
        grad_rows, weight, (((1,), (1,)), ((), ())), preferred_element_type=jnp.float32
    )


def weight_grad(left, grad_rows):
    return lax.dot_general(
        left, grad_rows, (((0,), (0,)), ((), ())), preferred_element_type=jnp.float32
    )


def block_scores(query_block, keys, ids_block, places_block, key_ids, causal):
    score_scale = query_block.shape[-1] ** (-0.5)
    scores = (
        jnp.einsum("thd,shd->hts", query_block, keys, preferred_element_type=jnp.float32)
        * score_scale
    )
    allowed = ids_block[:, None] == key_ids[None, :]
    if causal:
        key_places = jnp.arange(keys.shape[0], dtype=jnp.int32)
        allowed = allowed & (key_places[None, :] <= places_block[:, None])
    return jnp.where(allowed[None], scores, masked_score)


def attend_forward(queries, keys, values, query_ids, key_ids, causal):
    row_count, head_count, head_size = queries.shape
    block_rows = min(512, row_count)
    block_count = row_count // block_rows
    places = jnp.arange(row_count, dtype=jnp.int32)

    def one_block(pieces):
        query_block, ids_block, places_block = pieces
        scores = block_scores(query_block, keys, ids_block, places_block, key_ids, causal)
        row_max = jnp.max(scores, axis=-1, keepdims=True)
        raised = jnp.exp(scores - row_max)
        row_total = jnp.sum(raised, axis=-1, keepdims=True)
        weights = (raised / row_total).astype(jnp.bfloat16)
        mixed = jnp.einsum("hts,shd->thd", weights, values, preferred_element_type=jnp.float32)
        return (mixed.astype(jnp.bfloat16), (row_max + jnp.log(row_total))[..., 0])

    mixed, log_totals = lax.map(
        one_block,
        (
            queries.reshape(block_count, block_rows, head_count, head_size),
            query_ids.reshape(block_count, block_rows),
            places.reshape(block_count, block_rows),
        ),
    )
    return (mixed.reshape(row_count, head_count * head_size), log_totals)


def attend_backward(queries, keys, values, query_ids, key_ids, log_totals, grad_mixed, causal):
    row_count, head_count, head_size = queries.shape
    block_rows = min(512, row_count)
    block_count = row_count // block_rows
    places = jnp.arange(row_count, dtype=jnp.int32)
    score_scale = head_size ** (-0.5)

    def one_block(carried, pieces):
        key_grad, value_grad = carried
        query_block, ids_block, places_block, totals_block, grad_block = pieces
        scores = block_scores(query_block, keys, ids_block, places_block, key_ids, causal)
        weights = jnp.exp(scores - totals_block[..., None])
        grad_weights = jnp.einsum(
            "thd,shd->hts", grad_block, values, preferred_element_type=jnp.float32
        )
        inner = jnp.sum(weights * grad_weights, axis=-1, keepdims=True)
        grad_scores = (weights * (grad_weights - inner)).astype(jnp.bfloat16)
        query_grad = (
            jnp.einsum("hts,shd->thd", grad_scores, keys, preferred_element_type=jnp.float32)
            * score_scale
        )
        key_grad = (
            key_grad
            + jnp.einsum(
                "hts,thd->shd", grad_scores, query_block, preferred_element_type=jnp.float32
            )
            * score_scale
        )
        value_grad = value_grad + jnp.einsum(
            "hts,thd->shd",
            weights.astype(jnp.bfloat16),
            grad_block,
            preferred_element_type=jnp.float32,
        )
        return ((key_grad, value_grad), query_grad.astype(jnp.bfloat16))

    empty = jnp.zeros(keys.shape, jnp.float32)
    (key_grad, value_grad), query_grad = lax.scan(
        one_block,
        (empty, empty),
        (
            queries.reshape(block_count, block_rows, head_count, head_size),
            query_ids.reshape(block_count, block_rows),
            places.reshape(block_count, block_rows),
            log_totals,
            grad_mixed.reshape(block_count, block_rows, head_count, head_size),
        ),
    )
    flat_width = head_count * head_size
    return (
        query_grad.reshape(row_count, flat_width),
        key_grad.astype(jnp.bfloat16).reshape(-1, flat_width),
        value_grad.astype(jnp.bfloat16).reshape(-1, flat_width),
    )


def norm_backward(residual, gain_row, shift_row, incoming):
    pullback = jax.vjp(layer_norm, residual, gain_row, shift_row)[1]
    return pullback(incoming)


def body(
    inputs,
    memory,
    seg_lengths,
    mem_lengths,
    self_query,
    self_key,
    self_value,
    self_out,
    cross_query,
    cross_key,
    cross_value,
    cross_out,
    ffn_in,
    ffn_out,
    norm_params,
    cotangent,
):
    row_count, model_width = inputs.shape
    head_count = model_width // HD
    query_ids = segment_ids(seg_lengths[0], row_count)
    memory_ids = segment_ids(mem_lengths[0], memory.shape[0])

    def square(flat):
        return flat.reshape(model_width, -1)

    def heads_view(source):
        return source.reshape(source.shape[0], head_count, HD)

    self_full = (
        lax.all_gather(self_query, ("dp", "fsdp"), axis=0, tiled=True),
        lax.all_gather(self_key, ("dp", "fsdp"), axis=0, tiled=True),
        lax.all_gather(self_value, ("dp", "fsdp"), axis=0, tiled=True),
        lax.all_gather(self_out, ("dp", "fsdp"), axis=0, tiled=True),
        lax.all_gather(norm_params.astype(jnp.bfloat16), ("dp", "fsdp"), axis=0, tiled=True).astype(
            norm_params.dtype
        ),
    )
    self_query_full = square(self_full[0])
    self_key_full = square(self_full[1])
    self_value_full = square(self_full[2])
    self_out_full = square(self_full[3])
    norms_full = self_full[4].reshape(6, model_width)
    queries = project(inputs, self_query_full).astype(jnp.bfloat16)
    keys = project(inputs, self_key_full).astype(jnp.bfloat16)
    values = project(inputs, self_value_full).astype(jnp.bfloat16)
    self_mixed, self_totals = attend_forward(
        heads_view(queries), heads_view(keys), heads_view(values), query_ids, query_ids, True
    )
    inputs_wide = inputs.astype(jnp.float32)
    residual_one = inputs_wide + project(self_mixed, self_out_full)
    first_norm = layer_norm(residual_one, norms_full[0], norms_full[1])
    first_low = first_norm.astype(jnp.bfloat16)
    cross_full = (
        lax.all_gather(cross_query, ("dp", "fsdp"), axis=0, tiled=True),
        lax.all_gather(cross_key, ("dp", "fsdp"), axis=0, tiled=True),
        lax.all_gather(cross_value, ("dp", "fsdp"), axis=0, tiled=True),
        lax.all_gather(cross_out, ("dp", "fsdp"), axis=0, tiled=True),
    )
    cross_query_full = square(cross_full[0])
    cross_key_full = square(cross_full[1])
    cross_value_full = square(cross_full[2])
    cross_out_full = square(cross_full[3])
    cross_queries = project(first_low, cross_query_full).astype(jnp.bfloat16)
    cross_keys = project(memory, cross_key_full).astype(jnp.bfloat16)
    cross_values = project(memory, cross_value_full).astype(jnp.bfloat16)
    cross_mixed, cross_totals = attend_forward(
        heads_view(cross_queries),
        heads_view(cross_keys),
        heads_view(cross_values),
        query_ids,
        memory_ids,
        False,
    )
    residual_two = first_norm + project(cross_mixed, cross_out_full)
    second_norm = layer_norm(residual_two, norms_full[2], norms_full[3])
    second_low = second_norm.astype(jnp.bfloat16)
    ffn_full = (
        lax.all_gather(ffn_in, ("dp", "fsdp"), axis=0, tiled=True),
        lax.all_gather(ffn_out, ("dp", "fsdp"), axis=0, tiled=True),
    )
    ffn_in_full = square(ffn_full[0])
    ffn_out_full = ffn_full[1].reshape(-1, model_width)
    hidden_pre = project(second_low, ffn_in_full)
    active = gelu_tanh(hidden_pre).astype(jnp.bfloat16)
    residual_three = second_norm + project(active, ffn_out_full) + inputs_wide
    block_output = layer_norm(residual_three, norms_full[4], norms_full[5]).astype(jnp.bfloat16)
    ffn_back = (
        lax.all_gather(ffn_in, ("dp", "fsdp"), axis=0, tiled=True),
        lax.all_gather(ffn_out, ("dp", "fsdp"), axis=0, tiled=True),
        lax.all_gather(norm_params.astype(jnp.bfloat16), ("dp", "fsdp"), axis=0, tiled=True).astype(
            norm_params.dtype
        ),
    )
    ffn_in_back = square(ffn_back[0])
    ffn_out_back = ffn_back[1].reshape(-1, model_width)
    norms_back = ffn_back[2].reshape(6, model_width)
    grad_third, grad_gain_three, grad_shift_three = norm_backward(
        residual_three, norms_back[4], norms_back[5], cotangent.astype(jnp.float32)
    )
    grad_ffn_low = grad_third.astype(jnp.bfloat16)
    grad_ffn_out_term = weight_grad(active, grad_ffn_low)
    grad_active = project_back(grad_ffn_low, ffn_out_back)
    grad_hidden = jax.vjp(gelu_tanh, hidden_pre)[1](grad_active)[0].astype(jnp.bfloat16)
    grad_ffn_in_term = weight_grad(second_low, grad_hidden)
    grad_second = grad_third + project_back(grad_hidden, ffn_in_back)
    grad_residual_two, grad_gain_two, grad_shift_two = norm_backward(
        residual_two, norms_back[2], norms_back[3], grad_second
    )
    ffn_sums = (
        lax.psum_scatter(
            grad_ffn_in_term.reshape(-1), ("dp", "fsdp"), scatter_dimension=0, tiled=True
        ),
        lax.psum_scatter(
            grad_ffn_out_term.reshape(-1), ("dp", "fsdp"), scatter_dimension=0, tiled=True
        ),
    )
    cross_back = (
        lax.all_gather(cross_query, ("dp", "fsdp"), axis=0, tiled=True),
        lax.all_gather(cross_key, ("dp", "fsdp"), axis=0, tiled=True),
        lax.all_gather(cross_value, ("dp", "fsdp"), axis=0, tiled=True),
        lax.all_gather(cross_out, ("dp", "fsdp"), axis=0, tiled=True),
    )
    cross_query_back = square(cross_back[0])
    cross_key_back = square(cross_back[1])
    cross_value_back = square(cross_back[2])
    cross_out_back = square(cross_back[3])
    grad_cross_low = grad_residual_two.astype(jnp.bfloat16)
    grad_cross_out_term = weight_grad(cross_mixed, grad_cross_low)
    grad_cross_mixed = project_back(grad_cross_low, cross_out_back).astype(jnp.bfloat16)
    grad_cross_queries, grad_cross_keys, grad_cross_values = attend_backward(
        heads_view(cross_queries),
        heads_view(cross_keys),
        heads_view(cross_values),
        query_ids,
        memory_ids,
        cross_totals,
        heads_view(grad_cross_mixed),
        False,
    )
    grad_cross_query_term = weight_grad(first_low, grad_cross_queries)
    grad_cross_key_term = weight_grad(memory, grad_cross_keys)
    grad_cross_value_term = weight_grad(memory, grad_cross_values)
    grad_memory = (
        project_back(grad_cross_keys, cross_key_back)
        + project_back(grad_cross_values, cross_value_back)
    ).astype(jnp.bfloat16)
    grad_first = grad_residual_two + project_back(grad_cross_queries, cross_query_back)
    grad_residual_one, grad_gain_one, grad_shift_one = norm_backward(
        residual_one, norms_back[0], norms_back[1], grad_first
    )
    cross_sums = (
        lax.psum_scatter(
            grad_cross_query_term.reshape(-1), ("dp", "fsdp"), scatter_dimension=0, tiled=True
        ),
        lax.psum_scatter(
            grad_cross_key_term.reshape(-1), ("dp", "fsdp"), scatter_dimension=0, tiled=True
        ),
        lax.psum_scatter(
            grad_cross_value_term.reshape(-1), ("dp", "fsdp"), scatter_dimension=0, tiled=True
        ),
        lax.psum_scatter(
            grad_cross_out_term.reshape(-1), ("dp", "fsdp"), scatter_dimension=0, tiled=True
        ),
    )
    self_back = (
        lax.all_gather(self_query, ("dp", "fsdp"), axis=0, tiled=True),
        lax.all_gather(self_key, ("dp", "fsdp"), axis=0, tiled=True),
        lax.all_gather(self_value, ("dp", "fsdp"), axis=0, tiled=True),
        lax.all_gather(self_out, ("dp", "fsdp"), axis=0, tiled=True),
    )
    self_query_back = square(self_back[0])
    self_key_back = square(self_back[1])
    self_value_back = square(self_back[2])
    self_out_back = square(self_back[3])
    grad_self_low = grad_residual_one.astype(jnp.bfloat16)
    grad_self_out_term = weight_grad(self_mixed, grad_self_low)
    grad_self_mixed = project_back(grad_self_low, self_out_back).astype(jnp.bfloat16)
    grad_queries, grad_keys, grad_values = attend_backward(
        heads_view(queries),
        heads_view(keys),
        heads_view(values),
        query_ids,
        query_ids,
        self_totals,
        heads_view(grad_self_mixed),
        True,
    )
    grad_self_query_term = weight_grad(inputs, grad_queries)
    grad_self_key_term = weight_grad(inputs, grad_keys)
    grad_self_value_term = weight_grad(inputs, grad_values)
    grad_inputs = (
        grad_residual_one
        + grad_third
        + project_back(grad_queries, self_query_back)
        + project_back(grad_keys, self_key_back)
        + project_back(grad_values, self_value_back)
    ).astype(jnp.bfloat16)
    grad_norm_term = jnp.stack(
        [
            grad_gain_one,
            grad_shift_one,
            grad_gain_two,
            grad_shift_two,
            grad_gain_three,
            grad_shift_three,
        ]
    ).reshape(-1)
    self_sums = (
        lax.psum_scatter(
            grad_self_query_term.reshape(-1), ("dp", "fsdp"), scatter_dimension=0, tiled=True
        ),
        lax.psum_scatter(
            grad_self_key_term.reshape(-1), ("dp", "fsdp"), scatter_dimension=0, tiled=True
        ),
        lax.psum_scatter(
            grad_self_value_term.reshape(-1), ("dp", "fsdp"), scatter_dimension=0, tiled=True
        ),
        lax.psum_scatter(
            grad_self_out_term.reshape(-1), ("dp", "fsdp"), scatter_dimension=0, tiled=True
        ),
        lax.psum_scatter(grad_norm_term, ("dp", "fsdp"), scatter_dimension=0, tiled=True),
    )
    layer_sums = (
        self_sums[0],
        self_sums[1],
        self_sums[2],
        self_sums[3],
        cross_sums[0],
        cross_sums[1],
        cross_sums[2],
        cross_sums[3],
        ffn_sums[0],
        ffn_sums[1],
        self_sums[4],
    )
    return (
        block_output,
        grad_inputs,
        grad_memory,
        layer_sums[0],
        layer_sums[1],
        layer_sums[2],
        layer_sums[3],
        layer_sums[4],
        layer_sums[5],
        layer_sums[6],
        layer_sums[7],
        layer_sums[8],
        layer_sums[9],
        layer_sums[10],
    )


def solution(mesh):
    return jax.shard_map(
        body,
        mesh=mesh,
        in_specs=(
            P(("dp", "fsdp"), None),
            P(("dp", "fsdp"), None),
            P(("dp", "fsdp"), None),
            P(("dp", "fsdp"), None),
            P(("dp", "fsdp")),
            P(("dp", "fsdp")),
            P(("dp", "fsdp")),
            P(("dp", "fsdp")),
            P(("dp", "fsdp")),
            P(("dp", "fsdp")),
            P(("dp", "fsdp")),
            P(("dp", "fsdp")),
            P(("dp", "fsdp")),
            P(("dp", "fsdp")),
            P(("dp", "fsdp")),
            P(("dp", "fsdp"), None),
        ),
        out_specs=(
            P(("dp", "fsdp"), None),
            P(("dp", "fsdp"), None),
            P(("dp", "fsdp"), None),
            P(("dp", "fsdp")),
            P(("dp", "fsdp")),
            P(("dp", "fsdp")),
            P(("dp", "fsdp")),
            P(("dp", "fsdp")),
            P(("dp", "fsdp")),
            P(("dp", "fsdp")),
            P(("dp", "fsdp")),
            P(("dp", "fsdp")),
            P(("dp", "fsdp")),
            P(("dp", "fsdp")),
        ),
        check_vma=False,
    )
```

profile of v0, /device:TPU:0, one launch (start us, length us, event | category | flops | bytes accessed | tf_op | source)
XLA Modules:
  0.0 1308.1 jit_solution(17564389907011012566)
XLA Ops:
  9.6 42.1 %all-reduce = bf16[3072]{0:T(1024)(128)(2,1)S(1)} all-reduce(bf16[3072]{0:T(1024)(128)(2,1)S(1)} %dynamic-update-slice), channel_id=1, replica_groups=mesh['dp'=8,'fsdp'=4] {'dp','fsdp'}, use_global_device_ids=true, to_apply=%add | all-reduce | flops 3072 | bytes 12288
  54.9 42.2 %all_gather.44 = bf16[262144]{0:T(1024)(128)(2,1)S(1)} all-gather(bf16[8192]{0:T(1024)(128)(2,1)} %param.28), channel_id=1, replica_groups=mesh['dp'=8,'fsdp'=4] {'dp','fsdp'}, dimensions={0}, use_global_device_ids=true | all-gather | bytes 540672 | tf_op jit(solution)/shard_map/all_gather | solution.py:181
  98.3 39.1 %all_gather.45 = bf16[262144]{0:T(1024)(128)(2,1)S(1)} all-gather(bf16[8192]{0:T(1024)(128)(2,1)} %param.29), channel_id=1, replica_groups=mesh['dp'=8,'fsdp'=4] {'dp','fsdp'}, dimensions={0}, use_global_device_ids=true | all-gather | bytes 540672 | tf_op jit(solution)/shard_map/all_gather | solution.py:182
  138.5 39.0 %all_gather.46 = bf16[262144]{0:T(1024)(128)(2,1)S(1)} all-gather(bf16[8192]{0:T(1024)(128)(2,1)S(1)} %copy-done.88), channel_id=1, replica_groups=mesh['dp'=8,'fsdp'=4] {'dp','fsdp'}, dimensions={0}, use_global_device_ids=true | all-gather | bytes 540672 | tf_op jit(solution)/shard_map/all_gather | solution.py:183
  177.9 38.4 %all_gather.47 = bf16[262144]{0:T(1024)(128)(2,1)S(1)} all-gather(bf16[8192]{0:T(1024)(128)(2,1)S(1)} %copy-done.89), channel_id=1, replica_groups=mesh['dp'=8,'fsdp'=4] {'dp','fsdp'}, dimensions={0}, use_global_device_ids=true | all-gather | bytes 540672 | tf_op jit(solution)/shard_map/all_gather | solution.py:184
  217.5 39.0 %all_gather.49 = bf16[262144]{0:T(1024)(128)(2,1)S(1)} all-gather(bf16[8192]{0:T(1024)(128)(2,1)S(1)} %copy-done.90), channel_id=1, replica_groups=mesh['dp'=8,'fsdp'=4] {'dp','fsdp'}, dimensions={0}, use_global_device_ids=true | all-gather | bytes 540672 | tf_op jit(solution)/shard_map/all_gather | solution.py:205
  257.6 38.4 %all_gather.50 = bf16[262144]{0:T(1024)(128)(2,1)S(1)} all-gather(bf16[8192]{0:T(1024)(128)(2,1)S(1)} %copy-done.91), channel_id=1, replica_groups=mesh['dp'=8,'fsdp'=4] {'dp','fsdp'}, dimensions={0}, use_global_device_ids=true | all-gather | bytes 540672 | tf_op jit(solution)/shard_map/all_gather | solution.py:206
  297.2 39.2 %all_gather.51 = bf16[262144]{0:T(1024)(128)(2,1)S(1)} all-gather(bf16[8192]{0:T(1024)(128)(2,1)S(1)} %copy-done.92), channel_id=1, replica_groups=mesh['dp'=8,'fsdp'=4] {'dp','fsdp'}, dimensions={0}, use_global_device_ids=true | all-gather | bytes 540672 | tf_op jit(solution)/shard_map/all_gather | solution.py:207
  353.8 30.9 %while.54 = (s32[]{:T(128)}, bf16[2,512,8,64]{1,3,2,0:T(8,128)(2,1)}, f32[2,8,512]{2,1,0:T(8,128)S(1)}, s32[2,512]{1,0:T(2,128)S(1)}, s32[1024]{0:T(1024)S(1)}, ...) while((s32[]{:T(128)}, ...), condition=%wide.region_5.6_spmd, body=%wide.region_2.0_spmd.sunk | while | flops 1125904384 | bytes 68305112 | solution.py:79
  362.8 5.4 fusion.198
  378.2 5.4 fusion.198
  402.8 93.2 %while.55 = (s32[]{:T(128)}, bf16[2,512,8,64]{1,3,2,0:T(8,128)(2,1)}, f32[2,8,512]{2,1,0:T(8,128)S(1)}, s32[2,512]{1,0:T(2,128)S(1)}, s32[2048]{0:T(1024)S(1)}, ...) while((s32[]{:T(128)}, ...), condition=%wide.region_13.14_spmd, body=%wide.region_10.13_spmd.sunk | while | flops 2249453568 | bytes 110246000 | solution.py:79
  403.9 15.1 %fusion.201 = (f32[8,512]{1,0:T(8,128)S(1)}, f32[8,512,2048]{2,1,0:T(8,128)}) fusion(pred[512,2048]{1,0:T(8,128)(4,1)S(1)} %broadcast_compare_fusion.4, bf16[2048,8,64]{0,2,1:T(8,128)(2,1)} %get-tuple-element.983, bf16[2,512,8,64]{1,3,2,0:T(8,128)(2,1)} %get-tuple-element.982, s32[]{:T(128)S(6)} %copy.183), kind=kOutput, calls=%fused_computation.23.clone.1 | convolution fusion | flops 1098903552 | bytes 37240836 | tf_op jit(solution)/shard_map/while/body/eval_jaxpr/thd,shd->hts/dot_general | solution.py:53
  419.1 15.0 %fusion.202 = f32[8,512]{1,0:T(8,128)S(1)} fusion(f32[8,512,2048]{2,1,0:T(8,128)} %get-tuple-element.898, f32[8,512]{1,0:T(8,128)S(1)} %get-tuple-element.899, pred[512,2048]{1,0:T(8,128)(4,1)S(1)} %broadcast_compare_fusion.4), kind=kLoop, calls=%fused_computation.24.clone.1 | loop fusion | flops 33550336 | bytes 34635776 | tf_op jit(solution)/shard_map/while/body/eval_jaxpr/reduce_sum | solution.py:74
  434.0 15.5 %fusion.203 = bf16[2,512,8,64]{1,3,2,0:T(8,128)(2,1)} fusion(bf16[2,512,8,64]{1,3,2,0:T(8,128)(2,1)} %get-tuple-element.969, s32[]{:T(128)S(6)} %copy.183, bf16[2048,8,64]{0,2,1:T(8,128)(2,1)} %get-tuple-element.984, f32[8,512,2048]{2,1,0:T(8,128)} %get-tuple-element.898, f32[8,512]{1,0:T(8,128)S(1)} %fusion.202, ...), kind=kOutput, calls=%fused_computation.29.clone.1 | convolution fusion | flops 1115947008 | bytes 37257220 | tf_op jit(solution)/shard_map/while/body/eval_jaxpr/hts,shd->thd/dot_general | solution.py:76
  450.3 15.1 %fusion.201 = (f32[8,512]{1,0:T(8,128)S(1)}, f32[8,512,2048]{2,1,0:T(8,128)}) fusion(pred[512,2048]{1,0:T(8,128)(4,1)S(1)} %broadcast_compare_fusion.4, bf16[2048,8,64]{0,2,1:T(8,128)(2,1)} %get-tuple-element.983, bf16[2,512,8,64]{1,3,2,0:T(8,128)(2,1)} %get-tuple-element.982, s32[]{:T(128)S(6)} %copy.183), kind=kOutput, calls=%fused_computation.23.clone.1 | convolution fusion | flops 1098903552 | bytes 37240836 | tf_op jit(solution)/shard_map/while/body/eval_jaxpr/thd,shd->hts/dot_general | solution.py:53
  465.4 15.0 %fusion.202 = f32[8,512]{1,0:T(8,128)S(1)} fusion(f32[8,512,2048]{2,1,0:T(8,128)} %get-tuple-element.898, f32[8,512]{1,0:T(8,128)S(1)} %get-tuple-element.899, pred[512,2048]{1,0:T(8,128)(4,1)S(1)} %broadcast_compare_fusion.4), kind=kLoop, calls=%fused_computation.24.clone.1 | loop fusion | flops 33550336 | bytes 34635776 | tf_op jit(solution)/shard_map/while/body/eval_jaxpr/reduce_sum | solution.py:74
  480.4 15.5 %fusion.203 = bf16[2,512,8,64]{1,3,2,0:T(8,128)(2,1)} fusion(bf16[2,512,8,64]{1,3,2,0:T(8,128)(2,1)} %get-tuple-element.969, s32[]{:T(128)S(6)} %copy.183, bf16[2048,8,64]{0,2,1:T(8,128)(2,1)} %get-tuple-element.984, f32[8,512,2048]{2,1,0:T(8,128)} %get-tuple-element.898, f32[8,512]{1,0:T(8,128)S(1)} %fusion.202, ...), kind=kOutput, calls=%fused_computation.29.clone.1 | convolution fusion | flops 1115947008 | bytes 37257220 | tf_op jit(solution)/shard_map/while/body/eval_jaxpr/hts,shd->thd/dot_general | solution.py:76
  496.0 38.5 %all_gather.52 = bf16[262144]{0:T(1024)(128)(2,1)S(1)} all-gather(bf16[8192]{0:T(1024)(128)(2,1)S(1)} %copy-done.93), channel_id=1, replica_groups=mesh['dp'=8,'fsdp'=4] {'dp','fsdp'}, dimensions={0}, use_global_device_ids=true | all-gather | bytes 540672 | tf_op jit(solution)/shard_map/all_gather | solution.py:208
  547.0 8.1 fusion.83
  559.4 8.9 fusion.93
  572.3 9.2 fusion.69
  581.5 5.0 convolution_bitcast_fusion
  590.3 4.5 convolution_bitcast_fusion.1
  605.0 210.4 %while.56 = (s32[]{:T(128)}, f32[2048,8,64]{0,2,1:T(8,128)}, f32[2048,8,64]{0,2,1:T(8,128)}, bf16[2,512,8,64]{1,3,2,0:T(8,128)(2,1)}, bf16[2,512,8,64]{1,3,2,0:T...) while((s32[]{:T(128)}, f32[2048,8,64]{0,2,1:T(8,128)}, ...), condition=%wide.region_24.25_spmd.clone, body=%wide.region_22.24_spmd.clone.sunk | while | flops 5451018240 | bytes 355039456 | solution.py:127
  606.1 17.5 %fusion.213 = f32[8,512,2048]{2,1,0:T(8,128)} fusion(bf16[2048,8,64]{0,2,1:T(8,128)(2,1)} %get-tuple-element.1022, bf16[2,512,8,64]{1,3,2,0:T(8,128)(2,1)} %get-tuple-element.1021, s32[]{:T(128)S(6)} %copy.193), kind=kOutput, calls=%fused_computation.51.clone.1 | convolution fusion | flops 1073741824 | bytes 36175876 | tf_op jit(solution)/shard_map/while/body/eval_jaxpr/thd,shd->hts/dot_general | solution.py:102
  623.6 24.7 %multiply_reduce_fusion.11 = (f32[8,512]{1,0:T(8,128)S(1)}, f32[8,512,2048]{2,1,0:T(8,128)}) fusion(f32[8,512,2048]{2,1,0:T(8,128)} %fusion.213, f32[8,512]{1,0:T(8,128)S(1)} %dynamic-slice_bitcast_fusion.4, bf16[2048,8,64]{0,2,1:T(8,128)(2,1)S(1)} %copy-done.4, bf16[2,512,8,64]{1,3,2,0:T(8,128)(2,1)} %get-tuple-element.1016, s32[]{:T(128)S(6)} %copy.193, ...), kind=kOutput, calls=%fused_computation.39.clone.1 | convolution fusion | flops 1115680768 | bytes 70811648 | tf_op jit(solution)/shard_map/while/body/eval_jaxpr/thd,shd->hts/dot_general | solution.py:53
  648.3 27.5 %multiply_convert_fusion.7 = bf16[8,512,2048]{2,1,0:T(8,128)(2,1)} fusion(f32[8,512,2048]{2,1,0:T(8,128)} %get-tuple-element.911, f32[8,512,2048]{2,1,0:T(8,128)} %fusion.213, f32[8,512]{1,0:T(8,128)S(1)} %get-tuple-element.912), kind=kLoop, calls=%fused_computation.38.clone.1 | loop fusion | flops 25165824 | bytes 83902464 | tf_op jit(solution)/shard_map/while/body/eval_jaxpr/convert_element_type | solution.py:106
  675.8 15.7 %bitcast_add_fusion.9 = f32[2048,8,64]{0,2,1:T(8,128)} fusion(f32[2048,8,64]{0,2,1:T(8,128)} %get-tuple-element.1001, f32[8,512,2048]{2,1,0:T(8,128)} %get-tuple-element.911, pred[]{:T(512)S(6)} %compare.6, bf16[2,512,8,64]{1,3,2,0:T(8,128)(2,1)} %get-tuple-element.1021, s32[]{:T(128)S(6)} %copy.193), kind=kOutput, calls=%fused_computation.43.clone.1 | convolution fusion | flops 1084227584 | bytes 42467332 | tf_op jit(solution)/shard_map/while/body/eval_jaxpr/hts,thd->shd/dot_general | solution.py:118
  691.5 10.2 fusion.214
  702.9 6.2 bitcast_add_fusion.8
  709.7 17.5 %fusion.213 = f32[8,512,2048]{2,1,0:T(8,128)} fusion(bf16[2048,8,64]{0,2,1:T(8,128)(2,1)} %get-tuple-element.1022, bf16[2,512,8,64]{1,3,2,0:T(8,128)(2,1)} %get-tuple-element.1021, s32[]{:T(128)S(6)} %copy.193), kind=kOutput, calls=%fused_computation.51.clone.1 | convolution fusion | flops 1073741824 | bytes 36175876 | tf_op jit(solution)/shard_map/while/body/eval_jaxpr/thd,shd->hts/dot_general | solution.py:102
  727.2 24.7 %multiply_reduce_fusion.11 = (f32[8,512]{1,0:T(8,128)S(1)}, f32[8,512,2048]{2,1,0:T(8,128)}) fusion(f32[8,512,2048]{2,1,0:T(8,128)} %fusion.213, f32[8,512]{1,0:T(8,128)S(1)} %dynamic-slice_bitcast_fusion.4, bf16[2048,8,64]{0,2,1:T(8,128)(2,1)S(1)} %copy-done.4, bf16[2,512,8,64]{1,3,2,0:T(8,128)(2,1)} %get-tuple-element.1016, s32[]{:T(128)S(6)} %copy.193, ...), kind=kOutput, calls=%fused_computation.39.clone.1 | convolution fusion | flops 1115680768 | bytes 70811648 | tf_op jit(solution)/shard_map/while/body/eval_jaxpr/thd,shd->hts/dot_general | solution.py:53
  752.0 27.5 %multiply_convert_fusion.7 = bf16[8,512,2048]{2,1,0:T(8,128)(2,1)} fusion(f32[8,512,2048]{2,1,0:T(8,128)} %get-tuple-element.911, f32[8,512,2048]{2,1,0:T(8,128)} %fusion.213, f32[8,512]{1,0:T(8,128)S(1)} %get-tuple-element.912), kind=kLoop, calls=%fused_computation.38.clone.1 | loop fusion | flops 25165824 | bytes 83902464 | tf_op jit(solution)/shard_map/while/body/eval_jaxpr/convert_element_type | solution.py:106
  779.4 16.9 %bitcast_add_fusion.9 = f32[2048,8,64]{0,2,1:T(8,128)} fusion(f32[2048,8,64]{0,2,1:T(8,128)} %get-tuple-element.1001, f32[8,512,2048]{2,1,0:T(8,128)} %get-tuple-element.911, pred[]{:T(512)S(6)} %compare.6, bf16[2,512,8,64]{1,3,2,0:T(8,128)(2,1)} %get-tuple-element.1021, s32[]{:T(128)S(6)} %copy.193), kind=kOutput, calls=%fused_computation.43.clone.1 | convolution fusion | flops 1084227584 | bytes 42467332 | tf_op jit(solution)/shard_map/while/body/eval_jaxpr/hts,thd->shd/dot_general | solution.py:118
  796.4 10.2 fusion.214
  807.7 7.5 bitcast_add_fusion.8
  841.9 108.9 %while.57 = (s32[]{:T(128)}, f32[1024,8,64]{0,2,1:T(8,128)}, f32[1024,8,64]{0,2,1:T(8,128)}, bf16[2,512,8,64]{1,3,2,0:T(8,128)(2,1)}, bf16[2,512,8,64]{1,3,2,0:T...) while((s32[]{:T(128)}, f32[1024,8,64]{0,2,1:T(8,128)}, ...), condition=%wide.region_29.30_spmd.clone, body=%wide.region_27.29_spmd.clone.sunk | while | flops 2726817792 | bytes 292127168 | solution.py:127
  842.7 9.6 fusion.224
  852.3 12.6 multiply_reduce_fusion.12
  865.0 15.0 %multiply_convert_fusion.8 = bf16[8,512,1024]{2,1,0:T(8,128)(2,1)} fusion(f32[8,512,1024]{2,1,0:T(8,128)} %get-tuple-element.927, f32[8,512,1024]{2,1,0:T(8,128)} %fusion.224, f32[8,512]{1,0:T(8,128)S(1)} %get-tuple-element.928), kind=kLoop, calls=%fused_computation.65.clone.1 | loop fusion | flops 12582912 | bytes 41959424 | tf_op jit(solution)/shard_map/while/body/eval_jaxpr/convert_element_type | solution.py:106
  886.1 6.8 fusion.226
  896.9 9.6 fusion.224
  906.5 12.6 multiply_reduce_fusion.12
  919.2 15.0 %multiply_convert_fusion.8 = bf16[8,512,1024]{2,1,0:T(8,128)(2,1)} fusion(f32[8,512,1024]{2,1,0:T(8,128)} %get-tuple-element.927, f32[8,512,1024]{2,1,0:T(8,128)} %fusion.224, f32[8,512]{1,0:T(8,128)S(1)} %get-tuple-element.928), kind=kLoop, calls=%fused_computation.65.clone.1 | loop fusion | flops 12582912 | bytes 41959424 | tf_op jit(solution)/shard_map/while/body/eval_jaxpr/convert_element_type | solution.py:106
  940.3 6.8 fusion.226
  1007.0 39.1 %all-reduce.11 = f32[3072]{0:T(1024)S(1)} all-reduce(f32[3072]{0:T(1024)S(1)} %reshape.585), channel_id=12, replica_groups=mesh['dp'=8,'fsdp'=4] {'dp','fsdp'}, use_global_device_ids=true, to_apply=%region_46.47.clone | all-reduce | flops 3072 | bytes 24576
  1052.5 234.4 %all-reduce.15.cloned.1.call-done = (f32[262144]{0:T(1024)}, f32[262144]{0:T(1024)}, f32[262144]{0:T(1024)}, f32[262144]{0:T(1024)}, f32[262144]{0:T(1024)}, /*i...) async-done(((f32[262144]{0:T(1024)}, f32[262144]{0:T(1024)}, f32[262144]{0:T(1024)}, f32[262144]{0:T(1024)}, ...) | async-done | bytes 16777232
  (414 shorter events, 228.8 us)
Async XLA Ops:
  7.2 380.6 %copy-start = (bf16[2048,512]{1,0:T(8,128)(2,1)S(1)}, bf16[2048,512]{1,0:T(8,128)(2,1)}, u32[]{:S(2)}) copy-start(bf16[2048,512]{1,0:T(8,128)(2,1)} %param.25) | copy-start | bytes 6291460
  7.2 131.3 %copy-start.88 = (bf16[8192]{0:T(1024)(128)(2,1)S(1)}, bf16[8192]{0:T(1024)(128)(2,1)}, u32[]{:S(2)}) copy-start(bf16[8192]{0:T(1024)(128)(2,1)} %param.30) | copy-start | bytes 49156
  7.2 535.6 %all-gather.3.cloned.1.call-start = ((), (), s32[]{:S(2)}) async-start(), calls=%async_computation | async-start | bytes 2162688 | tf_op jit(solution)/shard_map/all_gather | solution.py:229
  7.9 547.1 %all-gather.5.cloned.1.call-start = ((), (), s32[]{:S(2)}) async-start(), calls=%async_computation.1 | async-start | bytes 2162688 | tf_op jit(solution)/shard_map/all_gather | solution.py:230
  8.7 1278.2 %all-reduce.15.cloned.1.call-start = ((), (), s32[]{:S(2)}) async-start(), calls=%async_computation.2 | async-start | bytes 33554432
  97.2 80.7 %copy-start.89 = (bf16[8192]{0:T(1024)(128)(2,1)S(1)}, bf16[8192]{0:T(1024)(128)(2,1)}, u32[]{:S(2)}) copy-start(bf16[8192]{0:T(1024)(128)(2,1)} %param.31) | copy-start | bytes 49156
  137.4 80.1 %copy-start.90 = (bf16[8192]{0:T(1024)(128)(2,1)S(1)}, bf16[8192]{0:T(1024)(128)(2,1)}, u32[]{:S(2)}) copy-start(bf16[8192]{0:T(1024)(128)(2,1)} %param.32) | copy-start | bytes 49156
  177.6 80.1 %copy-start.91 = (bf16[8192]{0:T(1024)(128)(2,1)S(1)}, bf16[8192]{0:T(1024)(128)(2,1)}, u32[]{:S(2)}) copy-start(bf16[8192]{0:T(1024)(128)(2,1)} %param.33) | copy-start | bytes 49156
  177.9 161.9 %copy-start.48 = (bf16[512,512]{1,0:T(8,128)(2,1)}, bf16[512,512]{1,0:T(8,128)(2,1)S(1)}, u32[]{:S(2)}) copy-start(bf16[512,512]{1,0:T(8,128)(2,1)S(1)} %reshape.548) | copy-start | bytes 1572868
  216.4 80.8 %copy-start.92 = (bf16[8192]{0:T(1024)(128)(2,1)S(1)}, bf16[8192]{0:T(1024)(128)(2,1)}, u32[]{:S(2)}) copy-start(bf16[8192]{0:T(1024)(128)(2,1)} %param.34) | copy-start | bytes 49156
  358.5 4.3 copy-start.10
  358.5 4.3 copy-start.37
  373.9 4.3 copy-start.10
  373.9 4.3 copy-start.37
  387.8 5.3 copy-start.39
  398.4 4.4 copy-start.62
  402.8 93.2 %copy-start.93 = (bf16[8192]{0:T(1024)(128)(2,1)S(1)}, bf16[8192]{0:T(1024)(128)(2,1)}, u32[]{:S(2)}) copy-start(bf16[8192]{0:T(1024)(128)(2,1)} %param.35) | copy-start | bytes 49156
  542.8 4.2 copy-start.94
  542.8 4.2 copy-start.105
  559.4 12.9 copy-start.106
  572.3 14.3 %copy-start.28 = (f32[1024,512]{0,1:T(8,128)}, f32[1024,512]{0,1:T(8,128)S(1)}, u32[]{:S(2)}) copy-start(f32[1024,512]{0,1:T(8,128)S(1)} %get-tuple-element.633) | copy-start | bytes 6291460
  572.3 14.3 %copy-start.83 = (f32[1024]{0:T(1024)}, f32[1024]{0:T(1024)S(1)}, u32[]{:S(2)}) copy-start(f32[1024]{0:T(1024)S(1)} %negate_multiply_fusion.2) | copy-start | bytes 12292
  581.5 5.0 copy-start.23
  581.5 5.0 copy-start.51
  606.1 17.5 %copy-start.4 = (bf16[2048,8,64]{0,2,1:T(8,128)(2,1)S(1)}, bf16[2048,8,64]{0,2,1:T(8,128)(2,1)}, u32[]{:S(2)}) copy-start(bf16[2048,8,64]{0,2,1:T(8,128)(2,1)} %get-tuple-element.1019) | copy-start | bytes 6291460 | tf_op jit(solution)/shard_map/while
  691.5 11.3 copy-start.2
  709.7 17.5 %copy-start.4 = (bf16[2048,8,64]{0,2,1:T(8,128)(2,1)S(1)}, bf16[2048,8,64]{0,2,1:T(8,128)(2,1)}, u32[]{:S(2)}) copy-start(bf16[2048,8,64]{0,2,1:T(8,128)(2,1)} %get-tuple-element.1019) | copy-start | bytes 6291460 | tf_op jit(solution)/shard_map/while
  796.4 11.3 copy-start.2
  837.4 4.5 copy-start.9
  837.4 4.5 copy-start.64
  837.4 4.5 copy-start.68
  837.4 4.5 copy-start.70
  842.7 9.6 copy-start.11
  865.0 18.4 %copy-start.1 = (f32[8,512,1024]{2,1,0:T(8,128)S(1)}, f32[8,512,1024]{2,1,0:T(8,128)}, u32[]{:S(2)}) copy-start(f32[8,512,1024]{2,1,0:T(8,128)} %get-tuple-element.927) | copy-start | bytes 50331652 | tf_op jit(solution)/shard_map/while
  865.0 19.0 %copy-start.12 = (f32[1024,8,64]{0,2,1:T(8,128)S(1)}, f32[1024,8,64]{0,2,1:T(8,128)}, u32[]{:S(2)}) copy-start(f32[1024,8,64]{0,2,1:T(8,128)} %get-tuple-element.1041) | copy-start | bytes 6291460 | tf_op jit(solution)/shard_map/while
  865.0 19.2 %copy-start.15 = (bf16[2,512,8,64]{1,3,2,0:T(8,128)(2,1)S(1)}, bf16[2,512,8,64]{1,3,2,0:T(8,128)(2,1)}, u32[]{:S(2)}) copy-start(bf16[2,512,8,64]{1,3,2,0:T(8,128)(2,1)} %get-tuple-element.1063) | copy-start | bytes 3145732 | tf_op jit(solution)/shard_map/while
  886.1 6.9 copy-start.13
  886.1 6.9 copy-start.3
  886.1 7.1 copy-start.5
  896.9 9.6 copy-start.11
  919.2 18.4 %copy-start.1 = (f32[8,512,1024]{2,1,0:T(8,128)S(1)}, f32[8,512,1024]{2,1,0:T(8,128)}, u32[]{:S(2)}) copy-start(f32[8,512,1024]{2,1,0:T(8,128)} %get-tuple-element.927) | copy-start | bytes 50331652 | tf_op jit(solution)/shard_map/while
  919.2 19.0 %copy-start.12 = (f32[1024,8,64]{0,2,1:T(8,128)S(1)}, f32[1024,8,64]{0,2,1:T(8,128)}, u32[]{:S(2)}) copy-start(f32[1024,8,64]{0,2,1:T(8,128)} %get-tuple-element.1041) | copy-start | bytes 6291460 | tf_op jit(solution)/shard_map/while
  919.2 19.2 %copy-start.15 = (bf16[2,512,8,64]{1,3,2,0:T(8,128)(2,1)S(1)}, bf16[2,512,8,64]{1,3,2,0:T(8,128)(2,1)}, u32[]{:S(2)}) copy-start(bf16[2,512,8,64]{1,3,2,0:T(8,128)(2,1)} %get-tuple-element.1063) | copy-start | bytes 3145732 | tf_op jit(solution)/shard_map/while
  940.3 6.9 copy-start.13
  940.3 6.9 copy-start.3
  940.3 7.1 copy-start.5
  950.8 3.7 copy-start.56
  999.9 3.5 copy-start.29
  (77 other events, 165.8 us)
Sparse Core Ops, SparseCore 0:
  10.9 60.0 all-gather.2
  73.8 55.8 all-gather.4
  997.6 289.2 all-reduce.14
where the time goes:
time: 1320 us; the launch traced here: 1310 us
  blocking collectives  395 us (30%)
  matrix products  377 us (29%)
  waiting for transfers between devices  236 us (18%)
  local copies, waits for them, and re-layouts  141 us (11%)
  other arithmetic  141 us (11%)
  between operations  15.5 us (1%)
    unnamed x4, waiting for transfers between devices  236 us
    dot_general x8, matrix products, block_scores(): jnp.einsum('thd,shd->hts', query_block, keys, preferred_element_type=jnp....  113 us
    convert_element_type x4, other arithmetic, one_block(): grad_scores = (weights * (grad_weights - inner)).astype(jnp.bfloat16)  85 us
    unnamed x2, blocking collectives  81.2 us
    unnamed x217, local copies, waits for them, and re-layouts  63.9 us
    dot_general x4, matrix products, one_block(): jnp.einsum('thd,shd->hts', grad_block, values, preferred_element_type=jnp...  54.2 us
    all_gather x1, blocking collectives, body(): lax.all_gather(self_query, ('dp', 'fsdp'), axis=0, tiled=True)  42.2 us
    dot_general x4, matrix products, one_block(): jnp.einsum('hts,shd->thd', weights, values, preferred_element_type=jnp.fl...  41.8 us
  transfers between devices with their start and end apart: 3, of which 1 were waited for; matrix products, arithmetic and copies ran while one was open for 15% of the time, Pallas kernels for 0%

commit v1 on v0

v1 whole, which is shorter than its diff:
```python
import functools
import jax
import jax.numpy as jnp
from jax import lax
from jax.experimental import pallas as pl
from jax.experimental.pallas import tpu as pltpu
from jax.sharding import PartitionSpec as P

HD = 64
LANES = 128
MOST = 256
masked_score = -1e30
norm_eps = 1e-05
bf16, f32 = jnp.bfloat16, jnp.float32
NT = (((1,), (1,)), ((), ()))
TN = (((0,), (0,)), ((), ()))
NN = (((1,), (0,)), ((), ()))


def mm(left, right, dims=NN):
    return lax.dot_general(left, right, dims, preferred_element_type=f32)


def norm_rows(source):
    mean = jnp.mean(source, axis=-1, keepdims=True)
    centered = source - mean
    variance = jnp.mean(centered * centered, axis=-1, keepdims=True)
    rstd = lax.rsqrt(variance + norm_eps)
    return centered * rstd, rstd


def lane_below(rows):
    return lax.broadcasted_iota(jnp.int32, (rows, LANES), 1) < HD


def head_part(pair, which, low):
    return jnp.where(low == (which == 0), pair, jnp.zeros_like(pair))


def values_with_ones(values, low):
    parts = []
    for p in range(values.shape[1] // LANES):
        pair = values[:, p * LANES : (p + 1) * LANES]
        one = jnp.ones_like(pair)
        parts.append(jnp.where(low, pair, one))
        parts.append(jnp.where(low, pltpu.roll(pair, HD, 1), one))
    return jnp.concatenate(parts, axis=1)


def self_forward_kernel(
    block, x_ref, wq_ref, wk_ref, wv_ref, wo_ref, wcq_ref, norms_ref, idc_ref, idr_ref,
    q_ref, k_ref, v_ref, o_ref, l_ref, r1_ref, h1b_ref, q2_ref, k_all, vx_all,
):
    step = pl.program_id(0)
    rows, width = x_ref.shape
    total = k_all.shape[0]
    window = MOST + block
    pairs = width // LANES
    x = x_ref[...]
    q = mm(x, wq_ref[...]).astype(bf16)
    k = mm(x, wk_ref[...]).astype(bf16)
    v = mm(x, wv_ref[...]).astype(bf16)
    q_ref[...] = q
    k_ref[...] = k
    v_ref[...] = v
    low_rows = lane_below(rows)

    @pl.when(step == 0)
    def _():
        k_all[...] = jnp.zeros_like(k_all)
        vx_all[...] = jnp.zeros_like(vx_all)

    base = pl.multiple_of(step * rows, rows)
    k_all[pl.ds(base, rows), :] = k
    vx_all[pl.ds(base, rows), :] = values_with_ones(v, low_rows)
    scaled = q * jnp.asarray(HD ** -0.5, bf16)
    low = lane_below(block)
    lane = lax.broadcasted_iota(jnp.int32, (block, LANES), 1)
    for sub in range(rows // block):
        start = pl.multiple_of(jnp.maximum(base + sub * block - MOST, 0), LANES)
        ids_q = idc_ref[sub * block : (sub + 1) * block, :]
        ids_k = idr_ref[:, pl.ds(start, window)]
        pos_q = base + sub * block + lax.broadcasted_iota(jnp.int32, (block, window), 0)
        pos_k = start + lax.broadcasted_iota(jnp.int32, (block, window), 1)
        bias = jnp.where((ids_q == ids_k) & (pos_k <= pos_q), 0.0, masked_score).astype(f32)
        totals = jnp.zeros((block, LANES), f32)
        for p in range(pairs):
            cols = slice(p * LANES, (p + 1) * LANES)
            qp = scaled[sub * block : (sub + 1) * block, cols]
            kp = k_all[pl.ds(start, window), cols]
            mixed = []
            for h in range(2):
                s = mm(head_part(qp, h, low), kp, NT) + bias
                m = jnp.max(s, axis=1, keepdims=True)
                e = jnp.exp(s - m).astype(bf16)
                head = 2 * p + h
                o = mm(e, vx_all[pl.ds(start, window), head * LANES : (head + 1) * LANES])
                l = pltpu.roll(o, HD, 1)
                mixed.append(o / l)
                totals = jnp.where(lane == head, m + jnp.log(jnp.where(low, l, 1.0)[:, :1]), totals)
            o_ref[sub * block : (sub + 1) * block, cols] = jnp.where(
                low, mixed[0], pltpu.roll(mixed[1], HD, 1)
            ).astype(bf16)
        l_ref[:, sub * block : (sub + 1) * block] = totals.T[: 2 * pairs, :]
    r1 = x.astype(f32) + mm(o_ref[...], wo_ref[...])
    r1_ref[...] = r1
    n, _ = norm_rows(r1)
    h1b = (n * norms_ref[0:1, :] + norms_ref[1:2, :]).astype(bf16)
    h1b_ref[...] = h1b
    q2_ref[...] = mm(h1b, wcq_ref[...]).astype(bf16)


def whole(a):
    return pl.BlockSpec(a.shape, lambda *_: (0,) * a.ndim)


def self_forward(x, wq, wk, wv, wo, wcq, norms, idc, idr, rows=256, block=128, vmem=48 * 2**20):
    total, width = x.shape
    heads = width // HD
    steps = total // rows
    rowspec = lambda w: pl.BlockSpec((rows, w), lambda i: (i, 0))
    full = jax.ShapeDtypeStruct((total, width), bf16)
    return pl.pallas_call(
        functools.partial(self_forward_kernel, block),
        grid=(steps,),
        in_specs=[rowspec(width)] + [whole(a) for a in (wq, wk, wv, wo, wcq, norms)] + [rowspec(1), whole(idr)],
        out_specs=[rowspec(width)] * 4 + [pl.BlockSpec((heads, rows), lambda i: (0, i))] + [rowspec(width)] * 3,
        out_shape=[full] * 4
        + [jax.ShapeDtypeStruct((heads, total), f32), jax.ShapeDtypeStruct((total, width), f32), full, full],
        scratch_shapes=[pltpu.VMEM((total, width), bf16), pltpu.VMEM((total, 2 * width), bf16)],
        compiler_params=pltpu.CompilerParams(vmem_limit_bytes=vmem),
        name="self_forward",
    )(x, wq, wk, wv, wo, wcq, norms, idc, idr)


def cross_forward_kernel(
    tile, ranges_ref, q2_ref, k2_ref, v2_ref, r1_ref, wco_ref, norms_ref, idc_ref, idr_ref,
    o_ref, l_ref, r2_ref, vx_all, s_all, acc,
):
    step = pl.program_id(0)
    rows, width = q2_ref.shape
    keys = k2_ref.shape[0]
    pairs = width // LANES

    @pl.when(step == 0)
    def _():
        def fill(j, _):
            at = pl.ds(pl.multiple_of(j * tile, tile), tile)
            vx_all[at, :] = values_with_ones(v2_ref[at, :], lane_below(tile))
            return 0

        lax.fori_loop(0, keys // tile, fill, 0)

    low = lane_below(rows)
    lane = lax.broadcasted_iota(jnp.int32, (rows, LANES), 1)
    scaled = q2_ref[...] * jnp.asarray(HD ** -0.5, bf16)
    ids_q = idc_ref[...]
    first, count = ranges_ref[0, step], ranges_ref[1, step]

    def place(j):
        wanted = (first + j * (tile // LANES)) * LANES
        return wanted, pl.multiple_of(jnp.minimum(wanted, keys - tile), LANES)

    def scores(j, tops):
        wanted, start = place(j)
        pos = start + lax.broadcasted_iota(jnp.int32, (1, tile), 1)
        ids_k = jnp.where(pos >= wanted, idr_ref[:, pl.ds(start, tile)], -1)
        bias = jnp.where(ids_q == ids_k, 0.0, masked_score).astype(f32)
        new = []
        for p in range(pairs):
            cols = slice(p * LANES, (p + 1) * LANES)
            kp = k2_ref[pl.ds(start, tile), cols]
            for h in range(2):
                s = mm(head_part(scaled[:, cols], h, low), kp, NT) + bias
                s_all[2 * p + h, j] = s
                top = s[:, :LANES]
                for c in range(1, tile // LANES):
                    top = jnp.maximum(top, s[:, c * LANES : (c + 1) * LANES])
                tops[2 * p + h] = jnp.maximum(tops[2 * p + h], top)
        return 0

    acc[...] = jnp.full(acc.shape, masked_score, f32)
    lax.fori_loop(0, count, lambda j, c: scores(j, acc), 0)
    peaks = [jnp.max(acc[head], axis=1, keepdims=True) for head in range(2 * pairs)]
    for head in range(2 * pairs):
        acc[head] = jnp.zeros((rows, LANES), f32)

    def mix(j, _):
        wanted, start = place(j)
        for head in range(2 * pairs):
            e = jnp.exp(s_all[head, j] - peaks[head]).astype(bf16)
            acc[head] += mm(e, vx_all[pl.ds(start, tile), head * LANES : (head + 1) * LANES])
        return 0

    lax.fori_loop(0, count, mix, 0)
    totals = jnp.zeros((rows, LANES), f32)
    for p in range(pairs):
        mixed = []
        for h in range(2):
            head = 2 * p + h
            o = acc[head]
            l = pltpu.roll(o, HD, 1)
            mixed.append(o / l)
            totals = jnp.where(lane == head, peaks[head] + jnp.log(jnp.where(low, l, 1.0)[:, :1]), totals)
        o_ref[:, p * LANES : (p + 1) * LANES] = jnp.where(
            low, mixed[0], pltpu.roll(mixed[1], HD, 1)
        ).astype(bf16)
    l_ref[...] = totals.T[: 2 * pairs, :]
    n1, _ = norm_rows(r1_ref[...])
    h1 = n1 * norms_ref[0:1, :] + norms_ref[1:2, :]
    r2_ref[...] = h1 + mm(o_ref[...], wco_ref[...])


def cross_forward(ranges, q2, k2, v2, r1, wco, norms, idc, idr, rows=256, tile=256, vmem=56 * 2**20):
    total, width = q2.shape
    keys = k2.shape[0]
    heads = width // HD
    rowspec = lambda w: pl.BlockSpec((rows, w), lambda i, *_: (i, 0))
    return pl.pallas_call(
        functools.partial(cross_forward_kernel, tile),
        grid_spec=pltpu.PrefetchScalarGridSpec(
            num_scalar_prefetch=1,
            grid=(total // rows,),
            in_specs=[rowspec(width), whole(k2), whole(v2), rowspec(width), whole(wco), whole(norms), rowspec(1), whole(idr)],
            out_specs=[rowspec(width), pl.BlockSpec((heads, rows), lambda i, *_: (0, i)), rowspec(width)],
            scratch_shapes=[
                pltpu.VMEM((keys, 2 * width), bf16),
                pltpu.VMEM((heads, keys // tile, rows, tile), f32),
                pltpu.VMEM((heads, rows, LANES), f32),
            ],
        ),
        out_shape=[
            jax.ShapeDtypeStruct((total, width), bf16),
            jax.ShapeDtypeStruct((heads, total), f32),
            jax.ShapeDtypeStruct((total, width), f32),
        ],
        compiler_params=pltpu.CompilerParams(vmem_limit_bytes=vmem),
        name="cross_forward",
    )(ranges, q2, k2, v2, r1, wco, norms, idc, idr)


def norm_back(incoming, normal, rstd, gain):
    m = incoming * gain
    return rstd * (
        m - jnp.mean(m, axis=-1, keepdims=True) - normal * jnp.mean(m * normal, axis=-1, keepdims=True)
    )


def head_sums(left, right):
    width = left.shape[1]
    prod = left.astype(f32) * right.astype(f32)
    heads = width // HD
    own = lax.broadcasted_iota(jnp.int32, (heads, width), 1) // HD == lax.broadcasted_iota(
        jnp.int32, (heads, width), 0
    )
    return lax.dot_general(
        own.astype(f32), prod, NT, preferred_element_type=f32, precision=lax.Precision.HIGHEST
    )


def column_sums(a):
    return jnp.sum(a, axis=0, keepdims=True)


def ffn_kernel(
    r2_ref, x_ref, cot_ref, o2_ref, win_ref, wout_ref, wco_ref, norms_ref,
    out_ref, dr3_ref, dr2_ref, do2_ref, delta_ref, gin_ref, gout_ref, gco_ref, gn_ref, gin, gout, gco,
):
    step = pl.program_id(0)
    last = pl.num_programs(0) - 1

    @pl.when(step == 0)
    def _():
        gin[...] = jnp.zeros_like(gin)
        gout[...] = jnp.zeros_like(gout)
        gco[...] = jnp.zeros_like(gco)
        gn_ref[...] = jnp.zeros_like(gn_ref)

    n2, rstd2 = norm_rows(r2_ref[...])
    h2 = n2 * norms_ref[2:3, :] + norms_ref[3:4, :]
    h2b = h2.astype(bf16)
    u = mm(h2b, win_ref[...])
    square = u * u
    t = jnp.tanh(0.7978845608028654 * u * (1.0 + 0.044715 * square))
    half = 0.5 * (1.0 + t)
    act = (u * half).astype(bf16)
    slope = half + 0.5 * u * (1.0 - t * t) * (0.7978845608028654 * (1.0 + 3 * 0.044715 * square))
    r3 = h2 + mm(act, wout_ref[...]) + x_ref[...].astype(f32)
    n3, rstd3 = norm_rows(r3)
    gain3 = norms_ref[4:5, :]
    out_ref[...] = (n3 * gain3 + norms_ref[5:6, :]).astype(bf16)
    e = cot_ref[...].astype(f32)
    gn_ref[2:3, :] += column_sums(e * n3)
    gn_ref[3:4, :] += column_sums(e)
    dr3 = norm_back(e, n3, rstd3, gain3)
    dr3_ref[...] = dr3
    dfb = dr3.astype(bf16)
    gout[...] += mm(act, dfb, TN)
    du = (mm(dfb, wout_ref[...], NT) * slope).astype(bf16)
    gin[...] += mm(h2b, du, TN)
    dh2 = dr3 + mm(du, win_ref[...], NT)
    gn_ref[0:1, :] += column_sums(dh2 * n2)
    gn_ref[1:2, :] += column_sums(dh2)
    dr2 = norm_back(dh2, n2, rstd2, norms_ref[2:3, :])
    dr2_ref[...] = dr2
    da2 = dr2.astype(bf16)
    o2 = o2_ref[...]
    gco[...] += mm(o2, da2, TN)
    do2 = mm(da2, wco_ref[...], NT).astype(bf16)
    do2_ref[...] = do2
    delta_ref[...] = head_sums(do2, o2)

    @pl.when(step == last)
    def _():
        gin_ref[...] = gin[...].astype(bf16)
        gout_ref[...] = gout[...].astype(bf16)
        gco_ref[...] = gco[...].astype(bf16)


def ffn(r2, x, cot, o2, win, wout, wco, norms, rows=256, vmem=56 * 2**20):
    total, width = x.shape
    heads = width // HD
    hidden = win.shape[1]
    rowspec = lambda w: pl.BlockSpec((rows, w), lambda i: (i, 0))
    fixed = lambda s: pl.BlockSpec(s, lambda i: (0, 0))
    sds = jax.ShapeDtypeStruct
    return pl.pallas_call(
        ffn_kernel,
        grid=(total // rows,),
        in_specs=[rowspec(width)] * 4 + [whole(a) for a in (win, wout, wco, norms)],
        out_specs=[rowspec(width)] * 4
        + [pl.BlockSpec((heads, rows), lambda i: (0, i)), fixed((width, hidden)), fixed((hidden, width)), fixed((width, width)), fixed((4, width))],
        out_shape=[
            sds((total, width), bf16), sds((total, width), f32), sds((total, width), f32), sds((total, width), bf16),
            sds((heads, total), f32), sds((width, hidden), bf16), sds((hidden, width), bf16), sds((width, width), bf16), sds((4, width), f32),
        ],
        scratch_shapes=[pltpu.VMEM((width, hidden), f32), pltpu.VMEM((hidden, width), f32), pltpu.VMEM((width, width), f32)],
        compiler_params=pltpu.CompilerParams(vmem_limit_bytes=vmem),
        name="ffn",
    )(r2, x, cot, o2, win, wout, wco, norms)


def tile_back(kp, vp, qp, dop, bias, logs, deltas, low_k):
    dks, dvs, dss, kms = [], [], [], []
    for h in range(2):
        km = head_part(kp, h, low_k)
        s = mm(km, qp, NT) + bias
        e = jnp.exp(s - logs[h])
        dp = mm(head_part(vp, h, low_k), dop, NT)
        ds = (e * (dp - deltas[h])).astype(bf16)
        dvs.append(mm(e.astype(bf16), dop))
        dks.append(mm(ds, qp))
        dss.append(ds)
        kms.append(km)
    dq = mm(jnp.concatenate(dss, axis=0), jnp.concatenate(kms, axis=0), TN)
    return jnp.where(low_k, dks[0], dks[1]), jnp.where(low_k, dvs[0], dvs[1]), dq


def cross_backward_kernel(
    tile, ranges_ref, q2_ref, k2_ref, v2_ref, do_ref, l_ref, delta_ref, idr_ref, idc_ref,
    dq_ref, dk_ref, dv_ref, dk, dv, dq,
):
    step = pl.program_id(0)
    rows, width = q2_ref.shape
    keys = k2_ref.shape[0]
    pairs = width // LANES

    @pl.when(step == 0)
    def _():
        dk[...] = jnp.zeros_like(dk)
        dv[...] = jnp.zeros_like(dv)

    dq[...] = jnp.zeros_like(dq)
    scaled = q2_ref[...] * jnp.asarray(HD ** -0.5, bf16)
    do = do_ref[...]
    ids_q = idr_ref[...]
    low_k = lane_below(tile)
    first, count = ranges_ref[0, step], ranges_ref[1, step]

    def one(j, _):
        wanted = (first + j * (tile // LANES)) * LANES
        start = pl.multiple_of(jnp.minimum(wanted, keys - tile), LANES)
        at = pl.ds(start, tile)
        pos = start + lax.broadcasted_iota(jnp.int32, (tile, 1), 0)
        ids_k = jnp.where(pos >= wanted, idc_ref[at, :], -1)
        bias = jnp.where(ids_q == ids_k, 0.0, masked_score).astype(f32)
        for p in range(pairs):
            cols = slice(p * LANES, (p + 1) * LANES)
            logs = [l_ref[2 * p + h : 2 * p + h + 1, :] for h in range(2)]
            deltas = [delta_ref[2 * p + h : 2 * p + h + 1, :] for h in range(2)]
            gk, gv, gq = tile_back(
                k2_ref[at, cols], v2_ref[at, cols], scaled[:, cols], do[:, cols], bias, logs, deltas, low_k
            )
            dk[at, cols] += gk
            dv[at, cols] += gv
            dq[:, cols] += gq
        return 0

    lax.fori_loop(0, count, one, 0)
    dq_ref[...] = (dq[...] * HD ** -0.5).astype(bf16)

    @pl.when(step == pl.num_programs(0) - 1)
    def _():
        dk_ref[...] = dk[...].astype(bf16)
        dv_ref[...] = dv[...].astype(bf16)


def cross_backward(ranges, q2, k2, v2, do, l, delta, idr, idc, rows=256, tile=256, vmem=56 * 2**20):
    total, width = q2.shape
    keys = k2.shape[0]
    heads = width // HD
    rowspec = lambda w: pl.BlockSpec((rows, w), lambda i, *_: (i, 0))
    cols = lambda h: pl.BlockSpec((h, rows), lambda i, *_: (0, i))
    sds = jax.ShapeDtypeStruct
    return pl.pallas_call(
        functools.partial(cross_backward_kernel, tile),
        grid_spec=pltpu.PrefetchScalarGridSpec(
            num_scalar_prefetch=1,
            grid=(total // rows,),
            in_specs=[rowspec(width), whole(k2), whole(v2), rowspec(width), cols(heads), cols(heads), cols(1), whole(idc)],
            out_specs=[rowspec(width), pl.BlockSpec((keys, width), lambda i, *_: (0, 0)), pl.BlockSpec((keys, width), lambda i, *_: (0, 0))],
            scratch_shapes=[pltpu.VMEM((keys, width), f32), pltpu.VMEM((keys, width), f32), pltpu.VMEM((rows, width), f32)],
        ),
        out_shape=[sds((total, width), bf16), sds((keys, width), bf16), sds((keys, width), bf16)],
        compiler_params=pltpu.CompilerParams(vmem_limit_bytes=vmem),
        name="cross_backward",
    )(ranges, q2, k2, v2, do, l, delta, idr, idc)


def between_kernel(
    r1_ref, dr2_ref, dq2_ref, h1b_ref, o1_ref, wcq_ref, wso_ref, norms_ref,
    dr1_ref, do1_ref, delta_ref, grads_ref, gn_ref, gcq, gso,
):
    step = pl.program_id(0)

    @pl.when(step == 0)
    def _():
        gcq[...] = jnp.zeros_like(gcq)
        gso[...] = jnp.zeros_like(gso)
        gn_ref[...] = jnp.zeros_like(gn_ref)

    dq2 = dq2_ref[...]
    dh1 = dr2_ref[...] + mm(dq2, wcq_ref[...], NT)
    n1, rstd1 = norm_rows(r1_ref[...])
    gn_ref[0:1, :] += column_sums(dh1 * n1)
    gn_ref[1:2, :] += column_sums(dh1)
    dr1 = norm_back(dh1, n1, rstd1, norms_ref[0:1, :])
    dr1_ref[...] = dr1
    da1 = dr1.astype(bf16)
    o1 = o1_ref[...]
    do1 = mm(da1, wso_ref[...], NT).astype(bf16)
    do1_ref[...] = do1
    delta_ref[...] = head_sums(do1, o1)
    gcq[...] += mm(h1b_ref[...], dq2, TN)
    gso[...] += mm(o1, da1, TN)

    @pl.when(step == pl.num_programs(0) - 1)
    def _():
        grads_ref[0] = gcq[...].astype(bf16)
        grads_ref[1] = gso[...].astype(bf16)


def between(r1, dr2, dq2, h1b, o1, wcq, wso, norms, rows=256, vmem=40 * 2**20):
    total, width = r1.shape
    heads = width // HD
    rowspec = lambda w: pl.BlockSpec((rows, w), lambda i: (i, 0))
    fixed = lambda s: pl.BlockSpec(s, lambda i: (0, 0))
    sds = jax.ShapeDtypeStruct
    return pl.pallas_call(
        between_kernel,
        grid=(total // rows,),
        in_specs=[rowspec(width)] * 5 + [whole(a) for a in (wcq, wso, norms)],
        out_specs=[rowspec(width)] * 2 + [pl.BlockSpec((heads, rows), lambda i: (0, i)), pl.BlockSpec((2, width, width), lambda i: (0, 0, 0)), fixed((2, width))],
        out_shape=[sds((total, width), f32), sds((total, width), bf16), sds((heads, total), f32), sds((2, width, width), bf16), sds((2, width), f32)],
        scratch_shapes=[pltpu.VMEM((width, width), f32), pltpu.VMEM((width, width), f32)],
        compiler_params=pltpu.CompilerParams(vmem_limit_bytes=vmem),
        name="between",
    )(r1, dr2, dq2, h1b, o1, wcq, wso, norms)


def self_backward_kernel(
    block, q_ref, k_ref, v_ref, do_ref, l_ref, delta_ref, idc_ref, idr_ref, x_ref, wq_ref, wk_ref, wv_ref, dr1_ref, dr3_ref,
    gx_ref, grads_ref, dq, dk, dv, gq, gk, gv,
):
    step = pl.program_id(0)
    rows, width = k_ref.shape
    total = q_ref.shape[0]
    window = MOST + block
    pairs = width // LANES

    @pl.when(step == 0)
    def _():
        dq[...] = jnp.zeros_like(dq)
        gq[...] = jnp.zeros_like(gq)
        gk[...] = jnp.zeros_like(gk)
        gv[...] = jnp.zeros_like(gv)

    base = pl.multiple_of(step * rows, rows)
    low_k = lane_below(block)
    for sub in range(rows // block):
        here = slice(sub * block, (sub + 1) * block)
        start = pl.multiple_of(jnp.minimum(base + sub * block, total - window), LANES)
        at = pl.ds(start, window)
        pos_k = base + sub * block + lax.broadcasted_iota(jnp.int32, (block, window), 0)
        pos_q = start + lax.broadcasted_iota(jnp.int32, (block, window), 1)
        bias = jnp.where((idc_ref[here, :] == idr_ref[:, at]) & (pos_k <= pos_q), 0.0, masked_score).astype(f32)
        for p in range(pairs):
            cols = slice(p * LANES, (p + 1) * LANES)
            logs = [l_ref[2 * p + h : 2 * p + h + 1, at] for h in range(2)]
            deltas = [delta_ref[2 * p + h : 2 * p + h + 1, at] for h in range(2)]
            hk, hv, hq = tile_back(
                k_ref[here, cols], v_ref[here, cols], q_ref[at, cols] * jnp.asarray(HD ** -0.5, bf16), do_ref[at, cols],
                bias, logs, deltas, low_k,
            )
            dk[here, cols] = hk.astype(bf16)
            dv[here, cols] = hv.astype(bf16)
            dq[at, cols] += hq
    x = x_ref[...]
    dqb = (dq[pl.ds(base, rows), :] * HD ** -0.5).astype(bf16)
    dkb, dvb = dk[...], dv[...]
    gx = dr1_ref[...] + dr3_ref[...] + mm(dqb, wq_ref[...], NT) + mm(dkb, wk_ref[...], NT) + mm(dvb, wv_ref[...], NT)
    gx_ref[...] = gx.astype(bf16)
    gq[...] += mm(x, dqb, TN)
    gk[...] += mm(x, dkb, TN)
    gv[...] += mm(x, dvb, TN)

    @pl.when(step == pl.num_programs(0) - 1)
    def _():
        grads_ref[0] = gq[...].astype(bf16)
        grads_ref[1] = gk[...].astype(bf16)
        grads_ref[2] = gv[...].astype(bf16)


def self_backward(q, k, v, do, l, delta, idc, idr, x, wq, wk, wv, dr1, dr3, rows=256, block=256, vmem=48 * 2**20):
    total, width = x.shape
    rowspec = lambda w: pl.BlockSpec((rows, w), lambda i: (i, 0))
    fixed = lambda s: pl.BlockSpec(s, lambda i: (0, 0))
    sds = jax.ShapeDtypeStruct
    return pl.pallas_call(
        functools.partial(self_backward_kernel, block),
        grid=(total // rows,),
        in_specs=[whole(q), rowspec(width), rowspec(width), whole(do), whole(l), whole(delta), rowspec(1), whole(idr), rowspec(width)]
        + [whole(a) for a in (wq, wk, wv)] + [rowspec(width)] * 2,
        out_specs=[rowspec(width), pl.BlockSpec((3, width, width), lambda i: (0, 0, 0))],
        out_shape=[sds((total, width), bf16), sds((3, width, width), bf16)],
        scratch_shapes=[pltpu.VMEM((total, width), f32), pltpu.VMEM((rows, width), bf16), pltpu.VMEM((rows, width), bf16)]
        + [pltpu.VMEM((width, width), f32)] * 3,
        compiler_params=pltpu.CompilerParams(vmem_limit_bytes=vmem),
        name="self_backward",
    )(q, k, v, do, l, delta, idc, idr, x, wq, wk, wv, dr1, dr3)


def segment_ids(lengths, row_count):
    ends = jnp.cumsum(lengths)
    places = jnp.arange(row_count, dtype=jnp.int32)
    return jnp.sum((places[:, None] >= ends[None, :]).astype(jnp.int32), axis=1)


def cross_ranges(seg, mem, total, rows, tile):
    ends = jnp.cumsum(seg)
    starts = jnp.arange(0, total, rows, dtype=jnp.int32)
    head = starts[:, None] >= ends[None, :]
    tail = (starts + rows - 1)[:, None] >= ends[None, :]
    mem = mem[: seg.shape[0]]
    low = jnp.sum(jnp.where(head, mem[None, :], 0), axis=1)
    before = jnp.concatenate([jnp.ones((starts.shape[0], 1), bool), tail[:, :-1]], axis=1)
    high = jnp.sum(jnp.where(before, mem[None, :], 0), axis=1)
    first = low // LANES
    count = (high - first * LANES + tile - 1) // tile
    return jnp.stack([first, count]).astype(jnp.int32)


def index_bits():
    sizes = lax.axis_size("dp"), lax.axis_size("fsdp")
    count = (sizes[0] * sizes[1]).bit_length() - 1
    me = lax.axis_index("dp") * sizes[1] + lax.axis_index("fsdp")
    return count, me


def swap(x, b):
    count = lax.axis_size("dp") * lax.axis_size("fsdp")
    return lax.ppermute(x, ("dp", "fsdp"), [(i, i ^ (1 << b)) for i in range(count)])


def gather(x, order, lead=0):
    _, me = index_bits()
    have = []
    for b in order:
        mine = (me >> b) & 1 == 0
        other = swap(x, b)
        place = lead + sum(1 for h in have if h > b)
        x = jnp.stack([jnp.where(mine, x, other), jnp.where(mine, other, x)], axis=place)
        have.append(b)
    return x.reshape(x.shape[:lead] + (-1, x.shape[-1]))


def scatter_sum(x, order, lead=0, kind=bf16):
    count, me = index_bits()
    x = x.reshape(x.shape[:lead] + (2,) * count + (-1, x.shape[-1]))
    have = list(range(count))
    for b in order:
        mine = (me >> b) & 1
        place = lead + sum(1 for h in have if h > b)
        other = swap(lax.dynamic_index_in_dim(x, 1 - mine, place, keepdims=False), b)
        own = lax.dynamic_index_in_dim(x, mine, place, keepdims=False)
        have.remove(b)
        x = own.astype(f32) + other.astype(f32)
        if have:
            x = x.astype(kind)
    return x


def body(
    inputs, memory, seg_lengths, mem_lengths, self_query, self_key, self_value, self_out,
    cross_query, cross_key, cross_value, cross_out, ffn_in, ffn_out, norm_params, cotangent,
):
    total, width = inputs.shape
    keys = memory.shape[0]
    count, _ = index_bits()
    up, down = list(range(count)), list(range(count))[::-1]
    tile = 256

    def rows_of(flat, columns):
        return flat.reshape(-1, columns)

    first = gather(jnp.stack([rows_of(w, width) for w in (self_query, self_key, self_value)]), down, 1)
    wsq, wsk, wsv = first[0], first[1], first[2]
    second = gather(
        jnp.stack([rows_of(w, width) for w in (self_out, cross_query, cross_key, cross_value, cross_out)]), down, 1
    )
    wso, wcq, wck, wcv, wco = (second[i] for i in range(5))
    win = gather(rows_of(ffn_in, ffn_in.shape[0] * (1 << count) // width), down)
    wout = gather(rows_of(ffn_out, width), down)
    norms = gather(norm_params.reshape(1, -1), down).reshape(6, width)

    qid, mid = segment_ids(seg_lengths[0], total), segment_ids(mem_lengths[0], keys)
    qc, qr, mc, mr = qid[:, None], qid[None, :], mid[:, None], mid[None, :]
    ranges = cross_ranges(seg_lengths[0], mem_lengths[0], total, 256, tile)
    q1, k1, v1, o1, l1, r1, h1b, q2 = self_forward(inputs, wsq, wsk, wsv, wso, wcq, norms, qc, qr, block=256)
    k2 = mm(memory, wck).astype(bf16)
    v2 = mm(memory, wcv).astype(bf16)
    o2, l2, r2 = cross_forward(ranges, q2, k2, v2, r1, wco, norms, qc, mr, tile=tile)
    out, dr3, dr2, do2, delta2, gfi, gfo, gco, gn23 = ffn(r2, inputs, cotangent, o2, win, wout, wco, norms)
    gfi, gfo, gco = (scatter_sum(g, up) for g in (gfi, gfo, gco))
    dq2, dk2, dv2 = cross_backward(ranges, q2, k2, v2, do2, l2, delta2, qr, mc, tile=tile)
    gckv = scatter_sum(jnp.stack([mm(memory, dk2, TN).astype(bf16), mm(memory, dv2, TN).astype(bf16)]), up, 1)
    dr1, do1, delta1, gcqso, gn1 = between(r1, dr2, dq2, h1b, o1, wcq, wso, norms)
    gcqso = scatter_sum(gcqso, up, 1)
    gn = scatter_sum(jnp.concatenate([gn1, gn23]).reshape(1 << count, -1), up, kind=f32)
    gx, gself = self_backward(q1, k1, v1, do1, l1, delta1, qc, qr, inputs, wsq, wsk, wsv, dr1, dr3)
    gself = scatter_sum(gself, up, 1)
    gm = (mm(dk2, wck, NT) + mm(dv2, wcv, NT)).astype(bf16)
    flat = lambda g: g.reshape(-1)
    return (
        out, gx, gm, flat(gself[0]), flat(gself[1]), flat(gself[2]), flat(gcqso[1]),
        flat(gcqso[0]), flat(gckv[0]), flat(gckv[1]), flat(gco), flat(gfi), flat(gfo), flat(gn),
    )


def solution(mesh):
    rows, flat = P(("dp", "fsdp"), None), P(("dp", "fsdp"))
    return jax.shard_map(
        body,
        mesh=mesh,
        in_specs=(rows,) * 4 + (flat,) * 11 + (rows,),
        out_specs=(rows,) * 3 + (flat,) * 11,
        check_vma=False,
    )
```

time: 1320 us -> 384 us (0.29)
  blocking collectives: 395 us -> 0 us
  matrix products: 377 us -> 15.6 us
  Pallas kernels: 0 us -> 137 us
  waiting for transfers between devices: 236 us -> 102 us
  other arithmetic: 141 us -> 15.1 us
  local copies, waits for them, and re-layouts: 141 us -> 31 us
  starting transfers between devices: 0.11 us -> 73.2 us
    dot_general x58 -> x6, matrix products: 377 us -> 15.6 us  [mm(): return lax.dot_general(left, right, dims, preferred_element_type=f32)]
    all_gather x8 -> x0, blocking collectives: 314 us -> none  [the longest x1 42.2 us: body(): lax.all_gather(self_query, ('dp', 'fsdp'), axis=0, tiled=True)]
    unnamed x4 -> x0, waiting for transfers between devices: 236 us -> none
    pallas_call x0 -> x6, Pallas kernels: none -> 137 us  [the longest x1 35.1 us: cross_backward(): pl.pallas_call(functools.partial(cross_backward_kernel, tile), grid_spec=...]
    ppermute x0 -> x60, waiting for transfers between devices: none -> 102 us  [swap(): lax.ppermute(x, ('dp', 'fsdp'), [(i, i ^ 1 << b) for i in range(count)])]
    convert_element_type x9 -> x24, other arithmetic: 91 us -> 6.1 us  [scatter_sum(): x = x.astype(kind)]
    unnamed x2 -> x0, blocking collectives: 81.2 us -> none
    ppermute x0 -> x60, starting transfers between devices: none -> 73.2 us  [swap(): lax.ppermute(x, ('dp', 'fsdp'), [(i, i ^ 1 << b) for i in range(count)])]
  transfers between devices with their start and end apart: 3 -> 60, of which waited for: 1 -> 36; matrix products, arithmetic and copies ran while one was open for 15% -> 10% of each run, Pallas kernels for 0% -> 5%
where the time goes in v1:
time: 384 us; the launch traced here: 377 us
  Pallas kernels  137 us (36%)
  waiting for transfers between devices  102 us (27%)
  starting transfers between devices  73.2 us (19%)
  local copies, waits for them, and re-layouts  31 us (8%)
  matrix products  15.6 us (4%)
  other arithmetic  15.1 us (4%)
    ppermute x60, waiting for transfers between devices, swap(): lax.ppermute(x, ('dp', 'fsdp'), [(i, i ^ 1 << b) for i in range(count)])  102 us
    ppermute x60, starting transfers between devices, swap(): lax.ppermute(x, ('dp', 'fsdp'), [(i, i ^ 1 << b) for i in range(count)])  73.2 us
    pallas_call x1, Pallas kernels, cross_backward(): pl.pallas_call(functools.partial(cross_backward_kernel, tile), grid_spec=...  35.1 us
    pallas_call x1, Pallas kernels, ffn(): pl.pallas_call(ffn_kernel, grid=(total // rows,), in_specs=[rowspec(width...  31.4 us
    pallas_call x1, Pallas kernels, cross_forward(): pl.pallas_call(functools.partial(cross_forward_kernel, tile), grid_spec=p...  24.2 us
    pallas_call x1, Pallas kernels, self_forward(): pl.pallas_call(functools.partial(self_forward_kernel, block), grid=(steps...  20.1 us
    pallas_call x1, Pallas kernels, self_backward(): pl.pallas_call(functools.partial(self_backward_kernel, block), grid=(tota...  19.8 us
    dot_general x6, matrix products, mm(): return lax.dot_general(left, right, dims, preferred_element_type=f32)  15.6 us
  transfers between devices with their start and end apart: 60, of which 36 were waited for; matrix products, arithmetic and copies ran while one was open for 10% of the time, Pallas kernels for 5%

profile of v1, /device:TPU:0, one launch (start us, length us, event | category | flops | bytes accessed | tf_op | source)
XLA Modules:
  0.0 376.6 jit_solution(12341117326070167498)
XLA Ops:
  1.7 4.1 %collective-permute-start.20 = (bf16[64,512]{1,0:T(8,128)(2,1)S(1)}, bf16[64,512]{1,0:T(8,128)(2,1)S(1)}, u32[]{:S(2)}, u32[]{:S(2)}) collective-permute-start(bf16[64,512]{1,0:T(8,128)(2,1)S(1)} %reshape.328), channel_id=1, source_target_pairs={{0,16},{1,17},{2,18},{3,19},{4,20},{5,21},{6,22},{7,23},{8,24},{9,... | collective-permute-start | bytes 196616 | tf_op jit(solution)/shard_map/ppermute | solution.py:582
  10.5 3.0 collective-permute-start.5
  15.9 2.9 collective-permute-start
  26.6 1.9 collective-permute-done.12
  30.2 2.0 collective-permute-done.13
  34.7 1.6 collective-permute-start.1
  37.0 1.6 collective-permute-start.16
  55.3 4.0 %collective-permute-done.17 = bf16[2,2,16,2048]{3,2,1,0:T(8,128)(2,1)S(1)} collective-permute-done((bf16[2,2,16,2048]{3,2,1,0:T(8,128)(2,1)S(1)}, bf16[2,2,16,2048]{3,2,1,0:T(8,128)(2,1)S(1)}, u32[]{:S(2)}, u32[]{:S(2)}) %collective-permute-start.17) | collective-permute-done | bytes 262176 | tf_op jit(solution)/shard_map/ppermute | solution.py:582
  60.9 4.0 %collective-permute-done.7 = bf16[5,2,2,16,512]{4,3,2,1,0:T(8,128)(2,1)S(1)} collective-permute-done((bf16[5,2,2,16,512]{4,3,2,1,0:T(8,128)(2,1)S(1)}, bf16[5,2,2,16,512]{4,3,2,1,0:T(8,128)(2,1)S(1)}, u32[]{:S(2)}, u32[]{:S(2)}) %collective-permute-start.7) | collective-permute-done | bytes 327712 | tf_op jit(solution)/shard_map/ppermute | solution.py:582
  66.8 7.4 %collective-permute-done.23 = bf16[2,2,2,64,512]{4,3,2,1,0:T(8,128)(2,1)S(1)} collective-permute-done((bf16[2,2,2,64,512]{4,3,2,1,0:T(8,128)(2,1)S(1)}, bf16[2,2,2,64,512]{4,3,2,1,0:T(8,128)(2,1)S(1)}, u32[]{:S(2)}, u32[]{:S(2)}) %collective-permute-start.23) | collective-permute-done | bytes 524320 | tf_op jit(solution)/shard_map/ppermute | solution.py:582
  74.5 11.0 %collective-permute-done.18 = bf16[2,2,2,16,2048]{4,3,2,1,0:T(8,128)(2,1)S(1)} collective-permute-done((bf16[2,2,2,16,2048]{4,3,2,1,0:T(8,128)(2,1)S(1)}, bf16[2,2,2,16,2048]{4,3,2,1,0:T(8,128)(2,1)S(1)}, u32[]{:S(2)}, u32[]{:S(2)}) %collective-permute-start.18) | collective-permute-done | bytes 524320 | tf_op jit(solution)/shard_map/ppermute | solution.py:582
  85.7 12.2 %collective-permute-done.8 = bf16[5,2,2,2,16,512]{5,4,3,2,1,0:T(8,128)(2,1)S(1)} collective-permute-done((bf16[5,2,2,2,16,512]{5,4,3,2,1,0:T(8,128)(2,1)S(1)}, bf16[5,2,2,2,16,512]{5,4,3,2,1,0:T(8,128)(2,1)S(1)}, u32[]{:S(2)}, u32[]{:S(2)}) %collective-permute-start.8) | collective-permute-done | bytes 655392 | tf_op jit(solution)/shard_map/ppermute | solution.py:582
  103.1 2.6 fusion.k2_ref
  105.6 2.6 fusion.1.v2_ref
  108.2 20.1 %self_forward.1 = (bf16[1024,512]{1,0:T(8,128)(2,1)S(1)}, bf16[1024,512]{1,0:T(8,128)(2,1)S(1)}, bf16[1024,512]{1,0:T(8,128)(2,1)}, bf16[1024,512]{1,0:T(8,128)(...) custom-call(bf16[1024,512]{1,0:T(8,128)(2,1)} %x_ref.5, ...), custom_call_target="tpu_custom_call" | custom-call | tf_op jit(solution)/shard_map/self_forward/pallas_call | solution.py:123
  130.3 24.2 %cross_forward.1 = (bf16[1024,512]{1,0:T(8,128)(2,1)}, f32[8,1024]{1,0:T(8,128)}, f32[1024,512]{1,0:T(8,128)}) custom-call(s32[2,4]{1,0:T(2,128)} %pad_add_fusion.ranges_ref, bf16[1024,512]{1,0:T(8,128)(2,1)} %get-tuple-element.44.q2_ref, bf16[2048,512]{1,0:T(8,128)(2,1)} %fusion.k2_ref, bf16[2048,512]{1,0:T(8,128)(2,1)} %fusion.1.v2_ref, ...), custom_call_target="tpu_custom_call" | custom-call | tf_op jit(solution)/shard_map/cross_forward/pallas_call | solution.py:219
  154.5 31.4 %ffn.1 = (bf16[1024,512]{1,0:T(8,128)(2,1)}, f32[1024,512]{1,0:T(8,128)}, f32[1024,512]{1,0:T(8,128)}, bf16[1024,512]{1,0:T(8,128)(2,1)}, f32[8,1024]{1,0:T(8,12...) custom-call(f32[1024,512]{1,0:T(8,128)} %get-tuple-element.46.r2_ref, ...), custom_call_target="tpu_custom_call" | custom-call | tf_op jit(solution)/shard_map/ffn/pallas_call | solution.py:327
  185.9 35.1 %cross_backward.1 = (bf16[1024,512]{1,0:T(8,128)(2,1)}, bf16[2048,512]{1,0:T(8,128)(2,1)}, bf16[2048,512]{1,0:T(8,128)(2,1)}) custom-call(s32[2,4]{1,0:T(2,128)} %pad_add_fusion.ranges_ref, bf16[1024,512]{1,0:T(8,128)(2,1)} %get-tuple-element.44.q2_ref, bf16[2048,512]{1,0:T(8,128)(2,1)} %fusion.k2_ref, bf16[2048,512]{1,0:T(8,128)(2,1)} %fusion.1.v2_ref, ...), custom_call_target="tpu_custom_call" | custom-call | tf_op jit(solution)/shard_map/cross_backward/pallas_call | solution.py:415
  221.0 3.0 convolution_convert_fusion.3
  224.2 3.4 fusion.60
  228.9 6.8 %between.1 = (f32[1024,512]{1,0:T(8,128)S(1)}, bf16[1024,512]{1,0:T(8,128)(2,1)S(1)}, f32[8,1024]{1,0:T(8,128)S(1)}, bf16[2,512,512]{2,1,0:T(8,128)(2,1)S(1)}, f32[2,512]{1,0:T(2,128)S(1)}) custom-call(f32[1024,512]{1,0:T(8,128)S(1)} %copy-done.1, f32[1024,512]{1,0:T(8,128)S(1)} %copy-done.9, bf16[1024,512]{1,0:T(8,128)(2,1)S(1)} %copy-done.20, ...), custom_call_target="tpu_custom_call" | custom-call | tf_op jit(solution)/shard_map/between/pallas_call | solution.py:469
  239.3 2.5 dynamic-slice_bitcast_fusion
  246.2 2.6 add_convert_fusion
  248.9 19.8 %self_backward.1 = (bf16[1024,512]{1,0:T(8,128)(2,1)}, bf16[3,512,512]{2,1,0:T(8,128)(2,1)}) custom-call(bf16[1024,512]{1,0:T(8,128)(2,1)S(1)} %copy-done.13, bf16[1024,512]{1,0:T(8,128)(2,1)S(1)} %copy-done.15, bf16[1024,512]{1,0:T(8,128)(2,1)S(1)} %copy-done.16, bf16[1024,512]{1,0:T(8,128)(2,1)} %copy-done.17, f32[8,1024]{1,0:T(8,128)S(1)} %get-tuple-element.60.l_ref, ...), custom_call_target="tpu_custom_call" | custom-call | tf_op jit(solution)/shard_map/self_backward/pallas_call | solution.py:539
  276.1 3.0 collective-permute-done.41
  280.8 1.9 collective-permute-done.58
  284.2 2.7 collective-permute-done.42
  287.0 1.7 collective-permute-start.43
  288.7 2.3 collective-permute-done.43
  291.0 3.1 collective-permute-start.59
  295.5 2.9 collective-permute-start.44
  301.1 2.1 collective-permute-start.36
  303.5 6.8 %collective-permute-done.36 = bf16[2,2,2,2,16,512]{5,4,3,2,1,0:T(8,128)(2,1)S(1)} collective-permute-done((bf16[2,2,2,2,16,512]{5,4,3,2,1,0:T(8,128)(2,1)S(1)}, bf16[2,2,2,2,16,512]{5,4,3,2,1,0:T(8,128)(2,1)S(1)}, u32[]{:S(2)}, u32[]{:S(2)}) %collective-permute-start.36) | collective-permute-done | bytes 262176 | tf_op jit(solution)/shard_map/ppermute | solution.py:582
  310.4 1.7 collective-permute-start.37
  312.1 3.6 collective-permute-done.31
  317.9 1.8 collective-permute-start.26
  321.3 1.6 collective-permute-start.33
  324.5 3.3 collective-permute-start.39
  334.3 1.7 fusion.2
  337.2 2.7 collective-permute-done.27
  340.1 1.6 fusion.3
  341.7 3.5 collective-permute-done.28
  347.4 2.9 collective-permute-done.29
  352.5 5.9 %collective-permute-done.46 = bf16[2,2,2,16,2048]{4,3,2,1,0:T(8,128)(2,1)S(1)} collective-permute-done((bf16[2,2,2,16,2048]{4,3,2,1,0:T(8,128)(2,1)S(1)}, bf16[2,2,2,16,2048]{4,3,2,1,0:T(8,128)(2,1)S(1)}, u32[]{:S(2)}, u32[]{:S(2)}) %collective-permute-start.46) | collective-permute-done | bytes 524320 | tf_op jit(solution)/shard_map/ppermute | solution.py:582
  358.6 1.6 collective-permute-start.47
  360.5 4.6 %collective-permute-done.47 = bf16[2,2,16,2048]{3,2,1,0:T(8,128)(2,1)S(1)} collective-permute-done((bf16[2,2,16,2048]{3,2,1,0:T(8,128)(2,1)S(1)}, bf16[2,2,16,2048]{3,2,1,0:T(8,128)(2,1)S(1)}, u32[]{:S(2)}, u32[]{:S(2)}) %collective-permute-start.47) | collective-permute-done | bytes 262176 | tf_op jit(solution)/shard_map/ppermute | solution.py:582
  367.3 2.4 collective-permute-start.54
  370.3 3.1 collective-permute-start.49
  (341 shorter events, 95.8 us)
Async XLA Ops:
  1.7 34.7 %collective-permute-start.20 = (bf16[64,512]{1,0:T(8,128)(2,1)S(1)}, bf16[64,512]{1,0:T(8,128)(2,1)S(1)}, u32[]{:S(2)}, u32[]{:S(2)}) collective-permute-start(bf16[64,512]{1,0:T(8,128)(2,1)S(1)} %reshape.328), channel_id=1, source_target_pairs={{0,16},{1,17},{2,18},{3,19},{4,20},{5,21},{6,22},{7,23},{8,24},{9,... | collective-permute-start | bytes 196616 | tf_op jit(solution)/shard_map/ppermute | solution.py:582
  6.7 30.2 %collective-permute-start.15 = (bf16[16,2048]{1,0:T(8,128)(2,1)S(1)}, bf16[16,2048]{1,0:T(8,128)(2,1)S(1)}, u32[]{:S(2)}, u32[]{:S(2)}) collective-permute-start(bf16[16,2048]{1,0:T(8,128)(2,1)S(1)} %reshape.326), channel_id=1, source_target_pairs={{0,16},{1,17},{2,18},{3,19},{4,20},{5,21},{6,22},{7,23},{8,24},{9,... | collective-permute-start | bytes 196616 | tf_op jit(solution)/shard_map/ppermute | solution.py:582
  10.5 28.1 %collective-permute-start.5 = (bf16[5,16,512]{2,1,0:T(8,128)(2,1)S(1)}, bf16[5,16,512]{2,1,0:T(8,128)(2,1)S(1)}, u32[]{:S(2)}, u32[]{:S(2)}) collective-permute-start(bf16[5,16,512]{2,1,0:T(8,128)(2,1)S(1)} %constant_dynamic-update-slice_fusion.3), channel_id=1, source_target_pairs={{0,16},{1,17},{2,18},{3,19},{4,20},{5,21},{6,22},{7,23},{8,24},{9,... | collective-permute-start | bytes 245768 | tf_op jit(solution)/shard_map/ppermute | solution.py:582
  13.5 7.1 %collective-permute-start.10 = (f32[1,96]{1,0:T(1,128)}, f32[1,96]{1,0:T(1,128)S(1)}, u32[]{:S(2)}, u32[]{:S(2)}) collective-permute-start(f32[1,96]{1,0:T(1,128)} %bitcast.509), channel_id=1, source_target_pairs={{0,16},{1,17},{2,18},{3,19},{4,20},{5,21},{6,22},{7,23},{8,24},{9,... | collective-permute-start | bytes 1160 | tf_op jit(solution)/shard_map/ppermute | solution.py:582
  15.9 18.8 %collective-permute-start = (bf16[3,16,512]{2,1,0:T(8,128)(2,1)S(1)}, bf16[3,16,512]{2,1,0:T(8,128)(2,1)S(1)}, u32[]{:S(2)}, u32[]{:S(2)}) collective-permute-start(bf16[3,16,512]{2,1,0:T(8,128)(2,1)S(1)} %constant_dynamic-update-slice_fusion), channel_id=1, source_target_pairs={{0,16},{1,17},{2,18},{3,19},{4,20},{5,21},{6,22},{7,23},{8,24},{9,... | collective-permute-start | bytes 147464 | tf_op jit(solution)/shard_map/ppermute | solution.py:582
  34.7 5.7 %collective-permute-start.1 = (bf16[3,2,16,512]{3,2,1,0:T(8,128)(2,1)S(1)}, bf16[3,2,16,512]{3,2,1,0:T(8,128)(2,1)S(1)}, u32[]{:S(2)}, u32[]{:S(2)}) collective-permute-start(bf16[3,2,16,512]{3,2,1,0:T(8,128)(2,1)S(1)} %pad_maximum_fusion.19), channel_id=1, source_target_pairs={{0,8},{1,9},{2,10},{3,11},{4,12},{5,13},{6,14},{7,15},{8,0},{9,1},... | collective-permute-start | bytes 294920 | tf_op jit(solution)/shard_map/ppermute | solution.py:582
  36.4 6.8 %collective-permute-start.21 = (bf16[2,64,512]{2,1,0:T(8,128)(2,1)S(1)}, bf16[2,64,512]{2,1,0:T(8,128)(2,1)S(1)}, u32[]{:S(2)}, u32[]{:S(2)}) collective-permute-start(bf16[2,64,512]{2,1,0:T(8,128)(2,1)S(1)} %pad_maximum_fusion.18), channel_id=1, source_target_pairs={{0,8},{1,9},{2,10},{3,11},{4,12},{5,13},{6,14},{7,15},{8,0},{9,1},... | collective-permute-start | bytes 393224 | tf_op jit(solution)/shard_map/ppermute | solution.py:582
  37.0 9.0 %collective-permute-start.16 = (bf16[2,16,2048]{2,1,0:T(8,128)(2,1)S(1)}, bf16[2,16,2048]{2,1,0:T(8,128)(2,1)S(1)}, u32[]{:S(2)}, u32[]{:S(2)}) collective-permute-start(bf16[2,16,2048]{2,1,0:T(8,128)(2,1)S(1)} %pad_maximum_fusion.17), channel_id=1, source_target_pairs={{0,8},{1,9},{2,10},{3,11},{4,12},{5,13},{6,14},{7,15},{8,0},{9,1},... | collective-permute-start | bytes 393224 | tf_op jit(solution)/shard_map/ppermute | solution.py:582
  38.7 10.5 %collective-permute-start.6 = (bf16[5,2,16,512]{3,2,1,0:T(8,128)(2,1)S(1)}, bf16[5,2,16,512]{3,2,1,0:T(8,128)(2,1)S(1)}, u32[]{:S(2)}, u32[]{:S(2)}) collective-permute-start(bf16[5,2,16,512]{3,2,1,0:T(8,128)(2,1)S(1)} %pad_maximum_fusion.16), channel_id=1, source_target_pairs={{0,8},{1,9},{2,10},{3,11},{4,12},{5,13},{6,14},{7,15},{8,0},{9,1},... | collective-permute-start | bytes 491528 | tf_op jit(solution)/shard_map/ppermute | solution.py:582
  40.4 10.3 %collective-permute-start.2 = (bf16[3,2,2,16,512]{4,3,2,1,0:T(8,128)(2,1)S(1)}, bf16[3,2,2,16,512]{4,3,2,1,0:T(8,128)(2,1)S(1)}, u32[]{:S(2)}, u32[]{:S(2)}) collective-permute-start(bf16[3,2,2,16,512]{4,3,2,1,0:T(8,128)(2,1)S(1)} %pad_maximum_fusion.15), channel_id=1, source_target_pairs={{0,4},{1,5},{2,6},{3,7},{4,0},{5,1},{6,2},{7,3},{8,12},{9,13},{10,... | collective-permute-start | bytes 589832 | tf_op jit(solution)/shard_map/ppermute | solution.py:582
  43.2 10.4 %collective-permute-start.22 = (bf16[2,2,64,512]{3,2,1,0:T(8,128)(2,1)S(1)}, bf16[2,2,64,512]{3,2,1,0:T(8,128)(2,1)S(1)}, u32[]{:S(2)}, u32[]{:S(2)}) collective-permute-start(bf16[2,2,64,512]{3,2,1,0:T(8,128)(2,1)S(1)} %pad_maximum_fusion.14), channel_id=1, source_target_pairs={{0,4},{1,5},{2,6},{3,7},{4,0},{5,1},{6,2},{7,3},{8,12},{9,13},{10,... | collective-permute-start | bytes 786440 | tf_op jit(solution)/shard_map/ppermute | solution.py:582
  46.1 13.2 %collective-permute-start.17 = (bf16[2,2,16,2048]{3,2,1,0:T(8,128)(2,1)S(1)}, bf16[2,2,16,2048]{3,2,1,0:T(8,128)(2,1)S(1)}, u32[]{:S(2)}, u32[]{:S(2)}) collective-permute-start(bf16[2,2,16,2048]{3,2,1,0:T(8,128)(2,1)S(1)} %pad_maximum_fusion.13), channel_id=1, source_target_pairs={{0,4},{1,5},{2,6},{3,7},{4,0},{5,1},{6,2},{7,3},{8,12},{9,13},{10,... | collective-permute-start | bytes 786440 | tf_op jit(solution)/shard_map/ppermute | solution.py:582
  49.2 15.7 %collective-permute-start.7 = (bf16[5,2,2,16,512]{4,3,2,1,0:T(8,128)(2,1)S(1)}, bf16[5,2,2,16,512]{4,3,2,1,0:T(8,128)(2,1)S(1)}, u32[]{:S(2)}, u32[]{:S(2)}) collective-permute-start(bf16[5,2,2,16,512]{4,3,2,1,0:T(8,128)(2,1)S(1)} %pad_maximum_fusion.12), channel_id=1, source_target_pairs={{0,4},{1,5},{2,6},{3,7},{4,0},{5,1},{6,2},{7,3},{8,12},{9,13},{10,... | collective-permute-start | bytes 983048 | tf_op jit(solution)/shard_map/ppermute | solution.py:582
  50.8 15.7 %collective-permute-start.3 = (bf16[3,2,2,2,16,512]{5,4,3,2,1,0:T(8,128)(2,1)S(1)}, bf16[3,2,2,2,16,512]{5,4,3,2,1,0:T(8,128)(2,1)S(1)}, u32[]{:S(2)}, u32[]{:S(2)}) collective-permute-start(bf16[3,2,2,2,16,512]{5,4,3,2,1,0:T(8,128)(2,1)S(1)} %pad_maximum_fusion.11), channel_id=1, source_target_pairs={{0,2},{1,3},{2,0},{3,1},{4,6},{5,7},{6,4},{7,5},{8,10},{9,11},{10,... | collective-permute-start | bytes 1179656 | tf_op jit(solution)/shard_map/ppermute | solution.py:582
  53.7 20.5 %collective-permute-start.23 = (bf16[2,2,2,64,512]{4,3,2,1,0:T(8,128)(2,1)S(1)}, bf16[2,2,2,64,512]{4,3,2,1,0:T(8,128)(2,1)S(1)}, u32[]{:S(2)}, u32[]{:S(2)}) collective-permute-start(bf16[2,2,2,64,512]{4,3,2,1,0:T(8,128)(2,1)S(1)} %pad_maximum_fusion.10), channel_id=1, source_target_pairs={{0,2},{1,3},{2,0},{3,1},{4,6},{5,7},{6,4},{7,5},{8,10},{9,11},{10,... | collective-permute-start | bytes 1572872 | tf_op jit(solution)/shard_map/ppermute | solution.py:582
  59.3 26.1 %collective-permute-start.18 = (bf16[2,2,2,16,2048]{4,3,2,1,0:T(8,128)(2,1)S(1)}, bf16[2,2,2,16,2048]{4,3,2,1,0:T(8,128)(2,1)S(1)}, u32[]{:S(2)}, u32[]{:S(2)}) collective-permute-start(bf16[2,2,2,16,2048]{4,3,2,1,0:T(8,128)(2,1)S(1)} %pad_maximum_fusion.9), channel_id=1, source_target_pairs={{0,2},{1,3},{2,0},{3,1},{4,6},{5,7},{6,4},{7,5},{8,10},{9,11},{10,... | collective-permute-start | bytes 1572872 | tf_op jit(solution)/shard_map/ppermute | solution.py:582
  65.0 32.9 %collective-permute-start.8 = (bf16[5,2,2,2,16,512]{5,4,3,2,1,0:T(8,128)(2,1)S(1)}, bf16[5,2,2,2,16,512]{5,4,3,2,1,0:T(8,128)(2,1)S(1)}, u32[]{:S(2)}, u32[]{:S(2)}) collective-permute-start(bf16[5,2,2,2,16,512]{5,4,3,2,1,0:T(8,128)(2,1)S(1)} %pad_maximum_fusion.6), channel_id=1, source_target_pairs={{0,2},{1,3},{2,0},{3,1},{4,6},{5,7},{6,4},{7,5},{8,10},{9,11},{10,... | collective-permute-start | bytes 1966088 | tf_op jit(solution)/shard_map/ppermute | solution.py:582
  66.7 31.5 %collective-permute-start.4 = (bf16[3,2,2,2,2,16,512]{6,5,4,3,2,1,0:T(8,128)(2,1)S(1)}, bf16[3,2,2,2,2,16,512]{6,5,4,3,2,1,0:T(8,128)(2,1)S(1)}, u32[]{:S(2)}, u32[]{:S(2)}) collective-permute-start(bf16[3,2,2,2,2,16,512]{6,5,4,3,2,1,0:T(8,128)(2,1)S(1)} %pad_maximum_fusion.5), channel_id=1, source_target_pairs={{0,1},{1,0},{2,3},{3,2},{4,5},{5,4},{6,7},{7,6},{8,9},{9,8},{10,11... | collective-permute-start | bytes 2359304 | tf_op jit(solution)/shard_map/ppermute | solution.py:582
  74.4 24.1 %collective-permute-start.24 = (bf16[2,2,2,2,64,512]{5,4,3,2,1,0:T(8,128)(2,1)S(1)}, bf16[2,2,2,2,64,512]{5,4,3,2,1,0:T(8,128)(2,1)S(1)}, u32[]{:S(2)}, u32[]{:S(2)}) collective-permute-start(bf16[2,2,2,2,64,512]{5,4,3,2,1,0:T(8,128)(2,1)S(1)} %pad_maximum_fusion.4), channel_id=1, source_target_pairs={{0,1},{1,0},{2,3},{3,2},{4,5},{5,4},{6,7},{7,6},{8,9},{9,8},{10,11... | collective-permute-start | bytes 3145736 | tf_op jit(solution)/shard_map/ppermute | solution.py:582
  85.6 14.6 %collective-permute-start.19 = (bf16[2,2,2,2,16,2048]{5,4,3,2,1,0:T(8,128)(2,1)S(1)}, bf16[2,2,2,2,16,2048]{5,4,3,2,1,0:T(8,128)(2,1)S(1)}, u32[]{:S(2)}, u32[]{:S(2)}) collective-permute-start(bf16[2,2,2,2,16,2048]{5,4,3,2,1,0:T(8,128)(2,1)S(1)} %pad_maximum_fusion.3), channel_id=1, source_target_pairs={{0,1},{1,0},{2,3},{3,2},{4,5},{5,4},{6,7},{7,6},{8,9},{9,8},{10,11... | collective-permute-start | bytes 3145736 | tf_op jit(solution)/shard_map/ppermute | solution.py:582
  239.2 29.5 %collective-permute-start.55 = (f32[2,2,2,2,1,96]{5,2,1,0,4,3:T(2,128)S(1)}, f32[2,2,2,2,1,96]{5,2,1,0,4,3:T(2,128)S(1)}, u32[]{:S(2)}, u32[]{:S(2)}) collective-permute-start(f32[2,2,2,2,1,96]{5,2,1,0,4,3:T(2,128)S(1)} %bitcast.502), channel_id=1, source_target_pairs={{0,1},{1,0},{2,3},{3,2},{4,5},{5,4},{6,7},{7,6},{8,9},{9,8},{10,11... | collective-permute-start | bytes 18440 | tf_op jit(solution)/shard_map/ppermute | solution.py:582
  241.8 92.5 %collective-permute-start.50 = (bf16[2,2,2,2,64,512]{5,4,3,2,1,0:T(8,128)(2,1)}, bf16[2,2,2,2,64,512]{5,4,3,2,1,0:T(8,128)(2,1)}, u32[]{:S(2)}, u32[]{:S(2)}) collective-permute-start(bf16[2,2,2,2,64,512]{5,4,3,2,1,0:T(8,128)(2,1)} %dynamic-slice_bitcast_fusion), channel_id=1, source_target_pairs={{0,1},{1,0},{2,3},{3,2},{4,5},{5,4},{6,7},{7,6},{8,9},{9,8},{10,11... | collective-permute-start | bytes 3145736 | tf_op jit(solution)/shard_map/ppermute | solution.py:582
  243.3 96.8 %collective-permute-start.45 = (bf16[2,2,2,2,16,2048]{5,4,3,2,1,0:T(8,128)(2,1)}, bf16[2,2,2,2,16,2048]{5,4,3,2,1,0:T(8,128)(2,1)}, u32[]{:S(2)}, u32[]{:S(2)}) collective-permute-start(bf16[2,2,2,2,16,2048]{5,4,3,2,1,0:T(8,128)(2,1)} %dynamic-slice_bitcast_fusion.1), channel_id=1, source_target_pairs={{0,1},{1,0},{2,3},{3,2},{4,5},{5,4},{6,7},{7,6},{8,9},{9,8},{10,11... | collective-permute-start | bytes 3145736 | tf_op jit(solution)/shard_map/ppermute | solution.py:582
  243.4 29.6 %collective-permute-start.40 = (bf16[2,2,2,2,16,512]{5,4,3,2,1,0:T(8,128)(2,1)S(1)}, bf16[2,2,2,2,16,512]{5,4,3,2,1,0:T(8,128)(2,1)}, u32[]{:S(2)}, u32[]{:S(2)}) collective-permute-start(bf16[2,2,2,2,16,512]{5,4,3,2,1,0:T(8,128)(2,1)S(1)} %dynamic-slice_bitcast_fusion.9), channel_id=1, source_target_pairs={{0,1},{1,0},{2,3},{3,2},{4,5},{5,4},{6,7},{7,6},{8,9},{9,8},{10,11... | collective-permute-start | bytes 786440 | tf_op jit(solution)/shard_map/ppermute | solution.py:582
  245.4 55.4 %collective-permute-start.35 = (bf16[2,2,2,2,2,16,512]{6,5,4,3,2,1,0:T(8,128)(2,1)S(1)}, bf16[2,2,2,2,2,16,512]{6,5,4,3,2,1,0:T(8,128)(2,1)S(1)}, u32[]{:S(2)}, u32[]{:S(2)}) collective-permute-start(bf16[2,2,2,2,2,16,512]{6,5,4,3,2,1,0:T(8,128)(2,1)S(1)} %fusion.11), channel_id=1, source_target_pairs={{0,1},{1,0},{2,3},{3,2},{4,5},{5,4},{6,7},{7,6},{8,9},{9,8},{10,11... | collective-permute-start | bytes 1572872 | tf_op jit(solution)/shard_map/ppermute | solution.py:582
  274.1 5.0 %collective-permute-start.41 = (bf16[2,2,2,16,512]{4,3,2,1,0:T(8,128)(2,1)S(1)}, bf16[2,2,2,16,512]{4,3,2,1,0:T(8,128)(2,1)S(1)}, u32[]{:S(2)}, u32[]{:S(2)}) collective-permute-start(bf16[2,2,2,16,512]{4,3,2,1,0:T(8,128)(2,1)S(1)} %dynamic-slice_bitcast_fusion.15), channel_id=1, source_target_pairs={{0,2},{1,3},{2,0},{3,1},{4,6},{5,7},{6,4},{7,5},{8,10},{9,11},{10,... | collective-permute-start | bytes 393224 | tf_op jit(solution)/shard_map/ppermute | solution.py:582
  276.1 27.1 %collective-permute-start.30 = (bf16[2,2,2,2,2,16,512]{6,5,4,3,2,1,0:T(8,128)(2,1)S(1)}, bf16[2,2,2,2,2,16,512]{6,5,4,3,2,1,0:T(8,128)(2,1)S(1)}, u32[]{:S(2)}, u32[]{:S(2)}) collective-permute-start(bf16[2,2,2,2,2,16,512]{6,5,4,3,2,1,0:T(8,128)(2,1)S(1)} %dynamic-slice_bitcast_fusion.5), channel_id=1, source_target_pairs={{0,1},{1,0},{2,3},{3,2},{4,5},{5,4},{6,7},{7,6},{8,9},{9,8},{10,11... | collective-permute-start | bytes 1572872 | tf_op jit(solution)/shard_map/ppermute | solution.py:582
  300.2 17.3 %collective-permute-start.25 = (bf16[3,2,2,2,2,16,512]{6,5,4,3,2,1,0:T(8,128)(2,1)S(1)}, bf16[3,2,2,2,2,16,512]{6,5,4,3,2,1,0:T(8,128)(2,1)S(1)}, u32[]{:S(2)}, u32[]{:S(2)}) collective-permute-start(bf16[3,2,2,2,2,16,512]{6,5,4,3,2,1,0:T(8,128)(2,1)S(1)} %dynamic-slice_bitcast_fusion.2), channel_id=1, source_target_pairs={{0,1},{1,0},{2,3},{3,2},{4,5},{5,4},{6,7},{7,6},{8,9},{9,8},{10,11... | collective-permute-start | bytes 2359304 | tf_op jit(solution)/shard_map/ppermute | solution.py:582
  301.1 9.2 %collective-permute-start.36 = (bf16[2,2,2,2,16,512]{5,4,3,2,1,0:T(8,128)(2,1)S(1)}, bf16[2,2,2,2,16,512]{5,4,3,2,1,0:T(8,128)(2,1)S(1)}, u32[]{:S(2)}, u32[]{:S(2)}) collective-permute-start(bf16[2,2,2,2,16,512]{5,4,3,2,1,0:T(8,128)(2,1)S(1)} %dynamic-slice_bitcast_fusion.10), channel_id=1, source_target_pairs={{0,2},{1,3},{2,0},{3,1},{4,6},{5,7},{6,4},{7,5},{8,10},{9,11},{10,... | collective-permute-start | bytes 786440 | tf_op jit(solution)/shard_map/ppermute | solution.py:582
  303.4 12.4 %collective-permute-start.31 = (bf16[2,2,2,2,16,512]{5,4,3,2,1,0:T(8,128)(2,1)S(1)}, bf16[2,2,2,2,16,512]{5,4,3,2,1,0:T(8,128)(2,1)S(1)}, u32[]{:S(2)}, u32[]{:S(2)}) collective-permute-start(bf16[2,2,2,2,16,512]{5,4,3,2,1,0:T(8,128)(2,1)S(1)} %dynamic-slice_bitcast_fusion.11), channel_id=1, source_target_pairs={{0,2},{1,3},{2,0},{3,1},{4,6},{5,7},{6,4},{7,5},{8,10},{9,11},{10,... | collective-permute-start | bytes 786440 | tf_op jit(solution)/shard_map/ppermute | solution.py:582
  310.4 9.2 %collective-permute-start.37 = (bf16[2,2,2,16,512]{4,3,2,1,0:T(8,128)(2,1)S(1)}, bf16[2,2,2,16,512]{4,3,2,1,0:T(8,128)(2,1)S(1)}, u32[]{:S(2)}, u32[]{:S(2)}) collective-permute-start(bf16[2,2,2,16,512]{4,3,2,1,0:T(8,128)(2,1)S(1)} %dynamic-slice_bitcast_fusion.16), channel_id=1, source_target_pairs={{0,4},{1,5},{2,6},{3,7},{4,0},{5,1},{6,2},{7,3},{8,12},{9,13},{10,... | collective-permute-start | bytes 393224 | tf_op jit(solution)/shard_map/ppermute | solution.py:582
  315.9 5.4 %collective-permute-start.32 = (bf16[2,2,2,16,512]{4,3,2,1,0:T(8,128)(2,1)S(1)}, bf16[2,2,2,16,512]{4,3,2,1,0:T(8,128)(2,1)S(1)}, u32[]{:S(2)}, u32[]{:S(2)}) collective-permute-start(bf16[2,2,2,16,512]{4,3,2,1,0:T(8,128)(2,1)S(1)} %dynamic-slice_bitcast_fusion.17), channel_id=1, source_target_pairs={{0,4},{1,5},{2,6},{3,7},{4,0},{5,1},{6,2},{7,3},{8,12},{9,13},{10,... | collective-permute-start | bytes 393224 | tf_op jit(solution)/shard_map/ppermute | solution.py:582
  317.9 16.1 %collective-permute-start.26 = (bf16[3,2,2,2,16,512]{5,4,3,2,1,0:T(8,128)(2,1)S(1)}, bf16[3,2,2,2,16,512]{5,4,3,2,1,0:T(8,128)(2,1)S(1)}, u32[]{:S(2)}, u32[]{:S(2)}) collective-permute-start(bf16[3,2,2,2,16,512]{5,4,3,2,1,0:T(8,128)(2,1)S(1)} %dynamic-slice_bitcast_fusion.6), channel_id=1, source_target_pairs={{0,2},{1,3},{2,0},{3,1},{4,6},{5,7},{6,4},{7,5},{8,10},{9,11},{10,... | collective-permute-start | bytes 1179656 | tf_op jit(solution)/shard_map/ppermute | solution.py:582
  319.7 4.7 %collective-permute-start.38 = (bf16[2,2,16,512]{3,2,1,0:T(8,128)(2,1)S(1)}, bf16[2,2,16,512]{3,2,1,0:T(8,128)(2,1)S(1)}, u32[]{:S(2)}, u32[]{:S(2)}) collective-permute-start(bf16[2,2,16,512]{3,2,1,0:T(8,128)(2,1)S(1)} %dynamic-slice_bitcast_fusion.22), channel_id=1, source_target_pairs={{0,8},{1,9},{2,10},{3,11},{4,12},{5,13},{6,14},{7,15},{8,0},{9,1},... | collective-permute-start | bytes 196616 | tf_op jit(solution)/shard_map/ppermute | solution.py:582
  321.3 6.5 %collective-permute-start.33 = (bf16[2,2,16,512]{3,2,1,0:T(8,128)(2,1)S(1)}, bf16[2,2,16,512]{3,2,1,0:T(8,128)(2,1)S(1)}, u32[]{:S(2)}, u32[]{:S(2)}) collective-permute-start(bf16[2,2,16,512]{3,2,1,0:T(8,128)(2,1)S(1)} %dynamic-slice_bitcast_fusion.23), channel_id=1, source_target_pairs={{0,8},{1,9},{2,10},{3,11},{4,12},{5,13},{6,14},{7,15},{8,0},{9,1},... | collective-permute-start | bytes 196616 | tf_op jit(solution)/shard_map/ppermute | solution.py:582
  324.5 5.6 %collective-permute-start.39 = (bf16[2,16,512]{2,1,0:T(8,128)(2,1)S(1)}, bf16[2,16,512]{2,1,0:T(8,128)(2,1)S(1)}, u32[]{:S(2)}, u32[]{:S(2)}) collective-permute-start(bf16[2,16,512]{2,1,0:T(8,128)(2,1)S(1)} %dynamic-slice_bitcast_fusion.26), channel_id=1, source_target_pairs={{0,16},{1,17},{2,18},{3,19},{4,20},{5,21},{6,22},{7,23},{8,24},{9,... | collective-permute-start | bytes 98312 | tf_op jit(solution)/shard_map/ppermute | solution.py:582
  327.8 4.9 %collective-permute-start.34 = (bf16[2,16,512]{2,1,0:T(8,128)(2,1)S(1)}, bf16[2,16,512]{2,1,0:T(8,128)(2,1)S(1)}, u32[]{:S(2)}, u32[]{:S(2)}) collective-permute-start(bf16[2,16,512]{2,1,0:T(8,128)(2,1)S(1)} %dynamic-slice_bitcast_fusion.27), channel_id=1, source_target_pairs={{0,16},{1,17},{2,18},{3,19},{4,20},{5,21},{6,22},{7,23},{8,24},{9,... | collective-permute-start | bytes 98312 | tf_op jit(solution)/shard_map/ppermute | solution.py:582
  334.2 5.7 %collective-permute-start.27 = (bf16[3,2,2,16,512]{4,3,2,1,0:T(8,128)(2,1)S(1)}, bf16[3,2,2,16,512]{4,3,2,1,0:T(8,128)(2,1)S(1)}, u32[]{:S(2)}, u32[]{:S(2)}) collective-permute-start(bf16[3,2,2,16,512]{4,3,2,1,0:T(8,128)(2,1)S(1)} %dynamic-slice_bitcast_fusion.12), channel_id=1, source_target_pairs={{0,4},{1,5},{2,6},{3,7},{4,0},{5,1},{6,2},{7,3},{8,12},{9,13},{10,... | collective-permute-start | bytes 589832 | tf_op jit(solution)/shard_map/ppermute | solution.py:582
  336.0 16.2 %collective-permute-start.51 = (bf16[2,2,2,64,512]{4,3,2,1,0:T(8,128)(2,1)S(1)}, bf16[2,2,2,64,512]{4,3,2,1,0:T(8,128)(2,1)S(1)}, u32[]{:S(2)}, u32[]{:S(2)}) collective-permute-start(bf16[2,2,2,64,512]{4,3,2,1,0:T(8,128)(2,1)S(1)} %dynamic-slice_bitcast_fusion.3), channel_id=1, source_target_pairs={{0,2},{1,3},{2,0},{3,1},{4,6},{5,7},{6,4},{7,5},{8,10},{9,11},{10,... | collective-permute-start | bytes 1572872 | tf_op jit(solution)/shard_map/ppermute | solution.py:582
  340.0 5.2 %collective-permute-start.28 = (bf16[3,2,16,512]{3,2,1,0:T(8,128)(2,1)S(1)}, bf16[3,2,16,512]{3,2,1,0:T(8,128)(2,1)S(1)}, u32[]{:S(2)}, u32[]{:S(2)}) collective-permute-start(bf16[3,2,16,512]{3,2,1,0:T(8,128)(2,1)S(1)} %dynamic-slice_bitcast_fusion.18), channel_id=1, source_target_pairs={{0,8},{1,9},{2,10},{3,11},{4,12},{5,13},{6,14},{7,15},{8,0},{9,1},... | collective-permute-start | bytes 294920 | tf_op jit(solution)/shard_map/ppermute | solution.py:582
  345.3 5.1 %collective-permute-start.29 = (bf16[3,16,512]{2,1,0:T(8,128)(2,1)S(1)}, bf16[3,16,512]{2,1,0:T(8,128)(2,1)S(1)}, u32[]{:S(2)}, u32[]{:S(2)}) collective-permute-start(bf16[3,16,512]{2,1,0:T(8,128)(2,1)S(1)} %dynamic-slice_bitcast_fusion.24), channel_id=1, source_target_pairs={{0,16},{1,17},{2,18},{3,19},{4,20},{5,21},{6,22},{7,23},{8,24},{9,... | collective-permute-start | bytes 147464 | tf_op jit(solution)/shard_map/ppermute | solution.py:582
  346.0 12.4 %collective-permute-start.46 = (bf16[2,2,2,16,2048]{4,3,2,1,0:T(8,128)(2,1)S(1)}, bf16[2,2,2,16,2048]{4,3,2,1,0:T(8,128)(2,1)S(1)}, u32[]{:S(2)}, u32[]{:S(2)}) collective-permute-start(bf16[2,2,2,16,2048]{4,3,2,1,0:T(8,128)(2,1)S(1)} %dynamic-slice_bitcast_fusion.4), channel_id=1, source_target_pairs={{0,2},{1,3},{2,0},{3,1},{4,6},{5,7},{6,4},{7,5},{8,10},{9,11},{10,... | collective-permute-start | bytes 1572872 | tf_op jit(solution)/shard_map/ppermute | solution.py:582
  352.4 7.8 %collective-permute-start.52 = (bf16[2,2,64,512]{3,2,1,0:T(8,128)(2,1)S(1)}, bf16[2,2,64,512]{3,2,1,0:T(8,128)(2,1)S(1)}, u32[]{:S(2)}, u32[]{:S(2)}) collective-permute-start(bf16[2,2,64,512]{3,2,1,0:T(8,128)(2,1)S(1)} %dynamic-slice_bitcast_fusion.7), channel_id=1, source_target_pairs={{0,4},{1,5},{2,6},{3,7},{4,0},{5,1},{6,2},{7,3},{8,12},{9,13},{10,... | collective-permute-start | bytes 786440 | tf_op jit(solution)/shard_map/ppermute | solution.py:582
  358.6 6.4 %collective-permute-start.47 = (bf16[2,2,16,2048]{3,2,1,0:T(8,128)(2,1)S(1)}, bf16[2,2,16,2048]{3,2,1,0:T(8,128)(2,1)S(1)}, u32[]{:S(2)}, u32[]{:S(2)}) collective-permute-start(bf16[2,2,16,2048]{3,2,1,0:T(8,128)(2,1)S(1)} %dynamic-slice_bitcast_fusion.8), channel_id=1, source_target_pairs={{0,4},{1,5},{2,6},{3,7},{4,0},{5,1},{6,2},{7,3},{8,12},{9,13},{10,... | collective-permute-start | bytes 786440 | tf_op jit(solution)/shard_map/ppermute | solution.py:582
  360.4 6.9 %collective-permute-start.53 = (bf16[2,64,512]{2,1,0:T(8,128)(2,1)S(1)}, bf16[2,64,512]{2,1,0:T(8,128)(2,1)S(1)}, u32[]{:S(2)}, u32[]{:S(2)}) collective-permute-start(bf16[2,64,512]{2,1,0:T(8,128)(2,1)S(1)} %dynamic-slice_bitcast_fusion.13), channel_id=1, source_target_pairs={{0,8},{1,9},{2,10},{3,11},{4,12},{5,13},{6,14},{7,15},{8,0},{9,1},... | collective-permute-start | bytes 393224 | tf_op jit(solution)/shard_map/ppermute | solution.py:582
  365.2 5.0 %collective-permute-start.48 = (bf16[2,16,2048]{2,1,0:T(8,128)(2,1)S(1)}, bf16[2,16,2048]{2,1,0:T(8,128)(2,1)S(1)}, u32[]{:S(2)}, u32[]{:S(2)}) collective-permute-start(bf16[2,16,2048]{2,1,0:T(8,128)(2,1)S(1)} %dynamic-slice_bitcast_fusion.14), channel_id=1, source_target_pairs={{0,8},{1,9},{2,10},{3,11},{4,12},{5,13},{6,14},{7,15},{8,0},{9,1},... | collective-permute-start | bytes 393224 | tf_op jit(solution)/shard_map/ppermute | solution.py:582
  367.3 6.5 %collective-permute-start.54 = (bf16[64,512]{1,0:T(8,128)(2,1)S(1)}, bf16[64,512]{1,0:T(8,128)(2,1)S(1)}, u32[]{:S(2)}, u32[]{:S(2)}) collective-permute-start(bf16[64,512]{1,0:T(8,128)(2,1)S(1)} %dynamic-slice_bitcast_fusion.19), channel_id=1, source_target_pairs={{0,16},{1,17},{2,18},{3,19},{4,20},{5,21},{6,22},{7,23},{8,24},{9,... | collective-permute-start | bytes 196616 | tf_op jit(solution)/shard_map/ppermute | solution.py:582
  370.3 5.4 %collective-permute-start.49 = (bf16[16,2048]{1,0:T(8,128)(2,1)S(1)}, bf16[16,2048]{1,0:T(8,128)(2,1)S(1)}, u32[]{:S(2)}, u32[]{:S(2)}) collective-permute-start(bf16[16,2048]{1,0:T(8,128)(2,1)S(1)} %dynamic-slice_bitcast_fusion.20), channel_id=1, source_target_pairs={{0,16},{1,17},{2,18},{3,19},{4,20},{5,21},{6,22},{7,23},{8,24},{9,... | collective-permute-start | bytes 196616 | tf_op jit(solution)/shard_map/ppermute | solution.py:582
  (52 other events, 615.4 us)

commit v2 on v1

v2 whole, which is shorter than its diff:
```python
import functools
import jax
import jax.numpy as jnp
from jax import lax
from jax.experimental import pallas as pl
from jax.experimental.pallas import tpu as pltpu
from jax.sharding import PartitionSpec as P

HD = 64
LANES = 128
MOST = 256
masked_score = -1e30
norm_eps = 1e-05
bf16, f32 = jnp.bfloat16, jnp.float32
NT = (((1,), (1,)), ((), ()))
TN = (((0,), (0,)), ((), ()))
NN = (((1,), (0,)), ((), ()))


def mm(left, right, dims=NN):
    return lax.dot_general(left, right, dims, preferred_element_type=f32)


def norm_rows(source):
    mean = jnp.mean(source, axis=-1, keepdims=True)
    centered = source - mean
    variance = jnp.mean(centered * centered, axis=-1, keepdims=True)
    rstd = lax.rsqrt(variance + norm_eps)
    return centered * rstd, rstd


def lane_below(rows):
    return lax.broadcasted_iota(jnp.int32, (rows, LANES), 1) < HD


def column_of(row):
    return jnp.broadcast_to(row, (LANES, row.shape[1])).T


def head_part(pair, which, low):
    return jnp.where(low == (which == 0), pair, jnp.zeros_like(pair))


def values_with_ones(values, low):
    parts = []
    for p in range(values.shape[1] // LANES):
        pair = values[:, p * LANES : (p + 1) * LANES]
        one = jnp.ones_like(pair)
        parts.append(jnp.where(low, pair, one))
        parts.append(jnp.where(low, pltpu.roll(pair, HD, 1), one))
    return jnp.concatenate(parts, axis=1)


def self_forward_kernel(block, x_ref, wq_ref, wk_ref, wv_ref, idr_ref, *rest):
    q_ref, k_ref, v_ref, o_ref, l_ref, k_all, vx_all = rest[-7:]
    step = pl.program_id(0)
    rows = x_ref.shape[0]
    width = k_ref.shape[1]
    window = MOST + block
    pairs = width // LANES
    x = x_ref[...]
    q = mm(x, wq_ref[0]).astype(bf16)
    k = mm(x, wk_ref[0]).astype(bf16)
    v = mm(x, wv_ref[0]).astype(bf16)
    q_ref[...] = q
    k_ref[...] = k
    v_ref[...] = v

    @pl.when(step == 0)
    def _():
        k_all[...] = jnp.zeros_like(k_all)
        vx_all[...] = jnp.zeros_like(vx_all)

    base = pl.multiple_of(step * rows, rows)
    k_all[pl.ds(base, rows), :] = k
    vx_all[pl.ds(base, rows), :] = values_with_ones(v, lane_below(rows))
    scaled = q * jnp.asarray(HD ** -0.5, bf16)
    low = lane_below(block)
    lane = lax.broadcasted_iota(jnp.int32, (block, LANES), 1)
    for sub in range(rows // block):
        start = pl.multiple_of(jnp.maximum(base + sub * block - MOST, 0), LANES)
        ids_q = column_of(idr_ref[:, pl.ds(base + sub * block, block)])[:, :1]
        ids_k = idr_ref[:, pl.ds(start, window)]
        pos_q = base + sub * block + lax.broadcasted_iota(jnp.int32, (block, window), 0)
        pos_k = start + lax.broadcasted_iota(jnp.int32, (block, window), 1)
        bias = jnp.where((ids_q == ids_k) & (pos_k <= pos_q), 0.0, masked_score).astype(f32)
        totals = jnp.zeros((block, LANES), f32)
        for p in range(pairs):
            cols = slice(p * LANES, (p + 1) * LANES)
            qp = scaled[sub * block : (sub + 1) * block, cols]
            kp = k_all[pl.ds(start, window), cols]
            mixed = []
            for h in range(2):
                s = mm(head_part(qp, h, low), kp, NT) + bias
                m = jnp.max(s, axis=1, keepdims=True)
                e = jnp.exp(s - m).astype(bf16)
                head = 2 * p + h
                o = mm(e, vx_all[pl.ds(start, window), head * LANES : (head + 1) * LANES])
                l = pltpu.roll(o, HD, 1)
                mixed.append(o / l)
                totals = jnp.where(lane == head, m + jnp.log(jnp.where(low, l, 1.0)[:, :1]), totals)
            o_ref[sub * block : (sub + 1) * block, cols] = jnp.where(
                low, mixed[0], pltpu.roll(mixed[1], HD, 1)
            ).astype(bf16)
        l_ref[:, sub * block : (sub + 1) * block] = totals.T[: 2 * pairs, :]


def whole(a):
    return pl.BlockSpec(a.shape, lambda *_: (0,) * a.ndim)


def part(weights, index, columns, half):
    return pl.BlockSpec((1, weights.shape[1], columns), lambda *_: (index, 0, half))


def params(us, vmem):
    return dict(
        compiler_params=pltpu.CompilerParams(vmem_limit_bytes=vmem * 2**20),
        cost_estimate=pl.CostEstimate(flops=us * 10**9, bytes_accessed=2**20, transcendentals=0),
    )


apart = pl.BlockSpec(memory_space=pl.ANY)


def self_forward(x, weights, idr, half, after, rows=256, block=256):
    total, width = x.shape
    columns = width // 2
    heads = columns // HD
    rowspec = lambda w: pl.BlockSpec((rows, w), lambda i: (i, 0))
    full = jax.ShapeDtypeStruct((total, columns), bf16)
    return pl.pallas_call(
        functools.partial(self_forward_kernel, block),
        grid=(total // rows,),
        in_specs=[rowspec(width)] + [part(weights, i, columns, half) for i in range(3)] + [whole(idr)]
        + [apart] * len(after),
        out_specs=[rowspec(columns)] * 4 + [pl.BlockSpec((heads, rows), lambda i: (0, i))],
        out_shape=[full] * 4 + [jax.ShapeDtypeStruct((heads, total), f32)],
        scratch_shapes=[pltpu.VMEM((total, columns), bf16), pltpu.VMEM((total, 2 * columns), bf16)],
        name="self_forward",
        **params(8, 24),
    )(x, weights, weights, weights, idr, *after)


def project_memory_kernel(memory_ref, wk_ref, wv_ref, k_ref, v_ref):
    memory = memory_ref[...]
    k_ref[...] = mm(memory, wk_ref[0]).astype(bf16)
    v_ref[...] = mm(memory, wv_ref[0]).astype(bf16)


def project_memory(memory, weights, index, rows=512):
    keys, width = memory.shape
    rowspec = pl.BlockSpec((rows, width), lambda i: (i, 0))
    return pl.pallas_call(
        project_memory_kernel,
        grid=(keys // rows,),
        in_specs=[rowspec, part(weights, index, width, 0), part(weights, index + 1, width, 0)],
        out_specs=[rowspec] * 2,
        out_shape=[jax.ShapeDtypeStruct((keys, width), bf16)] * 2,
        name="project_memory",
        **params(5, 24),
    )(memory, weights, weights)


def cross_forward_kernel(
    tile, ranges_ref, x_ref, oa_ref, ob_ref, wso_ref, wcq_ref, wco_ref, norms_ref, k2_ref, v2_ref, idq_ref, idr_ref,
    r1_ref, h1b_ref, q2_ref, o_ref, l_ref, r2_ref, vx_all, s_all, acc,
):
    step = pl.program_id(0)
    rows, width = x_ref.shape
    keys = k2_ref.shape[0]
    pairs = width // LANES

    @pl.when(step == 0)
    def _():
        def fill(j, _):
            at = pl.ds(pl.multiple_of(j * tile, tile), tile)
            vx_all[at, :] = values_with_ones(v2_ref[at, :], lane_below(tile))
            return 0

        lax.fori_loop(0, keys // tile, fill, 0)

    half = width // 2
    r1 = x_ref[...].astype(f32) + mm(oa_ref[...], wso_ref[0, :half, :]) + mm(ob_ref[...], wso_ref[0, half:, :])
    r1_ref[...] = r1
    n1, _ = norm_rows(r1)
    h1 = n1 * norms_ref[0:1, :] + norms_ref[1:2, :]
    h1b = h1.astype(bf16)
    h1b_ref[...] = h1b
    q2 = mm(h1b, wcq_ref[0]).astype(bf16)
    q2_ref[...] = q2
    low = lane_below(rows)
    lane = lax.broadcasted_iota(jnp.int32, (rows, LANES), 1)
    scaled = q2 * jnp.asarray(HD ** -0.5, bf16)
    ids_q = column_of(idq_ref[...])[:, :1]
    first, count = ranges_ref[0, step], ranges_ref[1, step]

    def place(j):
        wanted = (first + j * (tile // LANES)) * LANES
        return wanted, pl.multiple_of(jnp.minimum(wanted, keys - tile), LANES)

    def scores(j, tops):
        wanted, start = place(j)
        pos = start + lax.broadcasted_iota(jnp.int32, (1, tile), 1)
        ids_k = jnp.where(pos >= wanted, idr_ref[:, pl.ds(start, tile)], -1)
        bias = jnp.where(ids_q == ids_k, 0.0, masked_score).astype(f32)
        new = []
        for p in range(pairs):
            cols = slice(p * LANES, (p + 1) * LANES)
            kp = k2_ref[pl.ds(start, tile), cols]
            for h in range(2):
                s = mm(head_part(scaled[:, cols], h, low), kp, NT) + bias
                s_all[2 * p + h, j] = s
                top = s[:, :LANES]
                for c in range(1, tile // LANES):
                    top = jnp.maximum(top, s[:, c * LANES : (c + 1) * LANES])
                tops[2 * p + h] = jnp.maximum(tops[2 * p + h], top)
        return 0

    acc[...] = jnp.full(acc.shape, masked_score, f32)
    lax.fori_loop(0, count, lambda j, c: scores(j, acc), 0)
    peaks = [jnp.max(acc[head], axis=1, keepdims=True) for head in range(2 * pairs)]
    for head in range(2 * pairs):
        acc[head] = jnp.zeros((rows, LANES), f32)

    def mix(j, _):
        wanted, start = place(j)
        for head in range(2 * pairs):
            e = jnp.exp(s_all[head, j] - peaks[head]).astype(bf16)
            acc[head] += mm(e, vx_all[pl.ds(start, tile), head * LANES : (head + 1) * LANES])
        return 0

    lax.fori_loop(0, count, mix, 0)
    totals = jnp.zeros((rows, LANES), f32)
    for p in range(pairs):
        mixed = []
        for h in range(2):
            head = 2 * p + h
            o = acc[head]
            l = pltpu.roll(o, HD, 1)
            mixed.append(o / l)
            totals = jnp.where(lane == head, peaks[head] + jnp.log(jnp.where(low, l, 1.0)[:, :1]), totals)
        o_ref[:, p * LANES : (p + 1) * LANES] = jnp.where(
            low, mixed[0], pltpu.roll(mixed[1], HD, 1)
        ).astype(bf16)
    l_ref[...] = totals.T[: 2 * pairs, :]
    r2_ref[...] = h1 + mm(o_ref[...], wco_ref[0])


def cross_forward(ranges, x, oa, ob, weights, norms, k2, v2, idq, idr, rows=256, tile=256):
    total, width = x.shape
    keys = k2.shape[0]
    heads = width // HD
    rowspec = lambda w: pl.BlockSpec((rows, w), lambda i, *_: (i, 0))
    sds = jax.ShapeDtypeStruct
    return pl.pallas_call(
        functools.partial(cross_forward_kernel, tile),
        grid_spec=pltpu.PrefetchScalarGridSpec(
            num_scalar_prefetch=1,
            grid=(total // rows,),
            in_specs=[rowspec(width), rowspec(width // 2), rowspec(width // 2)]
            + [part(weights, i, width, 0) for i in range(3)]
            + [whole(norms), whole(k2), whole(v2), pl.BlockSpec((1, rows), lambda i, *_: (0, i)), whole(idr)],
            out_specs=[rowspec(width)] * 4 + [pl.BlockSpec((heads, rows), lambda i, *_: (0, i)), rowspec(width)],
            scratch_shapes=[
                pltpu.VMEM((keys, 2 * width), bf16),
                pltpu.VMEM((heads, keys // tile, rows, tile), f32),
                pltpu.VMEM((heads, rows, LANES), f32),
            ],
        ),
        out_shape=[
            sds((total, width), f32), sds((total, width), bf16), sds((total, width), bf16),
            sds((total, width), bf16), sds((heads, total), f32), sds((total, width), f32),
        ],
        name="cross_forward",
        **params(28, 50),
    )(ranges, x, oa, ob, weights, weights, weights, norms, k2, v2, idq, idr)


def norm_back(incoming, normal, rstd, gain):
    m = incoming * gain
    return rstd * (
        m - jnp.mean(m, axis=-1, keepdims=True) - normal * jnp.mean(m * normal, axis=-1, keepdims=True)
    )


def head_sums(left, right):
    width = left.shape[1]
    prod = left.astype(f32) * right.astype(f32)
    heads = width // HD
    own = lax.broadcasted_iota(jnp.int32, (heads, width), 1) // HD == lax.broadcasted_iota(
        jnp.int32, (heads, width), 0
    )
    return lax.dot_general(
        own.astype(f32), prod, NT, preferred_element_type=f32, precision=lax.Precision.HIGHEST
    )


def column_sums(a):
    return jnp.sum(a, axis=0, keepdims=True)


def spread(keep_ref, send_ref, core, write):
    def one(j, _):
        write(2 * j + core, keep_ref, j)
        write(2 * j + 1 - core, send_ref, j)
        return 0

    lax.fori_loop(0, keep_ref.shape[0], one, 0)


def ffn_kernel(
    core_ref, r2_ref, x_ref, cot_ref, o2_ref, w_ref, wco_ref, norms_ref,
    out_ref, dr3_ref, dr2_ref, do2_ref, delta_ref, keep_ref, send_ref, gn_ref, gin, gout, gco,
):
    step = pl.program_id(0)
    last = pl.num_programs(0) - 1
    width = x_ref.shape[1]
    blocks = w_ref.shape[1] // 2

    @pl.when(step == 0)
    def _():
        gin[...] = jnp.zeros_like(gin)
        gout[...] = jnp.zeros_like(gout)
        gco[...] = jnp.zeros_like(gco)
        gn_ref[...] = jnp.zeros_like(gn_ref)

    win = [w_ref[:, c].reshape(width, width) for c in range(blocks)]
    wout = w_ref[:, blocks:].reshape(blocks * width, width)
    n2, rstd2 = norm_rows(r2_ref[...])
    h2 = n2 * norms_ref[2:3, :] + norms_ref[3:4, :]
    h2b = h2.astype(bf16)
    acts, slopes = [], []
    ff = jnp.zeros(h2.shape, f32)
    for c in range(blocks):
        u = mm(h2b, win[c])
        square = u * u
        t = jnp.tanh(0.7978845608028654 * u * (1.0 + 0.044715 * square))
        half = 0.5 * (1.0 + t)
        act = (u * half).astype(bf16)
        slopes.append(half + 0.5 * u * (1.0 - t * t) * (0.7978845608028654 * (1.0 + 3 * 0.044715 * square)))
        acts.append(act)
        ff += mm(act, wout[c * width : (c + 1) * width, :])
    r3 = h2 + ff + x_ref[...].astype(f32)
    n3, rstd3 = norm_rows(r3)
    gain3 = norms_ref[4:5, :]
    out_ref[...] = (n3 * gain3 + norms_ref[5:6, :]).astype(bf16)
    e = cot_ref[...].astype(f32)
    gn_ref[2:3, :] += column_sums(e * n3)
    gn_ref[3:4, :] += column_sums(e)
    dr3 = norm_back(e, n3, rstd3, gain3)
    dr3_ref[...] = dr3
    dfb = dr3.astype(bf16)
    dh2 = dr3
    for c in range(blocks):
        rows = slice(c * width, (c + 1) * width)
        gout[rows, :] += mm(acts[c], dfb, TN)
        du = (mm(dfb, wout[rows, :], NT) * slopes[c]).astype(bf16)
        gin[:, rows] += mm(h2b, du, TN)
        dh2 += mm(du, win[c], NT)
    gn_ref[0:1, :] += column_sums(dh2 * n2)
    gn_ref[1:2, :] += column_sums(dh2)
    dr2 = norm_back(dh2, n2, rstd2, norms_ref[2:3, :])
    dr2_ref[...] = dr2
    da2 = dr2.astype(bf16)
    o2 = o2_ref[...]
    gco[...] += mm(o2, da2, TN)
    do2 = mm(da2, wco_ref[0], NT).astype(bf16)
    do2_ref[...] = do2
    delta_ref[...] = head_sums(do2, o2)

    @pl.when(step == last)
    def _():
        r = keep_ref.shape[2]

        def write(device, ref, j):
            here = pl.ds(pl.multiple_of(device * r, r), r)
            for c in range(blocks):
                ref[j, c] = gin[here, c * width : (c + 1) * width].astype(bf16)
            ref[j, blocks] = gco[here, :].astype(bf16)
            there = pl.ds(pl.multiple_of(device * blocks * r, blocks * r), blocks * r)
            ref[j, blocks + 1 :] = gout[there, :].astype(bf16).reshape(blocks, r, width)

        spread(keep_ref, send_ref, core_ref[0], write)


def ffn(core, pairs, r2, x, cot, o2, w, weights, index, norms, rows=256):
    total, width = x.shape
    heads = width // HD
    blocks = w.shape[1] // 2
    rowspec = lambda w: pl.BlockSpec((rows, w), lambda i: (i, 0))
    sds = jax.ShapeDtypeStruct
    side = sds((pairs, 2 * blocks + 1, width // (2 * pairs), width), bf16)
    return pl.pallas_call(
        ffn_kernel,
        grid=(total // rows,),
        in_specs=[pl.BlockSpec(memory_space=pltpu.SMEM)] + [rowspec(width)] * 4 + [whole(w), part(weights, index, width, 0), whole(norms)],
        out_specs=[rowspec(width)] * 4
        + [pl.BlockSpec((heads, rows), lambda i: (0, i)), whole(side), whole(side), pl.BlockSpec((4, width), lambda i: (0, 0))],
        out_shape=[
            sds((total, width), bf16), sds((total, width), f32), sds((total, width), f32), sds((total, width), bf16),
            sds((heads, total), f32), side, side, sds((4, width), f32),
        ],
        scratch_shapes=[pltpu.VMEM((width, blocks * width), f32), pltpu.VMEM((blocks * width, width), f32), pltpu.VMEM((width, width), f32)],
        name="ffn",
        **params(32, 50),
    )(core, r2, x, cot, o2, w, weights, norms)


def tile_back(kp, vp, qp, dop, bias, logs, deltas, low_k):
    dks, dvs, dss, kms = [], [], [], []
    for h in range(2):
        km = head_part(kp, h, low_k)
        s = mm(km, qp, NT) + bias
        e = jnp.exp(s - logs[h])
        dp = mm(head_part(vp, h, low_k), dop, NT)
        ds = (e * (dp - deltas[h])).astype(bf16)
        dvs.append(mm(e.astype(bf16), dop))
        dks.append(mm(ds, qp))
        dss.append(ds)
        kms.append(km)
    dq = mm(jnp.concatenate(dss, axis=0), jnp.concatenate(kms, axis=0), TN)
    return jnp.where(low_k, dks[0], dks[1]), jnp.where(low_k, dvs[0], dvs[1]), dq


def cross_backward_kernel(tile, half, ranges_ref, q2_ref, k2_ref, v2_ref, do_ref, l_ref, delta_ref, idr_ref, idk_ref, *rest):
    dq_ref, dk_ref, dv_ref, dk, dv, dq = rest[-6:]
    step = pl.program_id(0)
    rows, width = q2_ref.shape
    keys = k2_ref.shape[0]
    pairs = width // LANES

    @pl.when(step == 0)
    def _():
        dk[...] = jnp.zeros_like(dk)
        dv[...] = jnp.zeros_like(dv)

    dq[...] = jnp.zeros_like(dq)
    scaled = q2_ref[...] * jnp.asarray(HD ** -0.5, bf16)
    do = do_ref[...]
    ids_q = idr_ref[...]
    low_k = lane_below(tile)
    first, count = ranges_ref[0, step], ranges_ref[1, step]

    def one(j, _):
        wanted = (first + j * (tile // LANES)) * LANES
        start = pl.multiple_of(jnp.minimum(wanted, keys - tile), LANES)
        at = pl.ds(start, tile)
        pos = start + lax.broadcasted_iota(jnp.int32, (1, tile), 1)
        ids_k = column_of(jnp.where(pos >= wanted, idk_ref[:, at], -1))[:, :1]
        bias = jnp.where(ids_q == ids_k, 0.0, masked_score).astype(f32)
        for p in range(pairs):
            cols = slice(p * LANES, (p + 1) * LANES)
            heads = [2 * (half * pairs + p) + h for h in range(2)]
            logs = [l_ref[h : h + 1, :] for h in heads]
            deltas = [delta_ref[h : h + 1, :] for h in heads]
            gk, gv, gq = tile_back(
                k2_ref[at, cols], v2_ref[at, cols], scaled[:, cols], do[:, cols], bias, logs, deltas, low_k
            )
            dk[at, cols] += gk
            dv[at, cols] += gv
            dq[:, cols] += gq
        return 0

    lax.fori_loop(0, count, one, 0)
    dq_ref[...] = (dq[...] * HD ** -0.5).astype(bf16)

    @pl.when(step == pl.num_programs(0) - 1)
    def _():
        dk_ref[...] = dk[...].astype(bf16)
        dv_ref[...] = dv[...].astype(bf16)


def cross_backward(ranges, q2, k2, v2, do, l, delta, idr, idk, half, after, rows=256, tile=256):
    total, width = q2.shape
    keys = k2.shape[0]
    heads = width // HD
    columns = width // 2
    rowspec = lambda w: pl.BlockSpec((rows, columns), lambda i, *_: (i, w))
    allrows = lambda w: pl.BlockSpec((keys, columns), lambda i, *_: (0, w))
    cols = lambda h: pl.BlockSpec((h, rows), lambda i, *_: (0, i))
    sds = jax.ShapeDtypeStruct
    return pl.pallas_call(
        functools.partial(cross_backward_kernel, tile, half),
        grid_spec=pltpu.PrefetchScalarGridSpec(
            num_scalar_prefetch=1,
            grid=(total // rows,),
            in_specs=[rowspec(half), allrows(half), allrows(half), rowspec(half), cols(heads), cols(heads), cols(1), whole(idk)]
            + [apart] * len(after),
            out_specs=[rowspec(0), allrows(0), allrows(0)],
            scratch_shapes=[pltpu.VMEM((keys, columns), f32), pltpu.VMEM((keys, columns), f32), pltpu.VMEM((rows, columns), f32)],
        ),
        out_shape=[sds((total, columns), bf16), sds((keys, columns), bf16), sds((keys, columns), bf16)],
        name="cross_backward",
        **params(18, 40),
    )(ranges, q2, k2, v2, do, l, delta, idr, idk, *after)


def memory_weight_kernel(memory_ref, ka_ref, kb_ref, va_ref, vb_ref, *rest):
    grads_ref, total = rest[-2:]
    step = pl.program_id(0)

    @pl.when(step == 0)
    def _():
        total[...] = jnp.zeros_like(total)

    memory = memory_ref[...]
    half = ka_ref.shape[1]
    for i, ref in enumerate((ka_ref, kb_ref, va_ref, vb_ref)):
        total[i // 2, :, (i % 2) * half : (i % 2 + 1) * half] += mm(memory, ref[...], TN)

    @pl.when(step == pl.num_programs(0) - 1)
    def _():
        grads_ref[...] = total[...].astype(bf16)


def memory_weights(memory, ka, kb, va, vb, after, rows=512):
    keys, width = memory.shape
    rowspec = lambda w: pl.BlockSpec((rows, w), lambda i: (i, 0))
    return pl.pallas_call(
        memory_weight_kernel,
        grid=(keys // rows,),
        in_specs=[rowspec(width)] + [rowspec(width // 2)] * 4 + [apart] * len(after),
        out_specs=pl.BlockSpec((2, width, width), lambda i: (0, 0, 0)),
        out_shape=jax.ShapeDtypeStruct((2, width, width), bf16),
        scratch_shapes=[pltpu.VMEM((2, width, width), f32)],
        name="memory_weights",
        **params(6, 24),
    )(memory, ka, kb, va, vb, *after)


def memory_grad_kernel(ka_ref, kb_ref, va_ref, vb_ref, wk_ref, wv_ref, *rest):
    half = ka_ref.shape[1]
    total = mm(ka_ref[...], wk_ref[0, :, :half], NT) + mm(kb_ref[...], wk_ref[0, :, half:], NT)
    total += mm(va_ref[...], wv_ref[0, :, :half], NT) + mm(vb_ref[...], wv_ref[0, :, half:], NT)
    rest[-1][...] = total.astype(bf16)


def memory_grad(ka, kb, va, vb, weights, index, after, rows=512):
    keys, width = ka.shape[0], weights.shape[2]
    rowspec = lambda w: pl.BlockSpec((rows, w), lambda i: (i, 0))
    return pl.pallas_call(
        memory_grad_kernel,
        grid=(keys // rows,),
        in_specs=[rowspec(width // 2)] * 4 + [part(weights, index, width, 0), part(weights, index + 1, width, 0)] + [apart] * len(after),
        out_specs=rowspec(width),
        out_shape=jax.ShapeDtypeStruct((keys, width), bf16),
        name="memory_grad",
        **params(4, 24),
    )(ka, kb, va, vb, weights, weights, *after)


def between_kernel(
    core_ref, gckv_ref, gn23_ref, r1_ref, dr2_ref, dr3_ref, dqa_ref, dqb_ref, h1b_ref, oa_ref, ob_ref, wso_ref, wcq_ref, norms_ref, *rest
):
    dsum_ref, do1_ref, delta_ref, keep_ref, send_ref, gn_ref, total = rest[-7:]
    step = pl.program_id(0)

    @pl.when(step == 0)
    def _():
        total[...] = jnp.zeros_like(total)
        gn_ref[...] = jnp.zeros_like(gn_ref)

    dq2 = jnp.concatenate([dqa_ref[...], dqb_ref[...]], axis=1)
    dh1 = dr2_ref[...] + mm(dq2, wcq_ref[0], NT)
    n1, rstd1 = norm_rows(r1_ref[...])
    gn_ref[0:1, :] += column_sums(dh1 * n1)
    gn_ref[1:2, :] += column_sums(dh1)
    dr1 = norm_back(dh1, n1, rstd1, norms_ref[0:1, :])
    dsum_ref[...] = dr1 + dr3_ref[...]
    da1 = dr1.astype(bf16)
    o1 = jnp.concatenate([oa_ref[...], ob_ref[...]], axis=1)
    do1 = mm(da1, wso_ref[0], NT).astype(bf16)
    do1_ref[...] = do1
    delta_ref[...] = head_sums(do1, o1)
    total[0] += mm(h1b_ref[...], dq2, TN)
    total[1] += mm(o1, da1, TN)

    @pl.when(step == pl.num_programs(0) - 1)
    def _():
        gn_ref[2:6, :] = gn23_ref[...]
        r, width = keep_ref.shape[2:]
        norm_part = jnp.concatenate([gn_ref[...], jnp.zeros((r - 8, width), f32)]).astype(bf16)

        def write(device, ref, j):
            here = pl.ds(pl.multiple_of(device * r, r), r)
            for i in range(2):
                ref[j, i] = gckv_ref[i, here, :]
                ref[j, 2 + i] = total[i, here, :].astype(bf16)
            ref[j, 4] = norm_part

        spread(keep_ref, send_ref, core_ref[0], write)


def between(core, pairs, gckv, gn23, r1, dr2, dr3, dqa, dqb, h1b, oa, ob, weights, norms, after, rows=256):
    total, width = r1.shape
    heads = width // HD
    rowspec = lambda w: pl.BlockSpec((rows, w), lambda i: (i, 0))
    sds = jax.ShapeDtypeStruct
    side = sds((pairs, 5, width // (2 * pairs), width), bf16)
    return pl.pallas_call(
        between_kernel,
        grid=(total // rows,),
        in_specs=[pl.BlockSpec(memory_space=pltpu.SMEM), whole(gckv), whole(gn23)]
        + [rowspec(width)] * 3 + [rowspec(width // 2)] * 2 + [rowspec(width)] + [rowspec(width // 2)] * 2
        + [part(weights, 0, width, 0), part(weights, 1, width, 0), whole(norms)] + [apart] * len(after),
        out_specs=[rowspec(width)] * 2
        + [pl.BlockSpec((heads, rows), lambda i: (0, i)), whole(side), whole(side), pl.BlockSpec((8, width), lambda i: (0, 0))],
        out_shape=[sds((total, width), f32), sds((total, width), bf16), sds((heads, total), f32), side, side, sds((8, width), f32)],
        scratch_shapes=[pltpu.VMEM((2, width, width), f32)],
        name="between",
        **params(7, 32),
    )(core, gckv, gn23, r1, dr2, dr3, dqa, dqb, h1b, oa, ob, weights, weights, norms, *after)


def self_backward_kernel(
    block, half, q_ref, k_ref, v_ref, do_ref, l_ref, delta_ref, idr_ref, x_ref, wq_ref, wk_ref, wv_ref, sofar_ref, *rest
):
    if half:
        core_ref, before_ref = rest[:2]
        gx_ref, keep_ref, send_ref, dq, dk, dv, total_grad = rest[-7:]
    else:
        gx_ref, grads_ref, dq, dk, dv, total_grad = rest[-6:]
    step = pl.program_id(0)
    rows, width = k_ref.shape
    total = q_ref.shape[0]
    window = MOST + block
    pairs = width // LANES

    @pl.when(step == 0)
    def _():
        dq[...] = jnp.zeros_like(dq)
        total_grad[...] = jnp.zeros_like(total_grad)

    base = pl.multiple_of(step * rows, rows)
    low_k = lane_below(block)
    for sub in range(rows // block):
        here = slice(sub * block, (sub + 1) * block)
        start = pl.multiple_of(jnp.minimum(base + sub * block, total - window), LANES)
        at = pl.ds(start, window)
        pos_k = base + sub * block + lax.broadcasted_iota(jnp.int32, (block, window), 0)
        pos_q = start + lax.broadcasted_iota(jnp.int32, (block, window), 1)
        ids_k = column_of(idr_ref[:, pl.ds(base + sub * block, block)])[:, :1]
        bias = jnp.where((ids_k == idr_ref[:, at]) & (pos_k <= pos_q), 0.0, masked_score).astype(f32)
        for p in range(pairs):
            cols = slice(p * LANES, (p + 1) * LANES)
            logs = [l_ref[2 * p + h : 2 * p + h + 1, at] for h in range(2)]
            heads = [2 * (half * pairs + p) + h for h in range(2)]
            deltas = [delta_ref[h : h + 1, at] for h in heads]
            hk, hv, hq = tile_back(
                k_ref[here, cols], v_ref[here, cols], q_ref[at, cols] * jnp.asarray(HD ** -0.5, bf16), do_ref[at, cols],
                bias, logs, deltas, low_k,
            )
            dk[here, cols] = hk.astype(bf16)
            dv[here, cols] = hv.astype(bf16)
            dq[at, cols] += hq
    x = x_ref[...]
    grads = (dq[pl.ds(base, rows), :] * HD ** -0.5).astype(bf16), dk[...], dv[...]
    gx = sofar_ref[...]
    for i, (grad, w_ref) in enumerate(zip(grads, (wq_ref, wk_ref, wv_ref))):
        gx += mm(grad, w_ref[0], NT)
        total_grad[i] += mm(x, grad, TN)
    gx_ref[...] = gx.astype(gx_ref.dtype)

    @pl.when(step == pl.num_programs(0) - 1)
    def _():
        if not half:
            grads_ref[...] = total_grad[...].astype(bf16)
            return
        r = keep_ref.shape[2]

        def write(device, ref, j):
            place = pl.ds(pl.multiple_of(device * r, r), r)
            for i in range(3):
                ref[j, i, :, :width] = before_ref[i, place, :]
                ref[j, i, :, width:] = total_grad[i, place, :].astype(bf16)

        spread(keep_ref, send_ref, core_ref[0], write)


def self_backward(q, k, v, do, l, delta, idr, x, weights, sofar, half, after, core=None, before=None, pairs=1, rows=256, block=256):
    total, width = x.shape
    columns = width // 2
    kind = bf16 if half else f32
    sides = [jax.ShapeDtypeStruct((pairs, 3, width // (2 * pairs), width), bf16)] * 2
    if not half:
        sides = [jax.ShapeDtypeStruct((3, width, columns), bf16)]
    more = [core, before] if half else []
    rowspec = lambda w: pl.BlockSpec((rows, w), lambda i: (i, 0))
    sds = jax.ShapeDtypeStruct
    return pl.pallas_call(
        functools.partial(self_backward_kernel, block, half),
        grid=(total // rows,),
        in_specs=[whole(q), rowspec(columns), rowspec(columns), pl.BlockSpec((total, columns), lambda i: (0, half)), whole(l), whole(delta), whole(idr), rowspec(width)]
        + [part(weights, i, columns, half) for i in range(3)] + [rowspec(width)]
        + ([pl.BlockSpec(memory_space=pltpu.SMEM), whole(before)] if half else []) + [apart] * len(after),
        out_specs=[rowspec(width)] + [whole(side) for side in sides],
        out_shape=[sds((total, width), kind)] + sides,
        scratch_shapes=[pltpu.VMEM((total, columns), f32), pltpu.VMEM((rows, columns), bf16), pltpu.VMEM((rows, columns), bf16), pltpu.VMEM((3, width, columns), f32)],
        name="self_backward",
        **params(10, 40),
    )(q, k, v, do, l, delta, idr, x, weights, weights, weights, sofar, *more, *after)


def add_split_kernel(count, here_ref, *refs):
    places = refs[0].shape[1]
    for m in range(places):
        at = here_ref[0] ^ m
        total = refs[0][:, at].astype(f32)
        for ref in refs[1:count]:
            total += ref[:, at].astype(f32)
        refs[count + m][...] = total.astype(bf16)


def add_split(here, parts, outer, places):
    tail = parts[0].shape[1:]
    parts = [p.reshape((outer, places) + tail) for p in parts]
    out = pl.pallas_call(
        functools.partial(add_split_kernel, len(parts)),
        grid=(outer,),
        in_specs=[pl.BlockSpec(memory_space=pltpu.SMEM)] + [pl.BlockSpec((1, places) + tail, lambda i: (i, 0, 0, 0, 0))] * len(parts),
        out_specs=[pl.BlockSpec((1,) + tail, lambda i: (i, 0, 0, 0))] * places,
        out_shape=[jax.ShapeDtypeStruct((outer,) + tail, bf16)] * places,
        name="add_split",
        **params(3, 24),
    )(here, *parts)
    return list(out)


def segment_ids(lengths, row_count):
    ends = jnp.cumsum(lengths)
    places = jnp.arange(row_count, dtype=jnp.int32)
    return jnp.sum((places[:, None] >= ends[None, :]).astype(jnp.int32), axis=1)


def cross_ranges(seg, mem, total, rows, tile):
    ends = jnp.cumsum(seg)
    starts = jnp.arange(0, total, rows, dtype=jnp.int32)
    head = starts[:, None] >= ends[None, :]
    tail = (starts + rows - 1)[:, None] >= ends[None, :]
    mem = mem[: seg.shape[0]]
    low = jnp.sum(jnp.where(head, mem[None, :], 0), axis=1)
    before = jnp.concatenate([jnp.ones((starts.shape[0], 1), bool), tail[:, :-1]], axis=1)
    high = jnp.sum(jnp.where(before, mem[None, :], 0), axis=1)
    first = low // LANES
    count = (high - first * LANES + tile - 1) // tile
    return jnp.stack([first, count]).astype(jnp.int32)


def mesh_size():
    return lax.axis_size("dp") * lax.axis_size("fsdp")


def position():
    return lax.axis_index("dp") * lax.axis_size("fsdp") + lax.axis_index("fsdp")


def bit_groups():
    count = mesh_size().bit_length() - 1
    groups = [(0, 1)]
    while groups[-1][0] + groups[-1][1] < count:
        low = groups[-1][0] + groups[-1][1]
        groups.append((low, min(2, count - low)))
    return groups


def swap(x, mask):
    return lax.ppermute(x, ("dp", "fsdp"), [(i, i ^ mask) for i in range(mesh_size())])


def place_in(group):
    return (position() >> group[0]) & ((1 << group[1]) - 1)


def tie(x, *after):
    return lax.optimization_barrier((x, *after))[0] if after else x


def gather_step(x, group):
    low, width = group
    here = place_in(group)
    blocks = [x] + [swap(x, m << low) for m in range(1, 1 << width)]
    for j in range(width):
        flip = (here >> j) & 1 == 1
        blocks = [jnp.where(flip, blocks[p ^ (1 << j)], blocks[p]) for p in range(1 << width)]
    return jnp.stack(blocks, axis=x.ndim - 2)


def gathered(x):
    return x.reshape(x.shape[:1] + (-1, x.shape[-1]))


def swap_pieces(parts, group, after=()):
    return [parts[0]] + tie([swap(parts[m], m << group[0]) for m in range(1, len(parts))], *after)


def next_pieces(parts, groups, done):
    group = groups[done]
    outer = 1 << sum(g[1] for g in groups[done + 1 :])
    return add_split(place_in(group).reshape(1).astype(jnp.int32), parts, outer, 1 << group[1])


def norm_parts(norm_params, size):
    parts, left = [], norm_params
    for _ in range(3):
        part = left.astype(bf16)
        parts.append(part)
        left = left - part.astype(f32)
    flat = jnp.concatenate(parts)
    return jnp.pad(flat, (0, size - flat.size))


def resplit(keep, send, devices, core, squares):
    halves = jnp.concatenate([keep, send])
    width = halves.shape[-1]
    first = halves[:, :squares].transpose(1, 0, 2, 3).reshape(squares, devices, -1, width).transpose(1, 0, 2, 3)
    rows = first.shape[2]
    if halves.shape[1] > squares:
        rest = halves[:, squares:].reshape(devices, halves.shape[1] - squares, rows, width)
        first = jnp.concatenate([first, rest], axis=1)
    both = first.reshape(devices // 2, 2, -1, rows, width)
    return [lax.dynamic_index_in_dim(both, core ^ m, 1, keepdims=False) for m in range(2)]


def body(
    inputs, memory, seg_lengths, mem_lengths, self_query, self_key, self_value, self_out,
    cross_query, cross_key, cross_value, cross_out, ffn_in, ffn_out, norm_params, cotangent,
):
    total, width = inputs.shape
    keys = memory.shape[0]
    devices = mesh_size()
    groups = bit_groups()
    down = groups[::-1]
    tile = 256
    shard = norm_params.shape[0]
    size = self_query.shape[0]
    own_rows = size // width
    blocks = ffn_in.shape[0] // size
    whole_tiles = own_rows % 16 == 0
    core = place_in(groups[0]).reshape(1).astype(jnp.int32)

    first = jnp.concatenate([self_query, self_key, self_value]).reshape(3, own_rows, width)
    others = jnp.concatenate(
        [self_out, cross_query, cross_out, cross_key, cross_value, norm_parts(norm_params, size), ffn_out, ffn_in]
    ).reshape(-1, own_rows, width)
    second = others[:6]
    fi = others[6 + blocks :].reshape(own_rows, blocks, width).transpose(1, 0, 2)
    ffn_own = jnp.concatenate([fi, others[6 : 6 + blocks]]).reshape(-1, width)
    first = gather_step(first, down[0])
    second, ffn_own = tie((second, ffn_own), first)
    for g in down[1:]:
        second = gather_step(second, down[down.index(g) - 1])
        first = gather_step(first, g)
        if g == down[-2]:
            ffn_own = tie(ffn_own, first)
        second = tie(second, first)
    first = gathered(first)
    ffn_all = lax.all_gather(ffn_own, ("dp", "fsdp"), axis=0, tiled=True).reshape(devices, 2 * blocks, own_rows, width)
    if not whole_tiles:
        fi = ffn_all[:, :blocks].transpose(1, 0, 2, 3).reshape(1, blocks, width, width)
        ffn_all = jnp.concatenate([fi, ffn_all[:, blocks:].reshape(1, blocks, width, width)], axis=1)
    pairs = devices // 2 if whole_tiles else 1
    part_of = core if whole_tiles else jnp.zeros_like(core)

    qid, mid = segment_ids(seg_lengths[0], total)[None, :], segment_ids(mem_lengths[0], keys)[None, :]
    ranges = cross_ranges(seg_lengths[0], mem_lengths[0], total, 256, tile)

    qa, ka, va, oa, la = self_forward(inputs, first, qid, 0, [])
    qb, kb, vb, ob, lb = self_forward(inputs, first, qid, 1, [second, la])
    second = gathered(gather_step(second, down[-1]))
    norm_all = second[5].reshape(devices, -1)[:, : 3 * shard].astype(f32).reshape(devices, 3, shard)
    norms = jnp.sum(norm_all, axis=1).reshape(6, width)
    k2, v2 = project_memory(memory, second, 3)
    r1, h1b, q2, o2, l2, r2 = cross_forward(ranges, inputs, oa, ob, second, norms, k2, v2, qid, mid, tile=tile)
    out, dr3, dr2, do2, delta2, keep, send, gn23 = ffn(part_of, pairs, r2, inputs, cotangent, o2, ffn_all, second, 2, norms)

    one = [keep, send] if whole_tiles else resplit(keep, send, devices, core[0], blocks + 1)
    dq2a, dk2a, dv2a = cross_backward(ranges, q2, k2, v2, do2, l2, delta2, qid, mid, 0, [one[1]], tile=tile)
    one = next_pieces(swap_pieces(one, groups[0], [dq2a]), groups, 1)
    dq2b, dk2b, dv2b = cross_backward(ranges, q2, k2, v2, do2, l2, delta2, qid, mid, 1, one[1:], tile=tile)
    gckv = memory_weights(memory, dk2a, dk2b, dv2a, dv2b, [])
    dsum, do1, delta1, keep, send, gn = between(
        part_of, pairs, gckv, gn23, r1, dr2, dr3, dq2a, dq2b, h1b, oa, ob, second, norms, []
    )
    two = [keep, send]
    if not whole_tiles:
        two = resplit(keep, send, devices, core[0], 5)
        own_norms = jnp.pad(gn[:6].astype(bf16).reshape(devices, -1), ((0, 0), (0, size - shard)))
        own_norms = own_norms.reshape(devices // 2, 2, own_rows, width)
        two = [two[m].at[:, 4].set(lax.dynamic_index_in_dim(own_norms, core[0] ^ m, 1, keepdims=False)) for m in range(2)]
    one = next_pieces(swap_pieces(one, groups[1], [do1]), groups, 2)
    gxa, gsa = self_backward(qa, ka, va, do1, la, delta1, qid, inputs, first, dsum, 0, one[1:] + [two[1]])
    two = next_pieces(swap_pieces(two, groups[0], [gsa]), groups, 1)
    gx, keep, send = self_backward(
        qb, kb, vb, do1, lb, delta1, qid, inputs, first, gxa, 1, two[1:], core=part_of, before=gsa, pairs=pairs
    )
    three = [keep, send] if whole_tiles else resplit(keep, send, devices, core[0], 3)
    three = next_pieces(swap_pieces(three, groups[0]), groups, 1)
    two = next_pieces(swap_pieces(two, groups[1], [gx]), groups, 2)
    gm = memory_grad(dk2a, dk2b, dv2a, dv2b, second, 3, three[1:])
    for i in range(2, len(groups)):
        three = next_pieces(swap_pieces(three, groups[i - 1]), groups, i)
        if i > 2:
            one = next_pieces(swap_pieces(one, groups[i - 1]), groups, i)
            two = next_pieces(swap_pieces(two, groups[i - 1]), groups, i)
    one, two, three = (
        sum(p.astype(f32) for p in swap_pieces(chain, groups[-1])).reshape(-1, own_rows, width) for chain in (one, two, three)
    )

    def flat(g):
        return g.reshape(-1)

    gn = flat(two[4])[:shard]
    if whole_tiles:
        gn = lax.dynamic_slice_in_dim(flat(two[4][:6]), position() * shard, shard)
    return (
        out, gx, gm, flat(three[0]), flat(three[1]), flat(three[2]), flat(two[3]),
        flat(two[2]), flat(two[0]), flat(two[1]), flat(one[blocks]), flat(one[:blocks].transpose(1, 0, 2)), flat(one[blocks + 1 :]), gn,
    )


def solution(mesh):
    rows, flat = P(("dp", "fsdp"), None), P(("dp", "fsdp"))
    return jax.shard_map(
        body,
        mesh=mesh,
        in_specs=(rows,) * 4 + (flat,) * 11 + (rows,),
        out_specs=(rows,) * 3 + (flat,) * 11,
        check_vma=False,
    )
```

time: 384 us -> 302 us (0.79); the launches traced: 377 us -> 301 us
  waiting for transfers between devices: 102 us -> 43.5 us
  starting transfers between devices: 73.2 us -> 46 us
  matrix products: 15.6 us -> 0 us
  Pallas kernels: 137 us -> 151 us
  between operations: 2.32 us -> 14.9 us
  other arithmetic: 15.1 us -> 5.43 us
  local copies, waits for them, and re-layouts: 31 us -> 40.3 us
    ppermute x60 -> x35, waiting for transfers between devices: 102 us -> 43.5 us  [swap(): lax.ppermute(x, ('dp', 'fsdp'), [(i, i ^ mask) for i in range(mesh_size())])]
    ppermute x60 -> x35, starting transfers between devices: 73.2 us -> 45.9 us  [swap(): lax.ppermute(x, ('dp', 'fsdp'), [(i, i ^ mask) for i in range(mesh_size())])]
    dot_general x6 -> x0, matrix products: 15.6 us -> none  [mm(): return lax.dot_general(left, right, dims, preferred_element_type=f32)]
    unnamed x99 -> x137, local copies, waits for them, and re-layouts: 13.9 us -> 29.1 us
    pallas_call x5 -> x17, Pallas kernels: 113 us -> 126 us  [the longest x1 34.1 us: ffn(): pl.pallas_call(ffn_kernel, grid=(total // rows,), in_specs=[pl.BlockSpec(...]
    concatenate x0 -> x12, local copies, waits for them, and re-layouts: none -> 6.65 us  [the longest x7 3.73 us: body(): jnp.concatenate([self_out, cross_query, cross_out, cross_key, cross_value...]
    another operation x15 -> x3, local copies, waits for them, and re-layouts: 7.6 us -> 1.8 us  [the longest x6 3.71 us: body(): jnp.stack([rows_of(w, width) for w in (self_out, cross_query, cross_key,...]
    squeeze x32 -> x0, local copies, waits for them, and re-layouts: 5.38 us -> none  [scatter_sum(): lax.dynamic_index_in_dim(x, 1 - mine, place, keepdims=False)]
  transfers between devices with their start and end apart: 60 -> 36, of which waited for: 36 -> 14; matrix products, arithmetic and copies ran while one was open for 10% -> 6% of each run, Pallas kernels for 5% -> 38%
where the time goes in v2:
time: 302 us; the launch traced here: 301 us
  Pallas kernels  151 us (50%)
  starting transfers between devices  46 us (15%)
  waiting for transfers between devices  43.5 us (14%)
  local copies, waits for them, and re-layouts  40.3 us (13%)
  between operations  14.9 us (5%)
  other arithmetic  5.43 us (2%)
    ppermute x35, starting transfers between devices, swap(): lax.ppermute(x, ('dp', 'fsdp'), [(i, i ^ mask) for i in range(mesh_size())])  45.9 us
    ppermute x35, waiting for transfers between devices, swap(): lax.ppermute(x, ('dp', 'fsdp'), [(i, i ^ mask) for i in range(mesh_size())])  43.5 us
    pallas_call x1, Pallas kernels, ffn(): pl.pallas_call(ffn_kernel, grid=(total // rows,), in_specs=[pl.BlockSpec(...  34.1 us
    pallas_call x2, Pallas kernels, cross_backward(): pl.pallas_call(functools.partial(cross_backward_kernel, tile, half), grid...  32.7 us
    unnamed x137, local copies, waits for them, and re-layouts  29.1 us
    pallas_call x1, Pallas kernels, cross_forward(): pl.pallas_call(functools.partial(cross_forward_kernel, tile), grid_spec=p...  24.7 us
    pallas_call x2, Pallas kernels, self_backward(): pl.pallas_call(functools.partial(self_backward_kernel, block, half), grid...  20.5 us
    pallas_call x2, Pallas kernels, self_forward(): pl.pallas_call(functools.partial(self_forward_kernel, block), grid=(total...  18 us
  transfers between devices with their start and end apart: 36, of which 14 were waited for; matrix products, arithmetic and copies ran while one was open for 6% of the time, Pallas kernels for 38%

profile of v2, /device:TPU:0, one launch (start us, length us, event | category | flops | bytes accessed | tf_op | source)
XLA Modules:
  0.0 301.4 jit_solution(8629014500410020281)
XLA Ops:
  9.5 3.1 %collective-permute-start.2 = (bf16[3,16,512]{2,1,0:T(8,128)(2,1)S(1)}, bf16[3,16,512]{2,1,0:T(8,128)(2,1)S(1)}, u32[]{:S(2)}, u32[]{:S(2)}) collective-permute-start(bf16[3,16,512]{2,1,0:T(8,128)(2,1)S(1)} %constant_dynamic-update-slice_fusion), channel_id=1, source_target_pairs={{0,8},{1,9},{2,10},{3,11},{4,12},{5,13},{6,14},{7,15},{8,0},{9,1},... | collective-permute-start | bytes 147464 | tf_op jit(solution)/shard_map/ppermute | solution.py:768
  12.6 2.6 collective-permute-start.1
  24.3 1.8 collective-permute-start.5
  26.0 1.5 collective-permute-start.4
  27.8 4.3 %collective-permute-done.5 = bf16[3,4,16,512]{3,2,1,0:T(8,128)(2,1)S(1)} collective-permute-done((bf16[3,4,16,512]{3,2,1,0:T(8,128)(2,1)S(1)}, bf16[3,4,16,512]{3,2,1,0:T(8,128)(2,1)S(1)}, u32[]{:S(2)}, u32[]{:S(2)}) %collective-permute-start.5) | collective-permute-done | bytes 196640 | tf_op jit(solution)/shard_map/ppermute | solution.py:768
  32.2 3.7 %collective-permute-done.4 = bf16[3,4,16,512]{3,2,1,0:T(8,128)(2,1)S(1)} collective-permute-done((bf16[3,4,16,512]{3,2,1,0:T(8,128)(2,1)S(1)}, bf16[3,4,16,512]{3,2,1,0:T(8,128)(2,1)S(1)}, u32[]{:S(2)}, u32[]{:S(2)}) %collective-permute-start.4) | collective-permute-done | bytes 196640 | tf_op jit(solution)/shard_map/ppermute | solution.py:768
  37.9 3.5 %collective-permute-start.8 = (bf16[6,16,512]{2,1,0:T(8,128)(2,1)S(1)}, bf16[6,16,512]{2,1,0:T(8,128)(2,1)S(1)}, u32[]{:S(2)}, u32[]{:S(2)}) collective-permute-start(bf16[6,16,512]{2,1,0:T(8,128)(2,1)S(1)} %constant_dynamic-update-slice_fusion.3), channel_id=1, source_target_pairs={{0,16},{1,17},{2,18},{3,19},{4,20},{5,21},{6,22},{7,23},{8,24},{9,... | collective-permute-start | bytes 294920 | tf_op jit(solution)/shard_map/ppermute | solution.py:768
  41.9 4.3 %collective-permute-done.8 = bf16[6,16,512]{2,1,0:T(8,128)(2,1)S(1)} collective-permute-done((bf16[6,16,512]{2,1,0:T(8,128)(2,1)S(1)}, bf16[6,16,512]{2,1,0:T(8,128)(2,1)S(1)}, u32[]{:S(2)}, u32[]{:S(2)}) %collective-permute-start.8) | collective-permute-done | bytes 98336 | tf_op jit(solution)/shard_map/ppermute | solution.py:768
  46.2 1.7 collective-permute-done.7
  50.0 1.5 collective-permute-start.10
  52.0 8.2 %collective-permute-done.12 = bf16[6,4,16,512]{3,2,1,0:T(8,128)(2,1)S(1)} collective-permute-done((bf16[6,4,16,512]{3,2,1,0:T(8,128)(2,1)S(1)}, bf16[6,4,16,512]{3,2,1,0:T(8,128)(2,1)S(1)}, u32[]{:S(2)}, u32[]{:S(2)}) %collective-permute-start.12) | collective-permute-done | bytes 393248 | tf_op jit(solution)/shard_map/ppermute | solution.py:768
  60.1 8.2 %collective-permute-done.11 = bf16[6,4,16,512]{3,2,1,0:T(8,128)(2,1)} collective-permute-done((bf16[6,4,16,512]{3,2,1,0:T(8,128)(2,1)S(1)}, bf16[6,4,16,512]{3,2,1,0:T(8,128)(2,1)}, u32[]{:S(2)}, u32[]{:S(2)}) %collective-permute-start.11) | collective-permute-done | bytes 393248 | tf_op jit(solution)/shard_map/ppermute | solution.py:768
  70.2 1.3 copy-done.8
  71.5 9.0 %self_forward.2 = (bf16[1024,256]{1,0:T(8,128)(2,1)S(1)}, bf16[1024,256]{1,0:T(8,128)(2,1)S(1)}, bf16[1024,256]{1,0:T(8,128)(2,1)S(1)}, bf16[1024,256]{1,0:T(8,128)(2,1)S(1)}, f32[4,1024]{1,0:T(4,128)S(1)}) custom-call(bf16[1024,512]{1,0:T(8,128)(2,1)S(1)} %copy-done.8, bf16[3,512,512]{2,1,0:T(8,128)(2,1)S(1)} %bitcast.162, ...), custom_call_target="tpu_custom_call" | custom-call | flops 8000000000 | bytes 1048576 | tf_op jit(solution)/shard_map/self_forward/pallas_call | solution.py:132
  82.9 9.0 %self_forward.3 = (bf16[1024,256]{1,0:T(8,128)(2,1)S(1)}, bf16[1024,256]{1,0:T(8,128)(2,1)S(1)}, bf16[1024,256]{1,0:T(8,128)(2,1)S(1)}, bf16[1024,256]{1,0:T(8,128)(2,1)S(1)}, f32[4,1024]{1,0:T(4,128)S(1)}) custom-call(bf16[1024,512]{1,0:T(8,128)(2,1)S(1)} %copy-done.8, bf16[3,512,512]{2,1,0:T(8,128)(2,1)S(1)} %bitcast.165, ...), custom_call_target="tpu_custom_call" | custom-call | flops 8000000000 | bytes 1048576 | tf_op jit(solution)/shard_map/self_forward/pallas_call | solution.py:132
  96.2 1.7 copy-done.5
  97.9 2.9 project_memory.1
  100.7 1.3 copy-done.25
  102.1 1.4 copy-done.27
  103.4 24.7 %cross_forward.1 = (f32[1024,512]{1,0:T(8,128)}, bf16[1024,512]{1,0:T(8,128)(2,1)S(1)}, bf16[1024,512]{1,0:T(8,128)(2,1)S(1)}, bf16[1024,512]{1,0:T(8,128)(2,1)}...) custom-call(s32[2,4]{1,0:T(2,128)S(1)} %pad_add_fusion.ranges_ref, bf16[1024,512]{1,0:T(8,128)(2,1)} %x_ref.11, ...), custom_call_target="tpu_custom_call" | custom-call | flops 28000000000 | bytes 1048576 | tf_op jit(solution)/shard_map/cross_forward/pallas_call | solution.py:256
  129.2 34.1 %ffn.1 = (bf16[1024,512]{1,0:T(8,128)(2,1)}, f32[1024,512]{1,0:T(8,128)}, f32[1024,512]{1,0:T(8,128)}, bf16[1024,512]{1,0:T(8,128)(2,1)S(1)}, f32[8,1024]{1,0:T(...) custom-call(s32[1]{0:T(128)} %bitcast.core_ref.rest_0_, ...), custom_call_target="tpu_custom_call" | custom-call | flops 32000000000 | bytes 1048576 | tf_op jit(solution)/shard_map/ffn/pallas_call | solution.py:394
  164.4 1.7 copy-done.4
  166.1 1.6 copy-done.26
  167.7 1.6 copy-done.28
  171.7 16.3 %cross_backward.2 = (bf16[1024,256]{1,0:T(8,128)(2,1)S(1)}, bf16[2048,256]{1,0:T(8,128)(2,1)S(1)}, bf16[2048,256]{1,0:T(8,128)(2,1)S(1)}) custom-call(s32[2,4]{1,0:T(2,128)S(1)} %pad_add_fusion.ranges_ref, bf16[1024,512]{1,0:T(8,128)(2,1)S(1)} %copy-done.54, bf16[2048,512]{1,0:T(8,128)(2,1)S(1)} %copy-done.26, bf16[2048,512]{1,0:T(8,128)(2,1)S(1)} %copy-done.28, ...), custom_call_target="tpu_custom_call" | custom-call | flops 17999998976 | bytes 1048576 | tf_op jit(solution)/shard_map/cross_backward/pallas_call | solution.py:483
  188.8 2.0 collective-permute-start.15
  191.3 16.3 %cross_backward.3 = (bf16[1024,256]{1,0:T(8,128)(2,1)S(1)}, bf16[2048,256]{1,0:T(8,128)(2,1)S(1)}, bf16[2048,256]{1,0:T(8,128)(2,1)S(1)}) custom-call(s32[2,4]{1,0:T(2,128)S(1)} %pad_add_fusion.ranges_ref, bf16[1024,512]{1,0:T(8,128)(2,1)S(1)} %copy-done.54, bf16[2048,512]{1,0:T(8,128)(2,1)S(1)} %copy-done.26, bf16[2048,512]{1,0:T(8,128)(2,1)S(1)} %copy-done.28, ...), custom_call_target="tpu_custom_call" | custom-call | flops 17999998976 | bytes 1048576 | tf_op jit(solution)/shard_map/cross_backward/pallas_call | solution.py:483
  208.9 3.3 %memory_weights.1.gckv_ref = bf16[2,512,512]{2,1,0:T(8,128)(2,1)S(1)} custom-call(bf16[2048,512]{1,0:T(8,128)(2,1)S(1)} %copy-done.6, bf16[2048,256]{1,0:T(8,128)(2,1)S(1)} %get-tuple-element.114.ka_ref, bf16[2048,256]{1,0:T(8,128)(2,1)S(1)} %get-tuple-element.121.kb_ref, bf16[2048,256]{1,0:T(8,128)(2,1)S(1)} %get-tuple-element.122.va_ref, ...), custom_call_target="tpu_custom_call" | custom-call | flops 6000000000 | bytes 1048576 | tf_op jit(solution)/shard_map/memory_weights/pallas_call | solution.py:520
  213.2 7.6 %between.1 = (f32[1024,512]{1,0:T(8,128)S(1)}, bf16[1024,512]{1,0:T(8,128)(2,1)S(1)}, f32[8,1024]{1,0:T(8,128)S(1)}, bf16[16,5,16,512]{3,2,1,0:T(8,128)(2,1)S(1)...) custom-call(s32[1]{0:T(128)} %bitcast.core_ref.rest_0_, bf16[2,512,512]{2,1,0:T(8,128)(2,1)S(1)} %memory_weights.1.gckv_ref, ...), custom_call_target="tpu_custom_call" | custom-call | flops 7000000000 | bytes 1048576 | tf_op jit(solution)/shard_map/between/pallas_call | solution.py:601
  221.7 2.8 collective-permute-done.17
  224.9 2.6 collective-permute-start.33
  227.5 1.8 collective-permute-start.34
  229.3 9.7 %self_backward.2 = (f32[1024,512]{1,0:T(8,128)S(1)}, bf16[3,512,256]{2,1,0:T(8,128)(2,1)S(1)}) custom-call(bf16[1024,256]{1,0:T(8,128)(2,1)S(1)} %copy-done.48, bf16[1024,256]{1,0:T(8,128)(2,1)S(1)} %copy-done.50, bf16[1024,256]{1,0:T(8,128)(2,1)S(1)} %copy-done.52, bf16[1024,512]{1,0:T(8,128)(2,1)S(1)} %get-tuple-element.130.do_ref, ...), custom_call_target="tpu_custom_call" | custom-call | flops 10000000000 | bytes 1048576 | tf_op jit(solution)/shard_map/self_backward/pallas_call | solution.py:691
  240.0 2.2 collective-permute-start.27
  243.2 10.8 %self_backward.3 = (bf16[1024,512]{1,0:T(8,128)(2,1)}, bf16[16,3,16,512]{3,2,1,0:T(8,128)(2,1)S(1)}, bf16[16,3,16,512]{3,2,1,0:T(8,128)(2,1)}) custom-call(bf16[1024,256]{1,0:T(8,128)(2,1)S(1)} %copy-done.42, bf16[1024,256]{1,0:T(8,128)(2,1)S(1)} %copy-done.44, bf16[1024,256]{1,0:T(8,128)(2,1)S(1)} %copy-done.46, bf16[1024,512]{1,0:T(8,128)(2,1)S(1)} %copy-done.30, ...), custom_call_target="tpu_custom_call" | custom-call | flops 10000000000 | bytes 1048576 | tf_op jit(solution)/shard_map/self_backward/pallas_call | solution.py:691
  254.0 2.2 collective-permute-done.27
  256.4 3.4 %collective-permute-start.29 = (bf16[1,5,16,512]{3,2,1,0:T(8,128)(2,1)S(1)}, bf16[1,5,16,512]{3,2,1,0:T(8,128)(2,1)S(1)}, u32[]{:S(2)}, u32[]{:S(2)}) collective-permute-start(bf16[1,5,16,512]{3,2,1,0:T(8,128)(2,1)S(1)} %get-tuple-element.168), channel_id=1, source_target_pairs={{0,8},{1,9},{2,10},{3,11},{4,12},{5,13},{6,14},{7,15},{8,0},{9,1},... | collective-permute-start | bytes 245768 | tf_op jit(solution)/shard_map/ppermute | solution.py:768
  259.8 2.0 collective-permute-start.30
  261.8 1.4 collective-permute-start.31
  265.3 3.5 %collective-permute-done.30 = bf16[1,5,16,512]{3,2,1,0:T(8,128)(2,1)S(1)} collective-permute-done((bf16[1,5,16,512]{3,2,1,0:T(8,128)(2,1)S(1)}, bf16[1,5,16,512]{3,2,1,0:T(8,128)(2,1)S(1)}, u32[]{:S(2)}, u32[]{:S(2)}) %collective-permute-start.30) | collective-permute-done | bytes 81952 | tf_op jit(solution)/shard_map/ppermute | solution.py:768
  270.1 2.1 add_split.9
  272.2 1.7 collective-permute-start.20
  274.0 1.7 collective-permute-start.22
  279.1 3.0 %collective-permute-done.21 = bf16[4,3,16,512]{3,2,1,0:T(8,128)(2,1)S(1)} collective-permute-done((bf16[4,3,16,512]{3,2,1,0:T(8,128)(2,1)S(1)}, bf16[4,3,16,512]{3,2,1,0:T(8,128)(2,1)S(1)}, u32[]{:S(2)}, u32[]{:S(2)}) %collective-permute-start.21) | collective-permute-done | bytes 196640 | tf_op jit(solution)/shard_map/ppermute | solution.py:768
  282.3 2.9 collective-permute-start.23
  285.1 1.5 collective-permute-start.24
  286.6 1.4 collective-permute-start.25
  288.0 3.8 %memory_grad.1 = bf16[2048,512]{1,0:T(8,128)(2,1)} custom-call(bf16[2048,256]{1,0:T(8,128)(2,1)S(1)} %copy-done.15, bf16[2048,256]{1,0:T(8,128)(2,1)S(1)} %copy-done.19, bf16[2048,256]{1,0:T(8,128)(2,1)S(1)} %copy-done.17, bf16[2048,256]{1,0:T(8,128)(2,1)S(1)} %copy-done.21, bf16[6,512,512]{2,1,0:T(8,128)(2,1)S(1)} %bitcast.160, ...), custom_call_target="tpu_custom_call" | custom-call | flops 4000000000 | bytes 1048576 | tf_op jit(solution)/shard_map/memory_grad/pallas_call | solution.py:542
  (241 shorter events, 45.8 us)
Async XLA Ops:
  7.2 122.0 %all-gather.2.cloned.1.call-start = ((), (), s32[]{:S(2)}) async-start(), calls=%async_computation | async-start | bytes 4325376 | tf_op jit(solution)/shard_map/all_gather | solution.py:858
  9.5 14.7 %collective-permute-start.2 = (bf16[3,16,512]{2,1,0:T(8,128)(2,1)S(1)}, bf16[3,16,512]{2,1,0:T(8,128)(2,1)S(1)}, u32[]{:S(2)}, u32[]{:S(2)}) collective-permute-start(bf16[3,16,512]{2,1,0:T(8,128)(2,1)S(1)} %constant_dynamic-update-slice_fusion), channel_id=1, source_target_pairs={{0,8},{1,9},{2,10},{3,11},{4,12},{5,13},{6,14},{7,15},{8,0},{9,1},... | collective-permute-start | bytes 147464 | tf_op jit(solution)/shard_map/ppermute | solution.py:768
  12.6 11.6 %collective-permute-start.1 = (bf16[3,16,512]{2,1,0:T(8,128)(2,1)S(1)}, bf16[3,16,512]{2,1,0:T(8,128)(2,1)S(1)}, u32[]{:S(2)}, u32[]{:S(2)}) collective-permute-start(bf16[3,16,512]{2,1,0:T(8,128)(2,1)S(1)} %constant_dynamic-update-slice_fusion), channel_id=1, source_target_pairs={{0,16},{1,17},{2,18},{3,19},{4,20},{5,21},{6,22},{7,23},{8,24},{9,... | collective-permute-start | bytes 147464 | tf_op jit(solution)/shard_map/ppermute | solution.py:768
  15.2 9.0 %collective-permute-start = (bf16[3,16,512]{2,1,0:T(8,128)(2,1)S(1)}, bf16[3,16,512]{2,1,0:T(8,128)(2,1)S(1)}, u32[]{:S(2)}, u32[]{:S(2)}) collective-permute-start(bf16[3,16,512]{2,1,0:T(8,128)(2,1)S(1)} %constant_dynamic-update-slice_fusion), channel_id=1, source_target_pairs={{0,24},{1,25},{2,26},{3,27},{4,28},{5,29},{6,30},{7,31},{8,16},{9,... | collective-permute-start | bytes 147464 | tf_op jit(solution)/shard_map/ppermute | solution.py:768
  24.3 7.9 %collective-permute-start.5 = (bf16[3,4,16,512]{3,2,1,0:T(8,128)(2,1)S(1)}, bf16[3,4,16,512]{3,2,1,0:T(8,128)(2,1)S(1)}, u32[]{:S(2)}, u32[]{:S(2)}) collective-permute-start(bf16[3,4,16,512]{3,2,1,0:T(8,128)(2,1)S(1)} %pad_maximum_fusion.5), channel_id=1, source_target_pairs={{0,2},{1,3},{2,0},{3,1},{4,6},{5,7},{6,4},{7,5},{8,10},{9,11},{10,... | collective-permute-start | bytes 589832 | tf_op jit(solution)/shard_map/ppermute | solution.py:768
  26.0 9.9 %collective-permute-start.4 = (bf16[3,4,16,512]{3,2,1,0:T(8,128)(2,1)S(1)}, bf16[3,4,16,512]{3,2,1,0:T(8,128)(2,1)S(1)}, u32[]{:S(2)}, u32[]{:S(2)}) collective-permute-start(bf16[3,4,16,512]{3,2,1,0:T(8,128)(2,1)S(1)} %pad_maximum_fusion.5), channel_id=1, source_target_pairs={{0,4},{1,5},{2,6},{3,7},{4,0},{5,1},{6,2},{7,3},{8,12},{9,13},{10,... | collective-permute-start | bytes 589832 | tf_op jit(solution)/shard_map/ppermute | solution.py:768
  27.6 8.3 %collective-permute-start.3 = (bf16[3,4,16,512]{3,2,1,0:T(8,128)(2,1)S(1)}, bf16[3,4,16,512]{3,2,1,0:T(8,128)(2,1)S(1)}, u32[]{:S(2)}, u32[]{:S(2)}) collective-permute-start(bf16[3,4,16,512]{3,2,1,0:T(8,128)(2,1)S(1)} %pad_maximum_fusion.5), channel_id=1, source_target_pairs={{0,6},{1,7},{2,4},{3,5},{4,2},{5,3},{6,0},{7,1},{8,14},{9,15},{10,... | collective-permute-start | bytes 589832 | tf_op jit(solution)/shard_map/ppermute | solution.py:768
  37.3 4.6 %collective-permute-start.9 = (bf16[6,16,512]{2,1,0:T(8,128)(2,1)S(1)}, bf16[6,16,512]{2,1,0:T(8,128)(2,1)S(1)}, u32[]{:S(2)}, u32[]{:S(2)}) collective-permute-start(bf16[6,16,512]{2,1,0:T(8,128)(2,1)S(1)} %constant_dynamic-update-slice_fusion.3), channel_id=1, source_target_pairs={{0,8},{1,9},{2,10},{3,11},{4,12},{5,13},{6,14},{7,15},{8,0},{9,1},... | collective-permute-start | bytes 294920 | tf_op jit(solution)/shard_map/ppermute | solution.py:768
  37.9 8.3 %collective-permute-start.8 = (bf16[6,16,512]{2,1,0:T(8,128)(2,1)S(1)}, bf16[6,16,512]{2,1,0:T(8,128)(2,1)S(1)}, u32[]{:S(2)}, u32[]{:S(2)}) collective-permute-start(bf16[6,16,512]{2,1,0:T(8,128)(2,1)S(1)} %constant_dynamic-update-slice_fusion.3), channel_id=1, source_target_pairs={{0,16},{1,17},{2,18},{3,19},{4,20},{5,21},{6,22},{7,23},{8,24},{9,... | collective-permute-start | bytes 294920 | tf_op jit(solution)/shard_map/ppermute | solution.py:768
  41.4 6.5 %collective-permute-start.7 = (bf16[6,16,512]{2,1,0:T(8,128)(2,1)S(1)}, bf16[6,16,512]{2,1,0:T(8,128)(2,1)S(1)}, u32[]{:S(2)}, u32[]{:S(2)}) collective-permute-start(bf16[6,16,512]{2,1,0:T(8,128)(2,1)S(1)} %constant_dynamic-update-slice_fusion.3), channel_id=1, source_target_pairs={{0,24},{1,25},{2,26},{3,27},{4,28},{5,29},{6,30},{7,31},{8,16},{9,... | collective-permute-start | bytes 294920 | tf_op jit(solution)/shard_map/ppermute | solution.py:768
  48.0 12.1 %collective-permute-start.12 = (bf16[6,4,16,512]{3,2,1,0:T(8,128)(2,1)S(1)}, bf16[6,4,16,512]{3,2,1,0:T(8,128)(2,1)S(1)}, u32[]{:S(2)}, u32[]{:S(2)}) collective-permute-start(bf16[6,4,16,512]{3,2,1,0:T(8,128)(2,1)S(1)} %pad_maximum_fusion.4), channel_id=1, source_target_pairs={{0,2},{1,3},{2,0},{3,1},{4,6},{5,7},{6,4},{7,5},{8,10},{9,11},{10,... | collective-permute-start | bytes 1179656 | tf_op jit(solution)/shard_map/ppermute | solution.py:768
  49.2 19.1 %collective-permute-start.11 = (bf16[6,4,16,512]{3,2,1,0:T(8,128)(2,1)S(1)}, bf16[6,4,16,512]{3,2,1,0:T(8,128)(2,1)}, u32[]{:S(2)}, u32[]{:S(2)}) collective-permute-start(bf16[6,4,16,512]{3,2,1,0:T(8,128)(2,1)S(1)} %pad_maximum_fusion.4), channel_id=1, source_target_pairs={{0,4},{1,5},{2,6},{3,7},{4,0},{5,1},{6,2},{7,3},{8,12},{9,13},{10,... | collective-permute-start | bytes 1179656 | tf_op jit(solution)/shard_map/ppermute | solution.py:768
  50.0 18.3 %collective-permute-start.10 = (bf16[6,4,16,512]{3,2,1,0:T(8,128)(2,1)S(1)}, bf16[6,4,16,512]{3,2,1,0:T(8,128)(2,1)}, u32[]{:S(2)}, u32[]{:S(2)}) collective-permute-start(bf16[6,4,16,512]{3,2,1,0:T(8,128)(2,1)S(1)} %pad_maximum_fusion.4), channel_id=1, source_target_pairs={{0,6},{1,7},{2,4},{3,5},{4,2},{5,3},{6,0},{7,1},{8,14},{9,15},{10,... | collective-permute-start | bytes 1179656 | tf_op jit(solution)/shard_map/ppermute | solution.py:768
  51.8 18.0 %collective-permute-start.6 = (bf16[3,4,4,16,512]{4,3,2,1,0:T(8,128)(2,1)}, bf16[3,4,4,16,512]{4,3,2,1,0:T(8,128)(2,1)S(1)}, u32[]{:S(2)}, u32[]{:S(2)}) collective-permute-start(bf16[3,4,4,16,512]{4,3,2,1,0:T(8,128)(2,1)} %pad_maximum_fusion.3), channel_id=1, source_target_pairs={{0,1},{1,0},{2,3},{3,2},{4,5},{5,4},{6,7},{7,6},{8,9},{9,8},{10,11... | collective-permute-start | bytes 2359304 | tf_op jit(solution)/shard_map/ppermute | solution.py:768
  70.1 12.7 %copy-start.2 = (bf16[3,4,4,2,16,512]{5,4,3,2,1,0:T(8,128)(2,1)}, bf16[3,4,4,2,16,512]{5,4,3,2,1,0:T(8,128)(2,1)S(1)}, u32[]{:S(2)}) copy-start(bf16[3,4,4,2,16,512]{5,4,3,2,1,0:T(8,128)(2,1)S(1)} %pad_maximum_fusion.1) | copy-start | bytes 4718596
  70.1 22.6 %collective-permute-start.13 = (bf16[6,4,4,16,512]{4,3,2,1,0:T(8,128)(2,1)S(1)}, bf16[6,4,4,16,512]{4,3,2,1,0:T(8,128)(2,1)S(1)}, u32[]{:S(2)}, u32[]{:S(2)}) collective-permute-start(bf16[6,4,4,16,512]{4,3,2,1,0:T(8,128)(2,1)S(1)} %pad_maximum_fusion.2.rest_0_), channel_id=1, source_target_pairs={{0,1},{1,0},{2,3},{3,2},{4,5},{5,4},{6,7},{7,6},{8,9},{9,8},{10,11... | collective-permute-start | bytes 4718600 | tf_op jit(solution)/shard_map/ppermute | solution.py:768
  82.9 9.0 %copy-start.51 = (bf16[1024,256]{1,0:T(8,128)(2,1)}, bf16[1024,256]{1,0:T(8,128)(2,1)S(1)}, u32[]{:S(2)}) copy-start(bf16[1024,256]{1,0:T(8,128)(2,1)S(1)} %get-tuple-element.135.v_ref) | copy-start | bytes 1572868
  103.4 25.8 %copy-start.7 = (bf16[1024,512]{1,0:T(8,128)(2,1)S(1)}, bf16[1024,512]{1,0:T(8,128)(2,1)}, u32[]{:S(2)}) copy-start(bf16[1024,512]{1,0:T(8,128)(2,1)} %cot_ref.1) | copy-start | bytes 3145732
  103.4 25.8 %copy-start.9 = (bf16[1024,512]{1,0:T(8,128)(2,1)S(1)}, bf16[1024,512]{1,0:T(8,128)(2,1)}, u32[]{:S(2)}) copy-start(bf16[1024,512]{1,0:T(8,128)(2,1)} %x_ref.11) | copy-start | bytes 3145732
  129.2 34.1 %copy-start.31 = (bf16[1024,512]{1,0:T(8,128)(2,1)}, bf16[1024,512]{1,0:T(8,128)(2,1)S(1)}, u32[]{:S(2)}) copy-start(bf16[1024,512]{1,0:T(8,128)(2,1)S(1)} %get-tuple-element.129.h1b_ref) | copy-start | bytes 3145732
  164.3 23.8 %collective-permute-start.14 = (bf16[16,9,16,512]{3,2,1,0:T(8,128)(2,1)}, bf16[16,9,16,512]{3,2,1,0:T(8,128)(2,1)S(1)}, u32[]{:S(2)}, u32[]{:S(2)}) collective-permute-start(bf16[16,9,16,512]{3,2,1,0:T(8,128)(2,1)} %get-tuple-element.113.rest_0_), channel_id=1, source_target_pairs={{0,1},{1,0},{2,3},{3,2},{4,5},{5,4},{6,7},{7,6},{8,9},{9,8},{10,11... | collective-permute-start | bytes 7077896 | tf_op jit(solution)/shard_map/ppermute | solution.py:768
  171.7 16.4 %copy-start.11 = (bf16[16,9,16,512]{3,2,1,0:T(8,128)(2,1)S(1)}, bf16[16,9,16,512]{3,2,1,0:T(8,128)(2,1)}, u32[]{:S(2)}) copy-start(bf16[16,9,16,512]{3,2,1,0:T(8,128)(2,1)} %get-tuple-element.115) | copy-start | bytes 7077892
  188.1 20.8 %copy-start.14 = (bf16[2048,256]{1,0:T(8,128)(2,1)}, bf16[2048,256]{1,0:T(8,128)(2,1)S(1)}, u32[]{:S(2)}) copy-start(bf16[2048,256]{1,0:T(8,128)(2,1)S(1)} %get-tuple-element.114.ka_ref) | copy-start | bytes 3145732
  188.1 20.8 %copy-start.16 = (bf16[2048,256]{1,0:T(8,128)(2,1)}, bf16[2048,256]{1,0:T(8,128)(2,1)S(1)}, u32[]{:S(2)}) copy-start(bf16[2048,256]{1,0:T(8,128)(2,1)S(1)} %get-tuple-element.122.va_ref) | copy-start | bytes 3145732
  188.8 32.9 %collective-permute-start.15 = (bf16[4,9,16,512]{3,2,1,0:T(8,128)(2,1)S(1)}, bf16[4,9,16,512]{3,2,1,0:T(8,128)(2,1)S(1)}, u32[]{:S(2)}, u32[]{:S(2)}) collective-permute-start(bf16[4,9,16,512]{3,2,1,0:T(8,128)(2,1)S(1)} %get-tuple-element.118.rest_0_), channel_id=1, source_target_pairs={{0,2},{1,3},{2,0},{3,1},{4,6},{5,7},{6,4},{7,5},{8,10},{9,11},{10,... | collective-permute-start | bytes 1769480 | tf_op jit(solution)/shard_map/ppermute | solution.py:768
  190.9 30.8 %collective-permute-start.16 = (bf16[4,9,16,512]{3,2,1,0:T(8,128)(2,1)S(1)}, bf16[4,9,16,512]{3,2,1,0:T(8,128)(2,1)S(1)}, u32[]{:S(2)}, u32[]{:S(2)}) collective-permute-start(bf16[4,9,16,512]{3,2,1,0:T(8,128)(2,1)S(1)} %get-tuple-element.119.rest_1_), channel_id=1, source_target_pairs={{0,4},{1,5},{2,6},{3,7},{4,0},{5,1},{6,2},{7,3},{8,12},{9,13},{10,... | collective-permute-start | bytes 1769480 | tf_op jit(solution)/shard_map/ppermute | solution.py:768
  191.3 17.6 %copy-start.6 = (bf16[2048,512]{1,0:T(8,128)(2,1)S(1)}, bf16[2048,512]{1,0:T(8,128)(2,1)}, u32[]{:S(2)}) copy-start(bf16[2048,512]{1,0:T(8,128)(2,1)} %memory_ref.3) | copy-start | bytes 6291460
  207.6 16.9 %collective-permute-start.17 = (bf16[4,9,16,512]{3,2,1,0:T(8,128)(2,1)S(1)}, bf16[4,9,16,512]{3,2,1,0:T(8,128)(2,1)S(1)}, u32[]{:S(2)}, u32[]{:S(2)}) collective-permute-start(bf16[4,9,16,512]{3,2,1,0:T(8,128)(2,1)S(1)} %get-tuple-element.120.rest_2_), channel_id=1, source_target_pairs={{0,6},{1,7},{2,4},{3,5},{4,2},{5,3},{6,0},{7,1},{8,14},{9,15},{10,... | collective-permute-start | bytes 1769480 | tf_op jit(solution)/shard_map/ppermute | solution.py:768
  220.9 8.4 %copy-start.29 = (bf16[1024,512]{1,0:T(8,128)(2,1)}, bf16[1024,512]{1,0:T(8,128)(2,1)S(1)}, u32[]{:S(2)}) copy-start(bf16[1024,512]{1,0:T(8,128)(2,1)S(1)} %get-tuple-element.130.do_ref) | copy-start | bytes 3145732
  220.9 18.3 %collective-permute-start.18 = (bf16[16,5,16,512]{3,2,1,0:T(8,128)(2,1)S(1)}, bf16[16,5,16,512]{3,2,1,0:T(8,128)(2,1)S(1)}, u32[]{:S(2)}, u32[]{:S(2)}) collective-permute-start(bf16[16,5,16,512]{3,2,1,0:T(8,128)(2,1)S(1)} %get-tuple-element.144.rest_3_), channel_id=1, source_target_pairs={{0,1},{1,0},{2,3},{3,2},{4,5},{5,4},{6,7},{7,6},{8,9},{9,8},{10,11... | collective-permute-start | bytes 3932168 | tf_op jit(solution)/shard_map/ppermute | solution.py:768
  224.8 14.2 %collective-permute-start.32 = (bf16[1,9,16,512]{3,2,1,0:T(8,128)(2,1)S(1)}, bf16[1,9,16,512]{3,2,1,0:T(8,128)(2,1)S(1)}, u32[]{:S(2)}, u32[]{:S(2)}) collective-permute-start(bf16[1,9,16,512]{3,2,1,0:T(8,128)(2,1)S(1)} %get-tuple-element.141.rest_0_), channel_id=1, source_target_pairs={{0,8},{1,9},{2,10},{3,11},{4,12},{5,13},{6,14},{7,15},{8,0},{9,1},... | collective-permute-start | bytes 442376 | tf_op jit(solution)/shard_map/ppermute | solution.py:768
  224.9 14.1 %collective-permute-start.33 = (bf16[1,9,16,512]{3,2,1,0:T(8,128)(2,1)S(1)}, bf16[1,9,16,512]{3,2,1,0:T(8,128)(2,1)S(1)}, u32[]{:S(2)}, u32[]{:S(2)}) collective-permute-start(bf16[1,9,16,512]{3,2,1,0:T(8,128)(2,1)S(1)} %get-tuple-element.142.rest_1_), channel_id=1, source_target_pairs={{0,16},{1,17},{2,18},{3,19},{4,20},{5,21},{6,22},{7,23},{8,24},{9,... | collective-permute-start | bytes 442376 | tf_op jit(solution)/shard_map/ppermute | solution.py:768
  227.5 11.6 %collective-permute-start.34 = (bf16[1,9,16,512]{3,2,1,0:T(8,128)(2,1)S(1)}, bf16[1,9,16,512]{3,2,1,0:T(8,128)(2,1)S(1)}, u32[]{:S(2)}, u32[]{:S(2)}) collective-permute-start(bf16[1,9,16,512]{3,2,1,0:T(8,128)(2,1)S(1)} %get-tuple-element.143.rest_2_), channel_id=1, source_target_pairs={{0,24},{1,25},{2,26},{3,27},{4,28},{5,29},{6,30},{7,31},{8,16},{9,... | collective-permute-start | bytes 442376 | tf_op jit(solution)/shard_map/ppermute | solution.py:768
  239.6 14.4 %collective-permute-start.26 = (bf16[4,5,16,512]{3,2,1,0:T(8,128)(2,1)S(1)}, bf16[4,5,16,512]{3,2,1,0:T(8,128)(2,1)S(1)}, u32[]{:S(2)}, u32[]{:S(2)}) collective-permute-start(bf16[4,5,16,512]{3,2,1,0:T(8,128)(2,1)S(1)} %get-tuple-element.149.rest_2_), channel_id=1, source_target_pairs={{0,2},{1,3},{2,0},{3,1},{4,6},{5,7},{6,4},{7,5},{8,10},{9,11},{10,... | collective-permute-start | bytes 983048 | tf_op jit(solution)/shard_map/ppermute | solution.py:768
  240.0 16.2 %collective-permute-start.27 = (bf16[4,5,16,512]{3,2,1,0:T(8,128)(2,1)S(1)}, bf16[4,5,16,512]{3,2,1,0:T(8,128)(2,1)S(1)}, u32[]{:S(2)}, u32[]{:S(2)}) collective-permute-start(bf16[4,5,16,512]{3,2,1,0:T(8,128)(2,1)S(1)} %get-tuple-element.150.rest_3_), channel_id=1, source_target_pairs={{0,4},{1,5},{2,6},{3,7},{4,0},{5,1},{6,2},{7,3},{8,12},{9,13},{10,... | collective-permute-start | bytes 983048 | tf_op jit(solution)/shard_map/ppermute | solution.py:768
  242.2 14.0 %collective-permute-start.28 = (bf16[4,5,16,512]{3,2,1,0:T(8,128)(2,1)S(1)}, bf16[4,5,16,512]{3,2,1,0:T(8,128)(2,1)S(1)}, u32[]{:S(2)}, u32[]{:S(2)}) collective-permute-start(bf16[4,5,16,512]{3,2,1,0:T(8,128)(2,1)S(1)} %get-tuple-element.151.rest_4_), channel_id=1, source_target_pairs={{0,6},{1,7},{2,4},{3,5},{4,2},{5,3},{6,0},{7,1},{8,14},{9,15},{10,... | collective-permute-start | bytes 983048 | tf_op jit(solution)/shard_map/ppermute | solution.py:768
  254.0 14.9 %collective-permute-start.19 = (bf16[16,3,16,512]{3,2,1,0:T(8,128)(2,1)}, bf16[16,3,16,512]{3,2,1,0:T(8,128)(2,1)}, u32[]{:S(2)}, u32[]{:S(2)}) collective-permute-start(bf16[16,3,16,512]{3,2,1,0:T(8,128)(2,1)} %get-tuple-element.154), channel_id=1, source_target_pairs={{0,1},{1,0},{2,3},{3,2},{4,5},{5,4},{6,7},{7,6},{8,9},{9,8},{10,11... | collective-permute-start | bytes 2359304 | tf_op jit(solution)/shard_map/ppermute | solution.py:768
  256.4 8.9 %collective-permute-start.29 = (bf16[1,5,16,512]{3,2,1,0:T(8,128)(2,1)S(1)}, bf16[1,5,16,512]{3,2,1,0:T(8,128)(2,1)S(1)}, u32[]{:S(2)}, u32[]{:S(2)}) collective-permute-start(bf16[1,5,16,512]{3,2,1,0:T(8,128)(2,1)S(1)} %get-tuple-element.168), channel_id=1, source_target_pairs={{0,8},{1,9},{2,10},{3,11},{4,12},{5,13},{6,14},{7,15},{8,0},{9,1},... | collective-permute-start | bytes 245768 | tf_op jit(solution)/shard_map/ppermute | solution.py:768
  259.8 9.0 %collective-permute-start.30 = (bf16[1,5,16,512]{3,2,1,0:T(8,128)(2,1)S(1)}, bf16[1,5,16,512]{3,2,1,0:T(8,128)(2,1)S(1)}, u32[]{:S(2)}, u32[]{:S(2)}) collective-permute-start(bf16[1,5,16,512]{3,2,1,0:T(8,128)(2,1)S(1)} %get-tuple-element.169), channel_id=1, source_target_pairs={{0,16},{1,17},{2,18},{3,19},{4,20},{5,21},{6,22},{7,23},{8,24},{9,... | collective-permute-start | bytes 245768 | tf_op jit(solution)/shard_map/ppermute | solution.py:768
  261.8 7.0 %collective-permute-start.31 = (bf16[1,5,16,512]{3,2,1,0:T(8,128)(2,1)S(1)}, bf16[1,5,16,512]{3,2,1,0:T(8,128)(2,1)S(1)}, u32[]{:S(2)}, u32[]{:S(2)}) collective-permute-start(bf16[1,5,16,512]{3,2,1,0:T(8,128)(2,1)S(1)} %get-tuple-element.170), channel_id=1, source_target_pairs={{0,24},{1,25},{2,26},{3,27},{4,28},{5,29},{6,30},{7,31},{8,16},{9,... | collective-permute-start | bytes 245768 | tf_op jit(solution)/shard_map/ppermute | solution.py:768
  272.2 7.0 %collective-permute-start.20 = (bf16[4,3,16,512]{3,2,1,0:T(8,128)(2,1)S(1)}, bf16[4,3,16,512]{3,2,1,0:T(8,128)(2,1)S(1)}, u32[]{:S(2)}, u32[]{:S(2)}) collective-permute-start(bf16[4,3,16,512]{3,2,1,0:T(8,128)(2,1)S(1)} %get-tuple-element.155.rest_0_), channel_id=1, source_target_pairs={{0,2},{1,3},{2,0},{3,1},{4,6},{5,7},{6,4},{7,5},{8,10},{9,11},{10,... | collective-permute-start | bytes 589832 | tf_op jit(solution)/shard_map/ppermute | solution.py:768
  273.8 8.3 %collective-permute-start.21 = (bf16[4,3,16,512]{3,2,1,0:T(8,128)(2,1)S(1)}, bf16[4,3,16,512]{3,2,1,0:T(8,128)(2,1)S(1)}, u32[]{:S(2)}, u32[]{:S(2)}) collective-permute-start(bf16[4,3,16,512]{3,2,1,0:T(8,128)(2,1)S(1)} %get-tuple-element.156.rest_1_), channel_id=1, source_target_pairs={{0,4},{1,5},{2,6},{3,7},{4,0},{5,1},{6,2},{7,3},{8,12},{9,13},{10,... | collective-permute-start | bytes 589832 | tf_op jit(solution)/shard_map/ppermute | solution.py:768
  274.0 8.2 %collective-permute-start.22 = (bf16[4,3,16,512]{3,2,1,0:T(8,128)(2,1)S(1)}, bf16[4,3,16,512]{3,2,1,0:T(8,128)(2,1)S(1)}, u32[]{:S(2)}, u32[]{:S(2)}) collective-permute-start(bf16[4,3,16,512]{3,2,1,0:T(8,128)(2,1)S(1)} %get-tuple-element.157.rest_2_), channel_id=1, source_target_pairs={{0,6},{1,7},{2,4},{3,5},{4,2},{5,3},{6,0},{7,1},{8,14},{9,15},{10,... | collective-permute-start | bytes 589832 | tf_op jit(solution)/shard_map/ppermute | solution.py:768
  282.2 5.9 %copy-start.17 = (bf16[2048,256]{1,0:T(8,128)(2,1)S(1)}, bf16[2048,256]{1,0:T(8,128)(2,1)}, u32[]{:S(2)}) copy-start(bf16[2048,256]{1,0:T(8,128)(2,1)} %copy-done.16) | copy-start | bytes 3145732
  282.2 5.9 %copy-start.19 = (bf16[2048,256]{1,0:T(8,128)(2,1)S(1)}, bf16[2048,256]{1,0:T(8,128)(2,1)}, u32[]{:S(2)}) copy-start(bf16[2048,256]{1,0:T(8,128)(2,1)} %copy-done.18) | copy-start | bytes 3145732
  282.3 9.6 %collective-permute-start.23 = (bf16[1,3,16,512]{3,2,1,0:T(8,128)(2,1)S(1)}, bf16[1,3,16,512]{3,2,1,0:T(8,128)(2,1)S(1)}, u32[]{:S(2)}, u32[]{:S(2)}) collective-permute-start(bf16[1,3,16,512]{3,2,1,0:T(8,128)(2,1)S(1)} %get-tuple-element.160), channel_id=1, source_target_pairs={{0,8},{1,9},{2,10},{3,11},{4,12},{5,13},{6,14},{7,15},{8,0},{9,1},... | collective-permute-start | bytes 147464 | tf_op jit(solution)/shard_map/ppermute | solution.py:768
  285.1 6.7 %collective-permute-start.24 = (bf16[1,3,16,512]{3,2,1,0:T(8,128)(2,1)S(1)}, bf16[1,3,16,512]{3,2,1,0:T(8,128)(2,1)S(1)}, u32[]{:S(2)}, u32[]{:S(2)}) collective-permute-start(bf16[1,3,16,512]{3,2,1,0:T(8,128)(2,1)S(1)} %get-tuple-element.161), channel_id=1, source_target_pairs={{0,16},{1,17},{2,18},{3,19},{4,20},{5,21},{6,22},{7,23},{8,24},{9,... | collective-permute-start | bytes 147464 | tf_op jit(solution)/shard_map/ppermute | solution.py:768
  286.6 6.0 %collective-permute-start.25 = (bf16[1,3,16,512]{3,2,1,0:T(8,128)(2,1)S(1)}, bf16[1,3,16,512]{3,2,1,0:T(8,128)(2,1)S(1)}, u32[]{:S(2)}, u32[]{:S(2)}) collective-permute-start(bf16[1,3,16,512]{3,2,1,0:T(8,128)(2,1)S(1)} %get-tuple-element.162), channel_id=1, source_target_pairs={{0,24},{1,25},{2,26},{3,27},{4,28},{5,29},{6,30},{7,31},{8,16},{9,... | collective-permute-start | bytes 147464 | tf_op jit(solution)/shard_map/ppermute | solution.py:768
  (46 other events, 130.9 us)
Sparse Core Ops, SparseCore 0:
  37.2 62.4 all-gather.1

commit v3 on v2

v3 whole, which is shorter than its diff:
```python
import functools
import jax
import jax.numpy as jnp
from jax import lax
from jax.experimental import pallas as pl
from jax.experimental.pallas import tpu as pltpu
from jax.sharding import PartitionSpec as P

HD = 64
LANES = 128
MOST = 256
QROWS = 128
FORWARD_ITEMS = 2
BACKWARD_ITEMS = 3
FFN_CHUNK = 256
masked_score = -1e30
norm_eps = 1e-05
bf16, f32 = jnp.bfloat16, jnp.float32
NT = (((1,), (1,)), ((), ()))
TN = (((0,), (0,)), ((), ()))
NN = (((1,), (0,)), ((), ()))


def mm(left, right, dims=NN):
    return lax.dot_general(left, right, dims, preferred_element_type=f32)


def norm_rows(source):
    mean = jnp.mean(source, axis=-1, keepdims=True)
    centered = source - mean
    variance = jnp.mean(centered * centered, axis=-1, keepdims=True)
    rstd = lax.rsqrt(variance + norm_eps)
    return centered * rstd, rstd


def lane_below(rows):
    return lax.broadcasted_iota(jnp.int32, (rows, LANES), 1) < HD


def column_of(row):
    return jnp.broadcast_to(row, (LANES, row.shape[1])).T


def head_part(pair, which, low):
    return jnp.where(low == (which == 0), pair, jnp.zeros_like(pair))


def values_with_ones(values):
    parts = []
    for p in range(values.shape[1] // LANES):
        pair = values[:, p * LANES : (p + 1) * LANES]
        parts += [pair, jnp.ones_like(pair)]
    return jnp.concatenate(parts, axis=1)


def finish_heads(at, top, tot, acc, write):
    shape = acc.shape[0], at.size if hasattr(at, "size") else at.stop - at.start, LANES
    lane = lax.broadcasted_iota(jnp.int32, shape[1:], 1)
    sums, tops = jnp.ones(shape[1:], f32), jnp.zeros(shape[1:], f32)
    for p in range(shape[0]):
        total = tot[p, at, :]
        write(p, (acc[p, at, :] / total).astype(bf16))
        sums = jnp.where(lane % HD == p, total, sums)
        tops = jnp.where(lane == p, top[2 * p, at, :], jnp.where(lane == HD + p, top[2 * p + 1, at, :], tops))
    return tops + jnp.log(sums)


def column_at(head):
    return head % 2 * HD + head // 2


def item_at(items_ref, n, idk_ref, ids_q, keys, tile, block, causal):
    begin = pl.multiple_of(items_ref[0, n] * block, block)
    wanted = items_ref[1, n] * LANES
    start = pl.multiple_of(jnp.minimum(wanted, keys - tile), LANES)
    at = pl.ds(begin, block)
    pos = start + lax.broadcasted_iota(jnp.int32, (1, tile), 1)
    ids_k = jnp.where(pos >= wanted, idk_ref[:, pl.ds(start, tile)], -1)
    allowed = ids_q[at, :1] == ids_k
    if causal:
        allowed &= pos <= begin + lax.broadcasted_iota(jnp.int32, (block, 1), 0)
    return at, pl.ds(start, tile), jnp.where(allowed, 0.0, masked_score).astype(f32)


def attend(items_ref, idk_ref, ids_q, q_all, k_all, vx_all, top, tot, acc, tile, block, causal):
    keys, width = k_all.shape
    pairs = width // LANES
    heads = 2 * pairs
    low = lane_below(block)
    top[...] = jnp.full(top.shape, masked_score, f32)
    tot[...] = jnp.zeros(tot.shape, f32)
    acc[...] = jnp.zeros(acc.shape, f32)

    def some(i, _):
        loads, made = [], []
        for t in range(FORWARD_ITEMS):
            at, there, bias = item_at(items_ref, FORWARD_ITEMS * i + t, idk_ref, ids_q, keys, tile, block, causal)
            loads.append((at, there, bias))
            for p in range(pairs):
                cols = slice(p * LANES, (p + 1) * LANES)
                part = q_all[at, cols]
                both = jnp.concatenate([head_part(part, h, low) for h in range(2)])
                made.append(mm(both, k_all[there, cols], NT))
        weights, scales = [], []
        for t, (at, there, bias) in enumerate(loads):
            for head in range(heads):
                s = made[t * pairs + head // 2][head % 2 * block : (head % 2 + 1) * block] + bias
                old = top[head, at, :]
                new = jnp.maximum(old, jnp.max(s, axis=1, keepdims=True))
                top[head, at, :] = new
                scales.append(jnp.exp(old - new))
                weights.append(jnp.exp(s - jnp.concatenate([new] * (tile // LANES), axis=1)).astype(bf16))
        mixed = [
            mm(jnp.concatenate(weights[t * heads + 2 * p : t * heads + 2 * p + 2]), vx_all[there, 2 * p * LANES : 2 * (p + 1) * LANES])
            for t, (_, there, _) in enumerate(loads) for p in range(pairs)
        ]
        for t, (at, _, _) in enumerate(loads):
            for p in range(pairs):
                n = t * pairs + p
                scale = jnp.where(low, scales[2 * n], scales[2 * n + 1])
                o = mixed[n]
                acc[p, at, :] = acc[p, at, :] * scale + jnp.where(low, o[:block, :LANES], o[block:, :LANES])
                tot[p, at, :] = tot[p, at, :] * scale + jnp.where(low, o[:block, LANES:], o[block:, LANES:])
        return 0

    lax.fori_loop(0, items_ref[2, 0], some, 0)


def attend_back(items_ref, idk_ref, ids_q, q_all, do_ref, k_ref, v_ref, l_ref, delta_ref, dq, dk, dv, tile, block, first_log, first_head, causal):
    keys, width = k_ref.shape
    pairs = width // LANES
    low = lane_below(block)

    def some(i, _):
        loads, scores, grads = [], [], []
        for t in range(BACKWARD_ITEMS):
            at, there, bias = item_at(items_ref, BACKWARD_ITEMS * i + t, idk_ref, ids_q, keys, tile, block, causal)
            loads.append((at, there, bias))
            for p in range(pairs):
                cols = slice(p * LANES, (p + 1) * LANES)
                q, do = q_all[at, cols], do_ref[at, cols]
                qs = jnp.concatenate([head_part(q, h, low) for h in range(2)])
                dos = jnp.concatenate([head_part(do, h, low) for h in range(2)])
                scores.append((mm(qs, k_ref[there, cols], NT), qs))
                grads.append((mm(dos, v_ref[there, cols], NT), dos))
        weights, slopes = [], []
        for t, (at, there, bias) in enumerate(loads):
            logs, deltas = l_ref[at, :], delta_ref[at, :]
            for p in range(pairs):
                es, ds = [], []
                for h in range(2):
                    lane = column_at(first_log + 2 * p + h)
                    other = column_at(first_head + 2 * p + h)
                    rows = slice(h * block, (h + 1) * block)
                    e = jnp.exp(scores[t * pairs + p][0][rows] + bias - logs[:, lane : lane + 1])
                    es.append(e.astype(bf16))
                    ds.append((e * (grads[t * pairs + p][0][rows] - deltas[:, other : other + 1])).astype(bf16))
                weights.append(jnp.concatenate(es))
                slopes.append(jnp.concatenate(ds))
        for t, (at, there, _) in enumerate(loads):
            for p in range(pairs):
                cols = slice(p * LANES, (p + 1) * LANES)
                n = t * pairs + p
                gq = mm(slopes[n], k_ref[there, cols])
                gk = mm(slopes[n], scores[n][1], TN)
                gv = mm(weights[n], grads[n][1], TN)
                dq[at, cols] += jnp.where(low, gq[:block], gq[block:])
                dk[there, cols] += gk
                dv[there, cols] += gv
        return 0

    lax.fori_loop(0, items_ref[3, 0], some, 0)


def self_forward_kernel(tile, block, items_ref, x_ref, wq_ref, wk_ref, wv_ref, idr_ref, *rest):
    q_ref, k_ref, v_ref, o_ref, l_ref, q_all, k_all, vx_all, ids_all, top, tot, acc = rest[-12:]
    step = pl.program_id(0)
    rows = x_ref.shape[0]
    total, width = k_all.shape
    turns = total // rows

    @pl.when(step < turns)
    def _():
        x = x_ref[...]
        q = mm(x, wq_ref[0]).astype(bf16)
        k = mm(x, wk_ref[0]).astype(bf16)
        v = mm(x, wv_ref[0]).astype(bf16)
        q_ref[...] = q
        k_ref[...] = k
        v_ref[...] = v
        here = pl.ds(pl.multiple_of(step * rows, rows), rows)
        q_all[here, :] = q * jnp.asarray(HD ** -0.5, bf16)
        k_all[here, :] = k
        vx_all[here, :] = values_with_ones(v)
        ids_all[here, :] = column_of(idr_ref[:, here])

    @pl.when(step == turns)
    def _():
        attend(items_ref, idr_ref, ids_all, q_all, k_all, vx_all, top, tot, acc, tile, block, True)
        size = 2 * block
        for j in range(total // size):
            at = slice(j * size, (j + 1) * size)

            def write(p, value):
                o_ref[at, p * LANES : (p + 1) * LANES] = value

            l_ref[at, :] = finish_heads(at, top, tot, acc, write)


def whole(a):
    return pl.BlockSpec(a.shape, lambda *_: (0,) * a.ndim)


def part(weights, index, columns, half):
    return pl.BlockSpec((1, weights.shape[1], columns), lambda *_: (index, 0, half))


def params(us, vmem):
    return dict(
        compiler_params=pltpu.CompilerParams(vmem_limit_bytes=vmem * 2**20),
        cost_estimate=pl.CostEstimate(flops=us * 10**9, bytes_accessed=2**20, transcendentals=0),
    )


apart = pl.BlockSpec(memory_space=pl.ANY)


def out_array(shape, dtype):
    return pltpu.HBM(shape, dtype)


def placed(*arrays):
    return [pltpu.with_memory_space_constraint(a, pltpu.HBM) for a in arrays]


def self_forward(items, x, weights, idr, half, after, turns=4, block=QROWS, tile=256):
    total, width = x.shape
    columns = width // 2
    heads = columns // HD
    rows = total // turns
    early = lambda w: pl.BlockSpec((rows, w), lambda i, *_: (jnp.minimum(i, turns - 1), 0))
    fixed = lambda w: pl.BlockSpec((total, w), lambda i, *_: (0, 0))
    sds = out_array
    full = sds((total, columns), bf16)
    return pl.pallas_call(
        functools.partial(self_forward_kernel, tile, block),
        grid_spec=pltpu.PrefetchScalarGridSpec(
            num_scalar_prefetch=1,
            grid=(turns + 1,),
            in_specs=[early(width)] + [part(weights, i, columns, half) for i in range(3)] + [whole(idr)] + [apart] * len(after),
            out_specs=[early(columns)] * 3 + [fixed(columns), fixed(LANES)],
            scratch_shapes=[
                pltpu.VMEM((total, columns), bf16), pltpu.VMEM((total, columns), bf16), pltpu.VMEM((total, 2 * columns), bf16),
                pltpu.VMEM((total, LANES), jnp.int32),
                pltpu.VMEM((heads, total, LANES), f32), pltpu.VMEM((heads // 2, total, LANES), f32), pltpu.VMEM((heads // 2, total, LANES), f32),
            ],
        ),
        out_shape=[full] * 4 + [sds((total, LANES), f32)],
        name="self_forward",
        **params(6, 24),
    )(items, *placed(x, weights, weights, weights), idr, *after)


def cross_forward_kernel(
    tile, block, items_ref, memory_ref, wk_ref, wv_ref, x_ref, oa_ref, ob_ref, wso_ref, wcq_ref, wco_ref, norms_ref, idr_ref, idk_ref,
    k2_ref, v2_ref, r1_ref, h1b_ref, q2_ref, o_ref, l_ref, r2_ref, k_all, vx_all, q_all, h_all, ids_all, top, tot, acc,
):
    step = pl.program_id(0)
    rows, width = x_ref.shape
    keys = k_all.shape[0]
    turns = pl.num_programs(0) // 2

    @pl.when(step < turns)
    def _():
        per = memory_ref.shape[0]
        memory = memory_ref[...]
        half = width // 2
        r1 = x_ref[...].astype(f32) + mm(oa_ref[...], wso_ref[0, :half, :]) + mm(ob_ref[...], wso_ref[0, half:, :])
        k2 = mm(memory, wk_ref[0]).astype(bf16)
        r1_ref[...] = r1.astype(bf16)
        n1, _ = norm_rows(r1)
        v2 = mm(memory, wv_ref[0]).astype(bf16)
        h1 = n1 * norms_ref[0:1, :] + norms_ref[1:2, :]
        h1b = h1.astype(bf16)
        h1b_ref[...] = h1b
        q2 = mm(h1b, wcq_ref[0]).astype(bf16)
        q2_ref[...] = q2
        k2_ref[...] = k2
        v2_ref[...] = v2
        here = pl.ds(pl.multiple_of(step * rows, rows), rows)
        q_all[here, :] = q2 * jnp.asarray(HD ** -0.5, bf16)
        h_all[here, :] = h1
        ids_all[here, :] = column_of(idr_ref[:, here])
        there = pl.ds(pl.multiple_of(step * per, per), per)
        k_all[there, :] = k2
        vx_all[there, :] = values_with_ones(v2)

    @pl.when(step == turns)
    def _():
        attend(items_ref, idk_ref, ids_all, q_all, k_all, vx_all, top, tot, acc, tile, block, False)

    @pl.when(step >= turns)
    def _():
        for sub in range(rows // block):
            inner = slice(sub * block, (sub + 1) * block)
            at = pl.ds(pl.multiple_of((step - turns) * rows + sub * block, block), block)

            def write(p, value):
                o_ref[inner, p * LANES : (p + 1) * LANES] = value

            l_ref[inner, :] = finish_heads(at, top, tot, acc, write)
        here = pl.ds(pl.multiple_of((step - turns) * rows, rows), rows)
        r2_ref[...] = h_all[here, :] + mm(o_ref[...], wco_ref[0])


def cross_forward(items, memory, x, oa, ob, weights, norms, idr, idk, turns=4, block=QROWS, tile=256):
    total, width = x.shape
    keys = memory.shape[0]
    heads = width // HD
    rows, per = total // turns, keys // turns
    early = lambda r, w: pl.BlockSpec((r, w), lambda i, *_: (jnp.minimum(i, turns - 1), 0))
    late = lambda w: pl.BlockSpec((rows, w), lambda i, *_: (jnp.maximum(i - turns, 0), 0))
    sds = out_array
    return pl.pallas_call(
        functools.partial(cross_forward_kernel, tile, block),
        grid_spec=pltpu.PrefetchScalarGridSpec(
            num_scalar_prefetch=1,
            grid=(2 * turns,),
            in_specs=[early(per, width), part(weights, 3, width, 0), part(weights, 4, width, 0)]
            + [early(rows, width), early(rows, width // 2), early(rows, width // 2)]
            + [part(weights, i, width, 0) for i in range(3)]
            + [whole(norms), whole(idr), whole(idk)],
            out_specs=[early(per, width)] * 2 + [early(rows, width)] * 3 + [late(width), late(LANES), late(width)],
            scratch_shapes=[
                pltpu.VMEM((keys, width), bf16),
                pltpu.VMEM((keys, 2 * width), bf16),
                pltpu.VMEM((total, width), bf16),
                pltpu.VMEM((total, width), f32),
                pltpu.VMEM((total, LANES), jnp.int32),
                pltpu.VMEM((heads, total, LANES), f32),
                pltpu.VMEM((heads // 2, total, LANES), f32),
                pltpu.VMEM((heads // 2, total, LANES), f32),
            ],
        ),
        out_shape=[
            sds((keys, width), bf16), sds((keys, width), bf16), sds((total, width), bf16), sds((total, width), bf16),
            sds((total, width), bf16), sds((total, width), bf16), sds((total, LANES), f32), sds((total, width), f32),
        ],
        name="cross_forward",
        **params(24, 44),
    )(items, *placed(memory, weights, weights, x, oa, ob, weights, weights, weights), norms, idr, idk)


def norm_back(incoming, normal, rstd, gain):
    m = incoming * gain
    return rstd * (
        m - jnp.mean(m, axis=-1, keepdims=True) - normal * jnp.mean(m * normal, axis=-1, keepdims=True)
    )


def head_columns(left, right):
    width = left.shape[1]
    prod = left.astype(f32) * right.astype(f32)
    lane = lax.broadcasted_iota(jnp.int32, (width, LANES), 1)
    own = lax.broadcasted_iota(jnp.int32, (width, LANES), 0) // HD == 2 * (lane % HD) + lane // HD
    own = own.astype(bf16)
    high = prod.astype(bf16)
    low = (prod - high.astype(f32)).astype(bf16)
    return mm(high, own) + mm(low, own)


def column_sums(a):
    return jnp.sum(a, axis=0, keepdims=True)


def spread(keep_ref, send_ref, core, write):
    def one(j, _):
        write(2 * j + core, keep_ref, j)
        write(2 * j + 1 - core, send_ref, j)
        return 0

    lax.fori_loop(0, keep_ref.shape[0], one, 0)


def ffn_kernel(
    core_ref, r2_ref, x_ref, cot_ref, o2_ref, w_ref, wco_ref, norms_ref,
    out_ref, dr3_ref, dr2_ref, do2_ref, delta_ref, keep_ref, send_ref, gn_ref, gin, gout, gco,
):
    step = pl.program_id(0)
    last = pl.num_programs(0) - 1
    width = x_ref.shape[1]
    blocks = w_ref.shape[1] // 2

    @pl.when(step == 0)
    def _():
        gin[...] = jnp.zeros_like(gin)
        gout[...] = jnp.zeros_like(gout)
        gco[...] = jnp.zeros_like(gco)
        gn_ref[...] = jnp.zeros_like(gn_ref)

    win = [w_ref[:, c].reshape(width, width) for c in range(blocks)]
    wout = w_ref[:, blocks:].reshape(blocks * width, width)
    n2, rstd2 = norm_rows(r2_ref[...])
    h2 = n2 * norms_ref[2:3, :] + norms_ref[3:4, :]
    h2b = h2.astype(bf16)
    chunk = min(FFN_CHUNK, width)
    parts = blocks * width // chunk
    per = width // chunk

    def win_part(c):
        return win[c // per][:, (c % per) * chunk : (c % per + 1) * chunk]

    acts, slopes, hidden = [], [], [mm(h2b, win_part(0))]
    ff = jnp.zeros(h2.shape, f32)
    for c in range(parts):
        if c + 1 < parts:
            hidden.append(mm(h2b, win_part(c + 1)))
        u = hidden[c]
        square = u * u
        t = jnp.tanh(u * (0.7978845608028654 + (0.7978845608028654 * 0.044715) * square))
        half = 0.5 + 0.5 * t
        acts.append((u * half).astype(bf16))
        rise = u * (0.5 * 0.7978845608028654 + (0.5 * 0.7978845608028654 * 3 * 0.044715) * square)
        slopes.append(half + (1.0 - t * t) * rise)
        if c:
            ff += mm(acts[c - 1], wout[(c - 1) * chunk : c * chunk, :])
    ff += mm(acts[-1], wout[(parts - 1) * chunk :, :])
    r3 = h2 + ff + x_ref[...].astype(f32)
    n3, rstd3 = norm_rows(r3)
    gain3 = norms_ref[4:5, :]
    out_ref[...] = (n3 * gain3 + norms_ref[5:6, :]).astype(bf16)
    e = cot_ref[...].astype(f32)
    gn_ref[2:3, :] += column_sums(e * n3)
    gn_ref[3:4, :] += column_sums(e)
    dr3 = norm_back(e, n3, rstd3, gain3)
    dr3_ref[...] = dr3.astype(bf16)
    dfb = dr3.astype(bf16)
    dh2 = dr3
    raw, made = [mm(dfb, wout[:chunk, :], NT)], []
    for c in range(parts + 1):
        if c + 1 < parts:
            raw.append(mm(dfb, wout[(c + 1) * chunk : (c + 2) * chunk, :], NT))
        if c < parts:
            gout[c * chunk : (c + 1) * chunk, :] += mm(acts[c], dfb, TN)
            made.append((raw[c] * slopes[c]).astype(bf16))
        if c:
            gin[:, (c - 1) * chunk : c * chunk] += mm(h2b, made[c - 1], TN)
            dh2 += mm(made[c - 1], win_part(c - 1), NT)
    gn_ref[0:1, :] += column_sums(dh2 * n2)
    gn_ref[1:2, :] += column_sums(dh2)
    dr2 = norm_back(dh2, n2, rstd2, norms_ref[2:3, :])
    da2 = dr2.astype(bf16)
    dr2_ref[...] = da2
    o2 = o2_ref[...]
    gco[...] += mm(o2, da2, TN)
    do2 = mm(da2, wco_ref[0], NT).astype(bf16)
    do2_ref[...] = do2
    delta_ref[...] = head_columns(do2, o2)

    @pl.when(step == last)
    def _():
        r = keep_ref.shape[2]

        def write(device, ref, j):
            here = pl.ds(pl.multiple_of(device * r, r), r)
            for c in range(blocks):
                ref[j, c] = gin[here, c * width : (c + 1) * width].astype(bf16)
            ref[j, blocks] = gco[here, :].astype(bf16)
            there = pl.ds(pl.multiple_of(device * blocks * r, blocks * r), blocks * r)
            ref[j, blocks + 1 :] = gout[there, :].astype(bf16).reshape(blocks, r, width)

        spread(keep_ref, send_ref, core_ref[0], write)


def ffn(core, pairs, r2, x, cot, o2, w, weights, index, norms, rows=512):
    total, width = x.shape
    blocks = w.shape[1] // 2
    rowspec = lambda w: pl.BlockSpec((rows, w), lambda i: (i, 0))
    sds = out_array
    side = jax.ShapeDtypeStruct((pairs, 2 * blocks + 1, width // (2 * pairs), width), bf16)
    return pl.pallas_call(
        ffn_kernel,
        grid=(total // rows,),
        in_specs=[pl.BlockSpec(memory_space=pltpu.SMEM)] + [rowspec(width)] * 4 + [whole(w), part(weights, index, width, 0), whole(norms)],
        out_specs=[rowspec(width)] * 4
        + [rowspec(LANES), whole(side), whole(side), pl.BlockSpec((4, width), lambda i: (0, 0))],
        out_shape=[
            sds((total, width), bf16), sds((total, width), bf16), sds((total, width), bf16), sds((total, width), bf16),
            sds((total, LANES), f32), side, side, sds((4, width), f32),
        ],
        scratch_shapes=[pltpu.VMEM((width, blocks * width), f32), pltpu.VMEM((blocks * width, width), f32), pltpu.VMEM((width, width), f32)],
        name="ffn",
        **params(32, 50),
    )(core, *placed(r2, x, cot, o2, w, weights), norms)


def cross_backward_kernel(
    tile, block, half, items_ref, q2_ref, k2_ref, v2_ref, do_ref, l_ref, delta_ref, idr_ref, idk_ref, memory_ref, *rest
):
    dq_ref, dk_ref, dv_ref, grads_ref, q_all, ids_all, dq, dk, dv, grads = rest[-10:]
    step = pl.program_id(0)
    total, width = q2_ref.shape

    @pl.when(step == 0)
    def _():
        dq[...] = jnp.zeros_like(dq)
        dk[...] = jnp.zeros_like(dk)
        dv[...] = jnp.zeros_like(dv)
        grads[...] = jnp.zeros_like(grads)
        q_all[...] = q2_ref[...] * jnp.asarray(HD ** -0.5, bf16)
        for j in range(total // block):
            ids_all[j * block : (j + 1) * block, :] = column_of(idr_ref[:, j * block : (j + 1) * block])
        attend_back(
            items_ref, idk_ref, ids_all, q_all, do_ref, k2_ref, v2_ref, l_ref, delta_ref, dq, dk, dv, tile, block,
            2 * half * (width // LANES), 2 * half * (width // LANES), False,
        )

    memory = memory_ref[...]
    per = memory.shape[0]
    here = pl.ds(pl.multiple_of(step * per, per), per)
    for i, (ref, out_ref) in enumerate(((dk, dk_ref), (dv, dv_ref))):
        grad = ref[here, :].astype(bf16)
        out_ref[...] = grad
        grads[i] += mm(memory, grad, TN)
    rows = dq_ref.shape[0]
    dq_ref[...] = (dq[pl.ds(pl.multiple_of(step * rows, rows), rows), :] * HD ** -0.5).astype(bf16)

    @pl.when(step == pl.num_programs(0) - 1)
    def _():
        grads_ref[...] = grads[...].astype(bf16)


def cross_backward(items, q2, k2, v2, do, l, delta, idr, idk, memory, half, after, turns=4, block=QROWS, tile=256):
    total, width = q2.shape
    keys = k2.shape[0]
    columns = width // 2
    cols = lambda r: pl.BlockSpec((r, columns), lambda i, *_: (0, half))
    rowspec = lambda r, w: pl.BlockSpec((r, w), lambda i, *_: (i, 0))
    sds = out_array
    grad = jax.ShapeDtypeStruct((2, width, columns), bf16)
    return pl.pallas_call(
        functools.partial(cross_backward_kernel, tile, block, half),
        grid_spec=pltpu.PrefetchScalarGridSpec(
            num_scalar_prefetch=1,
            grid=(turns,),
            in_specs=[cols(total), cols(keys), cols(keys), cols(total)]
            + [whole(l), whole(delta), whole(idr), whole(idk), rowspec(keys // turns, width)] + [apart] * len(after),
            out_specs=[rowspec(total // turns, columns), rowspec(keys // turns, columns), rowspec(keys // turns, columns), whole(grad)],
            scratch_shapes=[
                pltpu.VMEM((total, columns), bf16), pltpu.VMEM((total, LANES), jnp.int32), pltpu.VMEM((total, columns), f32),
                pltpu.VMEM((keys, columns), f32), pltpu.VMEM((keys, columns), f32), pltpu.VMEM((2, width, columns), f32),
            ],
        ),
        out_shape=[sds((total, columns), bf16), sds((keys, columns), bf16), sds((keys, columns), bf16), grad],
        name="cross_backward",
        **params(12, 40),
    )(items, *placed(q2, k2, v2, do, l, delta), idr, idk, *placed(memory), *after)


def memory_grad_kernel(ka_ref, kb_ref, va_ref, vb_ref, wk_ref, wv_ref, *rest):
    half = ka_ref.shape[1]
    total = mm(ka_ref[...], wk_ref[0, :, :half], NT) + mm(kb_ref[...], wk_ref[0, :, half:], NT)
    total += mm(va_ref[...], wv_ref[0, :, :half], NT) + mm(vb_ref[...], wv_ref[0, :, half:], NT)
    rest[-1][...] = total.astype(bf16)


def memory_grad(ka, kb, va, vb, weights, index, after, rows=512):
    keys, width = ka.shape[0], weights.shape[2]
    rowspec = lambda w: pl.BlockSpec((rows, w), lambda i: (i, 0))
    return pl.pallas_call(
        memory_grad_kernel,
        grid=(keys // rows,),
        in_specs=[rowspec(width // 2)] * 4 + [part(weights, index, width, 0), part(weights, index + 1, width, 0)] + [apart] * len(after),
        out_specs=rowspec(width),
        out_shape=jax.ShapeDtypeStruct((keys, width), bf16),
        name="memory_grad",
        **params(4, 24),
    )(*placed(ka, kb, va, vb, weights, weights), *after)


def between_kernel(
    core_ref, ga_ref, gb_ref, gn23_ref, r1_ref, dr2_ref, dr3_ref, dqa_ref, dqb_ref, h1b_ref, oa_ref, ob_ref, wso_ref, wcq_ref, norms_ref, *rest
):
    dsum_ref, do1_ref, delta_ref, keep_ref, send_ref, gn_ref, total = rest[-7:]
    step = pl.program_id(0)

    @pl.when(step == 0)
    def _():
        total[...] = jnp.zeros_like(total)
        gn_ref[...] = jnp.zeros_like(gn_ref)

    dq2 = jnp.concatenate([dqa_ref[...], dqb_ref[...]], axis=1)
    dh1 = dr2_ref[...].astype(f32) + mm(dq2, wcq_ref[0], NT)
    n1, rstd1 = norm_rows(r1_ref[...].astype(f32))
    gn_ref[0:1, :] += column_sums(dh1 * n1)
    gn_ref[1:2, :] += column_sums(dh1)
    dr1 = norm_back(dh1, n1, rstd1, norms_ref[0:1, :])
    dsum_ref[...] = (dr1 + dr3_ref[...].astype(f32)).astype(bf16)
    da1 = dr1.astype(bf16)
    o1 = jnp.concatenate([oa_ref[...], ob_ref[...]], axis=1)
    do1 = mm(da1, wso_ref[0], NT).astype(bf16)
    do1_ref[...] = do1
    delta_ref[...] = head_columns(do1, o1)
    total[0] += mm(h1b_ref[...], dq2, TN)
    total[1] += mm(o1, da1, TN)

    @pl.when(step == pl.num_programs(0) - 1)
    def _():
        gn_ref[2:6, :] = gn23_ref[...]
        r, width = keep_ref.shape[2:]
        norm_part = jnp.concatenate([gn_ref[...], jnp.zeros((r - 8, width), f32)]).astype(bf16)

        def write(device, ref, j):
            here = pl.ds(pl.multiple_of(device * r, r), r)
            for i in range(2):
                ref[j, i, :, : width // 2] = ga_ref[i, here, :]
                ref[j, i, :, width // 2 :] = gb_ref[i, here, :]
                ref[j, 2 + i] = total[i, here, :].astype(bf16)
            ref[j, 4] = norm_part

        spread(keep_ref, send_ref, core_ref[0], write)


def between(core, pairs, ga, gb, gn23, r1, dr2, dr3, dqa, dqb, h1b, oa, ob, weights, norms, after, rows=256):
    total, width = r1.shape
    rowspec = lambda w: pl.BlockSpec((rows, w), lambda i: (i, 0))
    sds = out_array
    side = jax.ShapeDtypeStruct((pairs, 5, width // (2 * pairs), width), bf16)
    return pl.pallas_call(
        between_kernel,
        grid=(total // rows,),
        in_specs=[pl.BlockSpec(memory_space=pltpu.SMEM), whole(ga), whole(gb), whole(gn23)]
        + [rowspec(width)] * 3 + [rowspec(width // 2)] * 2 + [rowspec(width)] + [rowspec(width // 2)] * 2
        + [part(weights, 0, width, 0), part(weights, 1, width, 0), whole(norms)] + [apart] * len(after),
        out_specs=[rowspec(width)] * 2
        + [rowspec(LANES), whole(side), whole(side), pl.BlockSpec((8, width), lambda i: (0, 0))],
        out_shape=[sds((total, width), bf16), sds((total, width), bf16), sds((total, LANES), f32), side, side, sds((8, width), f32)],
        scratch_shapes=[pltpu.VMEM((2, width, width), f32)],
        name="between",
        **params(7, 32),
    )(core, ga, gb, gn23, *placed(r1, dr2, dr3, dqa, dqb, h1b, oa, ob, weights, weights), norms, *after)


def self_backward_kernel(
    tile, block, half, items_ref, q_ref, k_ref, v_ref, do_ref, l_ref, delta_ref, idr_ref, x_ref, wq_ref, wk_ref, wv_ref, sofar_ref, *rest
):
    if half:
        core_ref, before_ref = rest[:2]
        gx_ref, keep_ref, send_ref, q_all, ids_all, dq, dk, dv, grads = rest[-9:]
    else:
        gx_ref, grads_ref, q_all, ids_all, dq, dk, dv, grads = rest[-8:]
    step = pl.program_id(0)
    total, width = q_ref.shape

    @pl.when(step == 0)
    def _():
        dq[...] = jnp.zeros_like(dq)
        dk[...] = jnp.zeros_like(dk)
        dv[...] = jnp.zeros_like(dv)
        grads[...] = jnp.zeros_like(grads)
        q_all[...] = q_ref[...] * jnp.asarray(HD ** -0.5, bf16)
        for j in range(total // block):
            ids_all[j * block : (j + 1) * block, :] = column_of(idr_ref[:, j * block : (j + 1) * block])
        attend_back(
            items_ref, idr_ref, ids_all, q_all, do_ref, k_ref, v_ref, l_ref, delta_ref, dq, dk, dv, tile, block,
            0, 2 * half * (width // LANES), True,
        )

    x = x_ref[...]
    rows = x.shape[0]
    here = pl.ds(pl.multiple_of(step * rows, rows), rows)
    gx = sofar_ref[...].astype(f32)
    parts = (dq[here, :] * HD ** -0.5).astype(bf16), dk[here, :].astype(bf16), dv[here, :].astype(bf16)
    for i, (grad, w_ref) in enumerate(zip(parts, (wq_ref, wk_ref, wv_ref))):
        gx += mm(grad, w_ref[0], NT)
        grads[i] += mm(x, grad, TN)
    gx_ref[...] = gx.astype(bf16)

    @pl.when(step == pl.num_programs(0) - 1)
    def _():
        if not half:
            grads_ref[...] = grads[...].astype(bf16)
            return
        r = keep_ref.shape[2]

        def write(device, ref, j):
            place = pl.ds(pl.multiple_of(device * r, r), r)
            for i in range(3):
                ref[j, i, :, :width] = before_ref[i, place, :]
                ref[j, i, :, width:] = grads[i, place, :].astype(bf16)

        spread(keep_ref, send_ref, core_ref[0], write)


def self_backward(
    items, q, k, v, do, l, delta, idr, x, weights, sofar, half, after, core=None, before=None, pairs=1, turns=4, block=QROWS, tile=256
):
    total, width = x.shape
    columns = width // 2
    sds = out_array
    sides = [jax.ShapeDtypeStruct((pairs, 3, width // (2 * pairs), width), bf16)] * 2 if half else [jax.ShapeDtypeStruct((3, width, columns), bf16)]
    more = [core, before] if half else []
    rowspec = lambda w: pl.BlockSpec((total // turns, w), lambda i, *_: (i, 0))
    return pl.pallas_call(
        functools.partial(self_backward_kernel, tile, block, half),
        grid_spec=pltpu.PrefetchScalarGridSpec(
            num_scalar_prefetch=1,
            grid=(turns,),
            in_specs=[whole(q), whole(k), whole(v), pl.BlockSpec((total, columns), lambda i, *_: (0, half)), whole(l), whole(delta), whole(idr)]
            + [rowspec(width)] + [part(weights, i, columns, half) for i in range(3)] + [rowspec(width)]
            + ([pl.BlockSpec(memory_space=pltpu.SMEM), whole(before)] if half else []) + [apart] * len(after),
            out_specs=[rowspec(width)] + [whole(side) for side in sides],
            scratch_shapes=[
                pltpu.VMEM((total, columns), bf16), pltpu.VMEM((total, LANES), jnp.int32),
                pltpu.VMEM((total, columns), f32), pltpu.VMEM((total, columns), f32), pltpu.VMEM((total, columns), f32),
                pltpu.VMEM((3, width, columns), f32),
            ],
        ),
        out_shape=[sds((total, width), bf16)] + sides,
        name="self_backward",
        **params(10, 32),
    )(items, *placed(q, k, v, do, l, delta), idr, *placed(x, weights, weights, weights, sofar), *more, *after)


def add_split_kernel(count, here_ref, *refs):
    places = refs[0].shape[1]
    for m in range(places):
        at = here_ref[0] ^ m
        total = refs[0][:, at].astype(f32)
        for ref in refs[1:count]:
            total += ref[:, at].astype(f32)
        refs[count + m][...] = total.astype(bf16)


def add_split(here, parts, outer, places):
    tail = parts[0].shape[1:]
    parts = [p.reshape((outer, places) + tail) for p in parts]
    out = pl.pallas_call(
        functools.partial(add_split_kernel, len(parts)),
        grid=(outer,),
        in_specs=[pl.BlockSpec(memory_space=pltpu.SMEM)] + [pl.BlockSpec((1, places) + tail, lambda i: (i, 0, 0, 0, 0))] * len(parts),
        out_specs=[pl.BlockSpec((1,) + tail, lambda i: (i, 0, 0, 0))] * places,
        out_shape=[jax.ShapeDtypeStruct((outer,) + tail, bf16)] * places,
        name="add_split",
        **params(3, 24),
    )(here, *parts)
    return list(out)


def own_block(shape):
    return pl.BlockSpec(shape, lambda *_: (0,) * len(shape))


def pack_kernel(moves, count, *refs):
    ins, out_ref, wide = refs[:count], refs[count], refs[count + 1 :]
    rows = out_ref.shape[1]
    for ref, w in zip(ins, wide):
        w[...] = ref[...].astype(f32)
    for source, begin, step, square, block in moves:
        value = wide[source][pl.ds(begin, rows, stride=step), :]
        out_ref[square, :, block * LANES : (block + 1) * LANES] = value.astype(bf16)


def pack(arrays, moves, squares, rows, width, name):
    arrays = [a.reshape(-1, LANES) for a in arrays]
    return pl.pallas_call(
        functools.partial(pack_kernel, moves, len(arrays)),
        in_specs=[own_block(a.shape) for a in arrays],
        out_specs=own_block((squares, rows, width)),
        out_shape=jax.ShapeDtypeStruct((squares, rows, width), bf16),
        scratch_shapes=[pltpu.VMEM(a.shape, f32) for a in arrays],
        name=name,
        **params(1, 16),
    )(*arrays)


def square_moves(source, square, width):
    blocks = width // LANES
    return [(source, b, blocks, square, b) for b in range(blocks)]


def finish_kernel(moves, count, *refs):
    ins, outs = refs[:count], refs[count:]
    rows = ins[0].shape[1]
    for square, block, out, begin, step in moves:
        cols = slice(block * LANES, (block + 1) * LANES)
        total = ins[0][square, :, cols].astype(f32)
        for ref in ins[1:]:
            total += ref[square, :, cols].astype(f32)
        if step:
            outs[out][pl.ds(begin, rows, stride=step), :] = total
        else:
            outs[out][:, cols] = total


def finish(parts, moves, shapes, name):
    return pl.pallas_call(
        functools.partial(finish_kernel, moves, len(parts)),
        in_specs=[own_block(p.shape) for p in parts],
        out_specs=[own_block(s) for s in shapes],
        out_shape=[jax.ShapeDtypeStruct(s, f32) for s in shapes],
        name=name,
        **params(1, 16),
    )(*parts)


def segment_ids(lengths, row_count):
    ends = jnp.cumsum(lengths)
    places = jnp.arange(row_count, dtype=jnp.int32)
    return jnp.sum((places[:, None] >= ends[None, :]).astype(jnp.int32), axis=1)


def item_list(first, high, keys, block, tile):
    blocks = first.shape[0]
    count = (high - first * LANES + tile - 1) // tile
    upto = jnp.cumsum(count)
    most = blocks * (keys // tile)
    place = jnp.arange(most + FORWARD_ITEMS * BACKWARD_ITEMS, dtype=jnp.int32)
    passed = place[:, None] >= upto[None, :]
    which = jnp.minimum(jnp.sum(passed, axis=1), blocks - 1)
    skipped = jnp.sum(jnp.where(passed, count[None, :], 0), axis=1)
    mine = which[:, None] == jnp.arange(blocks)[None, :]
    begin = jnp.sum(jnp.where(mine, first[None, :], 0), axis=1) + (place - skipped) * (tile // LANES)
    begin = jnp.where(place < upto[-1], begin, keys // LANES)
    turns = [jnp.broadcast_to((upto[-1] + n - 1) // n, place.shape) for n in (FORWARD_ITEMS, BACKWARD_ITEMS)]
    return jnp.stack([which, begin] + turns).astype(jnp.int32)


def cross_items(seg, mem, total, keys, block=QROWS, tile=256):
    ends = jnp.cumsum(seg)
    starts = jnp.arange(0, total, block, dtype=jnp.int32)
    mem = mem[: seg.shape[0]]
    low = jnp.sum(jnp.where(starts[:, None] >= ends[None, :], mem[None, :], 0), axis=1)
    before = jnp.concatenate([jnp.zeros((1,), jnp.int32), ends[:-1].astype(jnp.int32)])
    high = jnp.sum(jnp.where((starts + block - 1)[:, None] >= before[None, :], mem[None, :], 0), axis=1)
    return item_list(low // LANES, high, keys, block, tile)


def self_items(seg, total, block=QROWS, tile=256):
    ends = jnp.cumsum(seg)
    starts = jnp.arange(0, total, block, dtype=jnp.int32)
    low = jnp.sum(jnp.where(starts[:, None] >= ends[None, :], seg[None, :], 0), axis=1)
    return item_list(low // LANES, starts + block, total, block, tile)


def mesh_size():
    return lax.axis_size("dp") * lax.axis_size("fsdp")


def position():
    return lax.axis_index("dp") * lax.axis_size("fsdp") + lax.axis_index("fsdp")


def bit_groups():
    count = mesh_size().bit_length() - 1
    groups = [(0, 1)]
    while groups[-1][0] + groups[-1][1] < count:
        low = groups[-1][0] + groups[-1][1]
        groups.append((low, min(2, count - low)))
    return groups


def swap(x, mask):
    return lax.ppermute(x, ("dp", "fsdp"), [(i, i ^ mask) for i in range(mesh_size())])


def place_in(group):
    return (position() >> group[0]) & ((1 << group[1]) - 1)


def tie(x, *after):
    return lax.optimization_barrier((x, *after))[0] if after else x


def gather_step(x, group, after=()):
    low, width = group
    here = place_in(group)
    blocks = [x] + tie([swap(x, m << low) for m in range(1, 1 << width)], *after)
    for j in range(width):
        flip = (here >> j) & 1 == 1
        blocks = [jnp.where(flip, blocks[p ^ (1 << j)], blocks[p]) for p in range(1 << width)]
    return jnp.stack(blocks, axis=x.ndim - 2)


def gathered(x):
    return x.reshape(x.shape[:1] + (-1, x.shape[-1]))


def swap_pieces(parts, group, after=()):
    return [parts[0]] + tie([swap(parts[m], m << group[0]) for m in range(1, len(parts))], *after)


def next_pieces(parts, groups, done):
    group = groups[done]
    outer = 1 << sum(g[1] for g in groups[done + 1 :])
    return add_split(place_in(group).reshape(1).astype(jnp.int32), parts, outer, 1 << group[1])


def norm_parts(norm_params, size):
    parts, left = [], norm_params
    for _ in range(3):
        part = left.astype(bf16)
        parts.append(jnp.pad(part, (0, LANES - part.size)))
        left = left - part.astype(f32)
    flat = jnp.concatenate(parts)
    return jnp.pad(flat, (0, size - flat.size))


def resplit(keep, send, devices, core, squares):
    halves = jnp.concatenate([keep, send])
    width = halves.shape[-1]
    first = halves[:, :squares].transpose(1, 0, 2, 3).reshape(squares, devices, -1, width).transpose(1, 0, 2, 3)
    rows = first.shape[2]
    if halves.shape[1] > squares:
        rest = halves[:, squares:].reshape(devices, halves.shape[1] - squares, rows, width)
        first = jnp.concatenate([first, rest], axis=1)
    both = first.reshape(devices // 2, 2, -1, rows, width)
    return [lax.dynamic_index_in_dim(both, core ^ m, 1, keepdims=False) for m in range(2)]


def body(
    inputs, memory, seg_lengths, mem_lengths, self_query, self_key, self_value, self_out,
    cross_query, cross_key, cross_value, cross_out, ffn_in, ffn_out, norm_params, cotangent,
):
    total, width = inputs.shape
    keys = memory.shape[0]
    devices = mesh_size()
    groups = bit_groups()
    down = groups[::-1]
    shard = norm_params.shape[0]
    size = self_query.shape[0]
    own_rows = size // width
    blocks = ffn_in.shape[0] // size
    whole_tiles = own_rows % 16 == 0
    core = place_in(groups[0]).reshape(1).astype(jnp.int32)

    firsts = (self_query, self_key, self_value)
    seconds = (self_out, cross_query, cross_out, cross_key, cross_value, norm_parts(norm_params, size))
    if whole_tiles:
        lane_blocks = width // LANES
        three = [m for i in range(3) for m in square_moves(i, i, width)]
        six = three + [m for i in range(3, 6) for m in square_moves(i, i, width)]
        wide = [(0, c * lane_blocks + b, blocks * lane_blocks, c, b) for c in range(blocks) for b in range(lane_blocks)]
        tall = [(1, j * own_rows * lane_blocks + b, lane_blocks, blocks + j, b) for j in range(blocks) for b in range(lane_blocks)]
        first = pack(firsts, three, 3, own_rows, width, "pack_self")
        second = pack(tie(seconds, first), six, 6, own_rows, width, "pack_cross")
        ffn_own = pack(tie((ffn_in, ffn_out), first), wide + tall, 2 * blocks, own_rows, width, "pack_ffn")
    else:
        first = jnp.concatenate(firsts).reshape(3, own_rows, width)
        second = jnp.concatenate(seconds).reshape(6, own_rows, width)
        fi = ffn_in.reshape(own_rows, blocks, width).transpose(1, 0, 2)
        ffn_own = jnp.concatenate([fi, ffn_out.reshape(blocks, own_rows, width)])
    for i, g in enumerate(down[:-1]):
        first = gather_step(first, g, [second] if i else [])
        if i < len(down) - 2:
            second = gather_step(second, g)
    early = second
    first = gathered(gather_step(first, down[-1]))
    ffn_all = lax.all_gather(ffn_own.reshape(-1, width), ("dp", "fsdp"), axis=0, tiled=True)
    ffn_all = ffn_all.reshape(devices, 2 * blocks, own_rows, width)
    if not whole_tiles:
        fi = ffn_all[:, :blocks].transpose(1, 0, 2, 3).reshape(1, blocks, width, width)
        ffn_all = jnp.concatenate([fi, ffn_all[:, blocks:].reshape(1, blocks, width, width)], axis=1)
    pairs = devices // 2 if whole_tiles else 1
    part_of = core if whole_tiles else jnp.zeros_like(core)

    qid, mid = segment_ids(seg_lengths[0], total)[None, :], segment_ids(mem_lengths[0], keys)[None, :]
    own_items = self_items(seg_lengths[0], total)
    items = cross_items(seg_lengths[0], mem_lengths[0], total, keys)

    qa, ka, va, oa, la = self_forward(own_items, inputs, first, qid, 0, [early])
    second = gather_step(second, down[-2], [la])
    qb, kb, vb, ob, lb = self_forward(own_items, inputs, first, qid, 1, [second])
    second = gathered(gather_step(second, down[-1], [lb]))
    norm_all = second[5].reshape(devices, -1)[:, : 3 * LANES].reshape(devices, 3, LANES)[:, :, :shard].astype(f32)
    norms = jnp.sum(norm_all, axis=1).reshape(6, width)
    k2, v2, r1, h1b, q2, o2, l2, r2 = cross_forward(items, memory, inputs, oa, ob, second, norms, qid, mid)
    out, dr3, dr2, do2, delta2, keep, send, gn23 = ffn(part_of, pairs, r2, inputs, cotangent, o2, ffn_all, second, 2, norms)

    one = [keep, send] if whole_tiles else resplit(keep, send, devices, core[0], blocks + 1)
    dq2a, dk2a, dv2a, gckva = cross_backward(items, q2, k2, v2, do2, l2, delta2, qid, mid, memory, 0, [one[1]])
    one = next_pieces(swap_pieces(one, groups[0], [dq2a]), groups, 1)
    dq2b, dk2b, dv2b, gckvb = cross_backward(items, q2, k2, v2, do2, l2, delta2, qid, mid, memory, 1, one[1:])
    dsum, do1, delta1, keep, send, gn = between(
        part_of, pairs, gckva, gckvb, gn23, r1, dr2, dr3, dq2a, dq2b, h1b, oa, ob, second, norms, []
    )
    two = [keep, send]
    if not whole_tiles:
        two = resplit(keep, send, devices, core[0], 5)
        own_norms = jnp.pad(gn[:6].astype(bf16).reshape(devices, -1), ((0, 0), (0, size - shard)))
        own_norms = own_norms.reshape(devices // 2, 2, own_rows, width)
        two = [two[m].at[:, 4].set(lax.dynamic_index_in_dim(own_norms, core[0] ^ m, 1, keepdims=False)) for m in range(2)]
    one = next_pieces(swap_pieces(one, groups[1], [do1]), groups, 2)
    gxa, gsa = self_backward(own_items, qa, ka, va, do1, la, delta1, qid, inputs, first, dsum, 0, one[1:] + [two[1]])
    two = next_pieces(swap_pieces(two, groups[0], [gsa]), groups, 1)
    gx, keep, send = self_backward(
        own_items, qb, kb, vb, do1, lb, delta1, qid, inputs, first, gxa, 1, two[1:], core=part_of, before=gsa, pairs=pairs
    )
    three = [keep, send] if whole_tiles else resplit(keep, send, devices, core[0], 3)
    three = next_pieces(swap_pieces(three, groups[0]), groups, 1)
    two = next_pieces(swap_pieces(two, groups[1], [three[1]]), groups, 2)
    gm = memory_grad(dk2a, dk2b, dv2a, dv2b, second, 3, two[1:])
    for i in range(2, len(groups)):
        three = next_pieces(swap_pieces(three, groups[i - 1]), groups, i)
        if i > 2:
            one = next_pieces(swap_pieces(one, groups[i - 1]), groups, i)
            two = next_pieces(swap_pieces(two, groups[i - 1]), groups, i)

    def flat(g):
        return g.reshape(-1)

    chains = [swap_pieces(one, groups[-1], [two[1]]), swap_pieces(two, groups[-1]), swap_pieces(three, groups[-1])]
    chains = [[p.reshape(-1, own_rows, width) for p in chain] for chain in chains]
    if whole_tiles:
        lane_rows = size // LANES
        square, long = (lane_rows, LANES), (blocks * lane_rows, LANES)

        moves = [(c, b, 0, c * lane_blocks + b, blocks * lane_blocks) for c in range(blocks) for b in range(lane_blocks)]
        moves += [(blocks, b, 1, b, lane_blocks) for b in range(lane_blocks)]
        moves += [
            (blocks + 1 + j, b, 2, j * own_rows * lane_blocks + b, lane_blocks) for j in range(blocks) for b in range(lane_blocks)
        ]
        gfi, gco, gfo = finish(chains[0], moves, [long, square, long], "finish_ffn")
        moves = [(i, b, i, b, lane_blocks) for i in range(4) for b in range(lane_blocks)] + [(4, b, 4, 0, 0) for b in range(lane_blocks)]
        gck, gcv, gcq, gso, gn = finish(chains[1], moves, [square] * 4 + [(own_rows, width)], "finish_cross")
        gn = lax.dynamic_slice_in_dim(flat(gn[:6]), position() * shard, shard)
        moves = [(i, b, i, b, lane_blocks) for i in range(3) for b in range(lane_blocks)]
        gsq, gsk, gsv = finish(chains[2], moves, [square] * 3, "finish_self")
    else:
        one, two, three = (sum(p.astype(f32) for p in chain) for chain in chains)
        gfi, gco, gfo = one[:blocks].transpose(1, 0, 2), one[blocks], one[blocks + 1 :]
        gck, gcv, gcq, gso, gn = two[0], two[1], two[2], two[3], flat(two[4])[:shard]
        gsq, gsk, gsv = three[0], three[1], three[2]
    return (out, gx, gm) + tuple(flat(g) for g in (gsq, gsk, gsv, gso, gcq, gck, gcv, gco, gfi, gfo, gn))


def solution(mesh):
    rows, flat = P(("dp", "fsdp"), None), P(("dp", "fsdp"))
    return jax.shard_map(
        body,
        mesh=mesh,
        in_specs=(rows,) * 4 + (flat,) * 11 + (rows,),
        out_specs=(rows,) * 3 + (flat,) * 11,
        check_vma=False,
    )
```

time: 302 us -> 259 us (0.86)
  local copies, waits for them, and re-layouts: 40.3 us -> 12.8 us
  Pallas kernels: 151 us -> 142 us
  starting transfers between devices: 46 us -> 42.1 us
    unnamed x137 -> x45, local copies, waits for them, and re-layouts: 29.1 us -> 6.91 us
    pallas_call x1, Pallas kernels: 34.1 us -> 26.9 us  [ffn(): pl.pallas_call(ffn_kernel, grid=(total // rows,), in_specs=[pl.BlockSpec(...]
    concatenate x12 -> x0, local copies, waits for them, and re-layouts: 6.65 us -> none  [the longest x7 3.73 us: body(): jnp.concatenate([self_out, cross_query, cross_out, cross_key, cross_value...]
    pallas_call x9 -> x13, Pallas kernels: 102 us -> 97.1 us  [the longest x2 31.7 us: cross_backward(): pl.pallas_call(functools.partial(cross_backward_kernel, tile, block, half...]
    ppermute x35, starting transfers between devices: 45.9 us -> 42.1 us  [swap(): lax.ppermute(x, ('dp', 'fsdp'), [(i, i ^ mask) for i in range(mesh_size())])]
    another operation x1 -> x2, local copies, waits for them, and re-layouts: 0.32 us -> 3.39 us  [gather_step(): return jnp.stack(blocks, axis=x.ndim - 2)]
    ppermute x35, waiting for transfers between devices: 43.5 us -> 40.4 us  [swap(): lax.ppermute(x, ('dp', 'fsdp'), [(i, i ^ mask) for i in range(mesh_size())])]
  transfers between devices with their start and end apart: 36 -> 36, of which waited for: 14 -> 13; matrix products, arithmetic and copies ran while one was open for 6% -> 4% of each run, Pallas kernels for 38% -> 39%
where the time goes in v3:
time: 259 us
  Pallas kernels  142 us (55%)
  starting transfers between devices  42.1 us (16%)
  waiting for transfers between devices  40.5 us (16%)
  between operations  17.3 us (7%)
  local copies, waits for them, and re-layouts  12.8 us (5%)
  other arithmetic  4.79 us (2%)
    ppermute x35, starting transfers between devices, swap(): lax.ppermute(x, ('dp', 'fsdp'), [(i, i ^ mask) for i in range(mesh_size())])  42.1 us
    ppermute x35, waiting for transfers between devices, swap(): lax.ppermute(x, ('dp', 'fsdp'), [(i, i ^ mask) for i in range(mesh_size())])  40.4 us
    pallas_call x2, Pallas kernels, cross_backward(): pl.pallas_call(functools.partial(cross_backward_kernel, tile, block, half...  31.7 us
    pallas_call x1, Pallas kernels, ffn(): pl.pallas_call(ffn_kernel, grid=(total // rows,), in_specs=[pl.BlockSpec(...  26.9 us
    pallas_call x2, Pallas kernels, self_backward(): pl.pallas_call(functools.partial(self_backward_kernel, tile, block, half)...  23.3 us
    pallas_call x1, Pallas kernels, cross_forward(): pl.pallas_call(functools.partial(cross_forward_kernel, tile, block), grid...  21.6 us
    pallas_call x2, Pallas kernels, self_forward(): pl.pallas_call(functools.partial(self_forward_kernel, tile, block), grid_...  17.7 us
    pallas_call x1, Pallas kernels, between(): pl.pallas_call(between_kernel, grid=(total // rows,), in_specs=[pl.BlockS...  8.75 us
  transfers between devices with their start and end apart: 36, of which 13 were waited for; matrix products, arithmetic and copies ran while one was open for 4% of the time, Pallas kernels for 39%

profile of v3, /device:TPU:0, one launch (start us, length us, event | category | flops | bytes accessed | tf_op | source)
XLA Modules:
  0.0 259.2 jit_solution(15741256684290837728)
XLA Ops:
  9.4 3.1 %collective-permute-start.8 = (bf16[3,16,512]{2,1,0:T(8,128)(2,1)S(1)}, bf16[3,16,512]{2,1,0:T(8,128)(2,1)S(1)}, u32[]{:S(2)}, u32[]{:S(2)}) collective-permute-start(bf16[3,16,512]{2,1,0:T(8,128)(2,1)S(1)} %pack_self.1), channel_id=1, source_target_pairs={{0,8},{1,9},{2,10},{3,11},{4,12},{5,13},{6,14},{7,15},{8,0},{9,1},... | collective-permute-start | bytes 147464 | tf_op jit(solution)/shard_map/ppermute | solution.py:864
  12.5 2.6 collective-permute-start.7
  15.3 1.0 collective-permute-start.2
  16.2 3.5 %collective-permute-start.1 = (bf16[6,16,512]{2,1,0:T(8,128)(2,1)S(1)}, bf16[6,16,512]{2,1,0:T(8,128)(2,1)S(1)}, u32[]{:S(2)}, u32[]{:S(2)}) collective-permute-start(bf16[6,16,512]{2,1,0:T(8,128)(2,1)S(1)} %pack_cross.1), channel_id=1, source_target_pairs={{0,16},{1,17},{2,18},{3,19},{4,20},{5,21},{6,22},{7,23},{8,24},{9,... | collective-permute-start | bytes 294920 | tf_op jit(solution)/shard_map/ppermute | solution.py:864
  19.7 0.7 pack_ffn.1
  26.2 2.6 collective-permute-start.11
  29.8 3.5 %collective-permute-done = bf16[6,16,512]{2,1,0:T(8,128)(2,1)S(1)} collective-permute-done((bf16[6,16,512]{2,1,0:T(8,128)(2,1)S(1)}, bf16[6,16,512]{2,1,0:T(8,128)(2,1)S(1)}, u32[]{:S(2)}, u32[]{:S(2)}) %collective-permute-start) | collective-permute-done | bytes 98336 | tf_op jit(solution)/shard_map/ppermute | solution.py:864
  33.3 2.4 collective-permute-done.11
  35.7 2.1 collective-permute-done.10
  39.3 1.7 collective-permute-start.5
  41.0 1.3 collective-permute-start.4
  43.1 1.3 copy.55
  44.4 8.8 %self_forward.2 = (bf16[1024,256]{1,0:T(8,128)(2,1)}, bf16[1024,256]{1,0:T(8,128)(2,1)}, bf16[1024,256]{1,0:T(8,128)(2,1)}, bf16[1024,256]{1,0:T(8,128)(2,1)}, f32[1024,128]{1,0:T(8,128)}) custom-call(s32[4,38]{1,0:T(4,128)S(1)} %add_add_fusion.1.items_ref, bf16[1024,512]{1,0:T(8,128)(2,1)} %x_ref.11, bf16[3,512,512]{2,1,0:T(8,128)(2,1)} %bitcast.239, ...), custom_call_target="tpu_custom_call" | custom-call | flops 6000000000 | bytes 1048576 | tf_op jit(solution)/shard_map/self_forward/pallas_call | solution.py:245
  53.2 1.0 collective-permute-done.5
  54.3 7.7 %collective-permute-done.4 = bf16[6,4,16,512]{3,2,1,0:T(8,128)(2,1)S(1)} collective-permute-done((bf16[6,4,16,512]{3,2,1,0:T(8,128)(2,1)S(1)}, bf16[6,4,16,512]{3,2,1,0:T(8,128)(2,1)S(1)}, u32[]{:S(2)}, u32[]{:S(2)}) %collective-permute-start.4) | collective-permute-done | bytes 393248 | tf_op jit(solution)/shard_map/ppermute | solution.py:864
  62.0 1.8 collective-permute-done.3
  65.4 8.9 %self_forward.3 = (bf16[1024,256]{1,0:T(8,128)(2,1)}, bf16[1024,256]{1,0:T(8,128)(2,1)}, bf16[1024,256]{1,0:T(8,128)(2,1)}, bf16[1024,256]{1,0:T(8,128)(2,1)}, f32[1024,128]{1,0:T(8,128)}) custom-call(s32[4,38]{1,0:T(4,128)S(1)} %add_add_fusion.1.items_ref, bf16[1024,512]{1,0:T(8,128)(2,1)} %x_ref.11, bf16[3,512,512]{2,1,0:T(8,128)(2,1)} %bitcast.242, ...), custom_call_target="tpu_custom_call" | custom-call | flops 6000000000 | bytes 1048576 | tf_op jit(solution)/shard_map/self_forward/pallas_call | solution.py:245
  74.9 2.1 copy.59
  77.6 21.6 %cross_forward.1 = (bf16[2048,512]{1,0:T(8,128)(2,1)}, bf16[2048,512]{1,0:T(8,128)(2,1)}, bf16[1024,512]{1,0:T(8,128)(2,1)}, bf16[1024,512]{1,0:T(8,128)(2,1)}, ...) custom-call(s32[4,70]{1,0:T(4,128)S(1)} %add_add_fusion.items_ref, ...), custom_call_target="tpu_custom_call" | custom-call | flops 24000000000 | bytes 1048576 | tf_op jit(solution)/shard_map/cross_forward/pallas_call | solution.py:324
  99.2 26.9 %ffn.1 = (bf16[1024,512]{1,0:T(8,128)(2,1)}, bf16[1024,512]{1,0:T(8,128)(2,1)}, bf16[1024,512]{1,0:T(8,128)(2,1)}, bf16[1024,512]{1,0:T(8,128)(2,1)}, f32[1024,1...) custom-call(s32[1]{0:T(128)} %bitcast.core_ref.rest_0_, ...), custom_call_target="tpu_custom_call" | custom-call | flops 32000000000 | bytes 1048576 | tf_op jit(solution)/shard_map/ffn/pallas_call | solution.py:481
  126.3 1.7 copy-done
  128.0 16.0 %cross_backward.2 = (bf16[1024,256]{1,0:T(8,128)(2,1)}, bf16[2048,256]{1,0:T(8,128)(2,1)}, bf16[2048,256]{1,0:T(8,128)(2,1)}, bf16[2,512,256]{2,1,0:T(8,128)(2,1)S(1)}) custom-call(s32[4,70]{1,0:T(4,128)S(1)} %add_add_fusion.items_ref, bf16[1024,512]{1,0:T(8,128)(2,1)} %get-tuple-element.144.q2_ref, bf16[2048,512]{1,0:T(8,128)(2,1)} %get-tuple-element.145.k2_ref, ...), custom_call_target="tpu_custom_call" | custom-call | flops 12000000000 | bytes 1048576 | tf_op jit(solution)/shard_map/cross_backward/pallas_call | solution.py:541
  144.6 3.9 %collective-permute-start.15 = (bf16[4,9,16,512]{3,2,1,0:T(8,128)(2,1)S(1)}, bf16[4,9,16,512]{3,2,1,0:T(8,128)(2,1)S(1)}, u32[]{:S(2)}, u32[]{:S(2)}) collective-permute-start(bf16[4,9,16,512]{3,2,1,0:T(8,128)(2,1)S(1)} %get-tuple-element.155.rest_0_), channel_id=1, source_target_pairs={{0,2},{1,3},{2,0},{3,1},{4,6},{5,7},{6,4},{7,5},{8,10},{9,11},{10,... | collective-permute-start | bytes 1769480 | tf_op jit(solution)/shard_map/ppermute | solution.py:864
  148.6 15.7 %cross_backward.3 = (bf16[1024,256]{1,0:T(8,128)(2,1)}, bf16[2048,256]{1,0:T(8,128)(2,1)}, bf16[2048,256]{1,0:T(8,128)(2,1)}, bf16[2,512,256]{2,1,0:T(8,128)(2,1)S(1)}) custom-call(s32[4,70]{1,0:T(4,128)S(1)} %add_add_fusion.items_ref, bf16[1024,512]{1,0:T(8,128)(2,1)} %get-tuple-element.144.q2_ref, bf16[2048,512]{1,0:T(8,128)(2,1)} %get-tuple-element.145.k2_ref, ...), custom_call_target="tpu_custom_call" | custom-call | flops 12000000000 | bytes 1048576 | tf_op jit(solution)/shard_map/cross_backward/pallas_call | solution.py:541
  164.4 8.7 %between.1 = (bf16[1024,512]{1,0:T(8,128)(2,1)}, bf16[1024,512]{1,0:T(8,128)(2,1)}, f32[1024,128]{1,0:T(8,128)}, bf16[16,5,16,512]{3,2,1,0:T(8,128)(2,1)S(1)}, b...) custom-call(s32[1]{0:T(128)} %bitcast.core_ref.rest_0_, bf16[2,512,256]{2,1,0:T(8,128)(2,1)S(1)} %get-tuple-element.151.ga_ref, ...), custom_call_target="tpu_custom_call" | custom-call | flops 7000000000 | bytes 1048576 | tf_op jit(solution)/shard_map/between/pallas_call | solution.py:629
  173.2 1.1 collective-permute-start.18
  174.3 6.9 %collective-permute-done.17 = bf16[4,9,16,512]{3,2,1,0:T(8,128)(2,1)S(1)} collective-permute-done((bf16[4,9,16,512]{3,2,1,0:T(8,128)(2,1)S(1)}, bf16[4,9,16,512]{3,2,1,0:T(8,128)(2,1)S(1)}, u32[]{:S(2)}, u32[]{:S(2)}) %collective-permute-start.17) | collective-permute-done | bytes 589856 | tf_op jit(solution)/shard_map/ppermute | solution.py:864
  181.5 11.3 %self_backward.2 = (bf16[1024,512]{1,0:T(8,128)(2,1)}, bf16[3,512,256]{2,1,0:T(8,128)(2,1)S(1)}) custom-call(s32[4,38]{1,0:T(4,128)S(1)} %add_add_fusion.1.items_ref, bf16[1024,256]{1,0:T(8,128)(2,1)} %get-tuple-element.167.q_ref, bf16[1024,256]{1,0:T(8,128)(2,1)} %get-tuple-element.168.k_ref, bf16[1024,256]{1,0:T(8,128)(2,1)} %get-tuple-element.169.v_ref, ...), custom_call_target="tpu_custom_call" | custom-call | flops 10000000000 | bytes 1048576 | tf_op jit(solution)/shard_map/self_backward/pallas_call | solution.py:704
  194.0 12.0 %self_backward.3 = (bf16[1024,512]{1,0:T(8,128)(2,1)}, bf16[16,3,16,512]{3,2,1,0:T(8,128)(2,1)S(1)}, bf16[16,3,16,512]{3,2,1,0:T(8,128)(2,1)S(1)}) custom-call(s32[4,38]{1,0:T(4,128)S(1)} %add_add_fusion.1.items_ref, bf16[1024,256]{1,0:T(8,128)(2,1)} %get-tuple-element.141.q_ref, bf16[1024,256]{1,0:T(8,128)(2,1)} %get-tuple-element.142.k_ref, ...), custom_call_target="tpu_custom_call" | custom-call | flops 10000000000 | bytes 1048576 | tf_op jit(solution)/shard_map/self_backward/pallas_call | solution.py:704
  205.9 0.9 copy-done.12
  206.9 2.9 %collective-permute-start.19 = (bf16[4,5,16,512]{3,2,1,0:T(8,128)(2,1)S(1)}, bf16[4,5,16,512]{3,2,1,0:T(8,128)(2,1)S(1)}, u32[]{:S(2)}, u32[]{:S(2)}) collective-permute-start(bf16[4,5,16,512]{3,2,1,0:T(8,128)(2,1)S(1)} %get-tuple-element.183.rest_2_), channel_id=1, source_target_pairs={{0,2},{1,3},{2,0},{3,1},{4,6},{5,7},{6,4},{7,5},{8,10},{9,11},{10,... | collective-permute-start | bytes 983048 | tf_op jit(solution)/shard_map/ppermute | solution.py:864
  209.8 1.9 collective-permute-start.20
  211.7 1.5 collective-permute-start.21
  213.5 1.1 copy-done.13
  214.9 3.4 %collective-permute-done.19 = bf16[4,5,16,512]{3,2,1,0:T(8,128)(2,1)S(1)} collective-permute-done((bf16[4,5,16,512]{3,2,1,0:T(8,128)(2,1)S(1)}, bf16[4,5,16,512]{3,2,1,0:T(8,128)(2,1)S(1)}, u32[]{:S(2)}, u32[]{:S(2)}) %collective-permute-start.19) | collective-permute-done | bytes 327712 | tf_op jit(solution)/shard_map/ppermute | solution.py:864
  218.3 1.6 collective-permute-start.34
  219.9 6.0 %collective-permute-done.20 = bf16[4,5,16,512]{3,2,1,0:T(8,128)(2,1)S(1)} collective-permute-done((bf16[4,5,16,512]{3,2,1,0:T(8,128)(2,1)S(1)}, bf16[4,5,16,512]{3,2,1,0:T(8,128)(2,1)S(1)}, u32[]{:S(2)}, u32[]{:S(2)}) %collective-permute-start.20) | collective-permute-done | bytes 327712 | tf_op jit(solution)/shard_map/ppermute | solution.py:864
  225.9 2.5 collective-permute-start.23
  228.4 1.7 collective-permute-start.24
  230.1 1.1 add_split.10
  231.4 6.2 %memory_grad.1 = bf16[2048,512]{1,0:T(8,128)(2,1)} custom-call(bf16[2048,256]{1,0:T(8,128)(2,1)} %get-tuple-element.187.ka_ref, bf16[2048,256]{1,0:T(8,128)(2,1)} %get-tuple-element.188.kb_ref, bf16[2048,256]{1,0:T(8,128)(2,1)} %get-tuple-element.189.va_ref, bf16[2048,256]{1,0:T(8,128)(2,1)} %get-tuple-element.190.vb_ref, bf16[6,512,512]{2,1,0:T(8,128)(2,1)} %bitcast.236, ...), custom_call_target="tpu_custom_call" | custom-call | flops 4000000000 | bytes 1048576 | tf_op jit(solution)/shard_map/memory_grad/pallas_call | solution.py:570
  237.6 1.7 collective-permute-start.31
  239.4 0.8 finish_ffn.1
  240.1 1.7 collective-permute-start.29
  242.3 1.5 collective-permute-start.27
  243.8 2.1 collective-permute-done.30
  245.9 1.3 collective-permute-start.28
  248.9 2.9 %collective-permute-done.28 = bf16[1,3,16,512]{3,2,1,0:T(8,128)(2,1)S(1)} collective-permute-done((bf16[1,3,16,512]{3,2,1,0:T(8,128)(2,1)S(1)}, bf16[1,3,16,512]{3,2,1,0:T(8,128)(2,1)S(1)}, u32[]{:S(2)}, u32[]{:S(2)}) %collective-permute-start.28) | collective-permute-done | bytes 49184 | tf_op jit(solution)/shard_map/ppermute | solution.py:864
  (154 shorter events, 17.2 us)
Async XLA Ops:
  7.2 92.0 %all-gather.2.cloned.1.call-start = ((), (), s32[]{:S(2)}) async-start(), calls=%async_computation | async-start | bytes 4325376 | tf_op jit(solution)/shard_map/all_gather | solution.py:959
  9.4 5.7 %copy-start.21 = (f32[96]{0:T(128)S(1)}, f32[96]{0:T(128)}, u32[]{:S(2)}) copy-start(f32[96]{0:T(128)} %param.30) | copy-start | bytes 1156
  9.4 5.8 %copy-start.7 = (bf16[8192]{0:T(1024)(128)(2,1)S(1)}, bf16[8192]{0:T(1024)(128)(2,1)}, u32[]{:S(2)}) copy-start(bf16[8192]{0:T(1024)(128)(2,1)} %param.23) | copy-start | bytes 49156
  9.4 5.8 %copy-start.8 = (bf16[8192]{0:T(1024)(128)(2,1)S(1)}, bf16[8192]{0:T(1024)(128)(2,1)}, u32[]{:S(2)}) copy-start(bf16[8192]{0:T(1024)(128)(2,1)} %param.24) | copy-start | bytes 49156
  9.4 5.8 %copy-start.9 = (bf16[8192]{0:T(1024)(128)(2,1)S(1)}, bf16[8192]{0:T(1024)(128)(2,1)}, u32[]{:S(2)}) copy-start(bf16[8192]{0:T(1024)(128)(2,1)} %param.27) | copy-start | bytes 49156
  9.4 5.8 %copy-start.10 = (bf16[8192]{0:T(1024)(128)(2,1)S(1)}, bf16[8192]{0:T(1024)(128)(2,1)}, u32[]{:S(2)}) copy-start(bf16[8192]{0:T(1024)(128)(2,1)} %param.25) | copy-start | bytes 49156
  9.4 5.8 %copy-start.11 = (bf16[8192]{0:T(1024)(128)(2,1)S(1)}, bf16[8192]{0:T(1024)(128)(2,1)}, u32[]{:S(2)}) copy-start(bf16[8192]{0:T(1024)(128)(2,1)} %param.26) | copy-start | bytes 49156
  9.4 16.5 %collective-permute-start.8 = (bf16[3,16,512]{2,1,0:T(8,128)(2,1)S(1)}, bf16[3,16,512]{2,1,0:T(8,128)(2,1)S(1)}, u32[]{:S(2)}, u32[]{:S(2)}) collective-permute-start(bf16[3,16,512]{2,1,0:T(8,128)(2,1)S(1)} %pack_self.1), channel_id=1, source_target_pairs={{0,8},{1,9},{2,10},{3,11},{4,12},{5,13},{6,14},{7,15},{8,0},{9,1},... | collective-permute-start | bytes 147464 | tf_op jit(solution)/shard_map/ppermute | solution.py:864
  12.5 13.6 %collective-permute-start.7 = (bf16[3,16,512]{2,1,0:T(8,128)(2,1)S(1)}, bf16[3,16,512]{2,1,0:T(8,128)(2,1)S(1)}, u32[]{:S(2)}, u32[]{:S(2)}) collective-permute-start(bf16[3,16,512]{2,1,0:T(8,128)(2,1)S(1)} %pack_self.1), channel_id=1, source_target_pairs={{0,16},{1,17},{2,18},{3,19},{4,20},{5,21},{6,22},{7,23},{8,24},{9,... | collective-permute-start | bytes 147464 | tf_op jit(solution)/shard_map/ppermute | solution.py:864
  15.1 11.0 %collective-permute-start.6 = (bf16[3,16,512]{2,1,0:T(8,128)(2,1)S(1)}, bf16[3,16,512]{2,1,0:T(8,128)(2,1)S(1)}, u32[]{:S(2)}, u32[]{:S(2)}) collective-permute-start(bf16[3,16,512]{2,1,0:T(8,128)(2,1)S(1)} %pack_self.1), channel_id=1, source_target_pairs={{0,24},{1,25},{2,26},{3,27},{4,28},{5,29},{6,30},{7,31},{8,16},{9,... | collective-permute-start | bytes 147464 | tf_op jit(solution)/shard_map/ppermute | solution.py:864
  15.2 4.5 %copy-start.2 = (bf16[32768]{0:T(1024)(128)(2,1)S(1)}, bf16[32768]{0:T(1024)(128)(2,1)}, u32[]{:S(2)}) copy-start(bf16[32768]{0:T(1024)(128)(2,1)} %param.28) | copy-start | bytes 196612
  15.3 14.0 %collective-permute-start.2 = (bf16[6,16,512]{2,1,0:T(8,128)(2,1)S(1)}, bf16[6,16,512]{2,1,0:T(8,128)(2,1)S(1)}, u32[]{:S(2)}, u32[]{:S(2)}) collective-permute-start(bf16[6,16,512]{2,1,0:T(8,128)(2,1)S(1)} %pack_cross.1), channel_id=1, source_target_pairs={{0,8},{1,9},{2,10},{3,11},{4,12},{5,13},{6,14},{7,15},{8,0},{9,1},... | collective-permute-start | bytes 294920 | tf_op jit(solution)/shard_map/ppermute | solution.py:864
  16.2 13.5 %collective-permute-start.1 = (bf16[6,16,512]{2,1,0:T(8,128)(2,1)S(1)}, bf16[6,16,512]{2,1,0:T(8,128)(2,1)S(1)}, u32[]{:S(2)}, u32[]{:S(2)}) collective-permute-start(bf16[6,16,512]{2,1,0:T(8,128)(2,1)S(1)} %pack_cross.1), channel_id=1, source_target_pairs={{0,16},{1,17},{2,18},{3,19},{4,20},{5,21},{6,22},{7,23},{8,24},{9,... | collective-permute-start | bytes 294920 | tf_op jit(solution)/shard_map/ppermute | solution.py:864
  25.9 7.3 %collective-permute-start = (bf16[6,16,512]{2,1,0:T(8,128)(2,1)S(1)}, bf16[6,16,512]{2,1,0:T(8,128)(2,1)S(1)}, u32[]{:S(2)}, u32[]{:S(2)}) collective-permute-start(bf16[6,16,512]{2,1,0:T(8,128)(2,1)S(1)} %pack_cross.1), channel_id=1, source_target_pairs={{0,24},{1,25},{2,26},{3,27},{4,28},{5,29},{6,30},{7,31},{8,16},{9,... | collective-permute-start | bytes 294920 | tf_op jit(solution)/shard_map/ppermute | solution.py:864
  26.2 9.5 %collective-permute-start.11 = (bf16[3,4,16,512]{3,2,0,1:T(8,128)(2,1)S(1)}, bf16[3,4,16,512]{3,2,0,1:T(8,128)(2,1)S(1)}, u32[]{:S(2)}, u32[]{:S(2)}) collective-permute-start(bf16[3,4,16,512]{3,2,0,1:T(8,128)(2,1)S(1)} %pad_maximum_fusion.5), channel_id=1, source_target_pairs={{0,6},{1,7},{2,4},{3,5},{4,2},{5,3},{6,0},{7,1},{8,14},{9,15},{10,... | collective-permute-start | bytes 589832 | tf_op jit(solution)/shard_map/ppermute | solution.py:864
  28.8 9.1 %collective-permute-start.10 = (bf16[3,4,16,512]{3,2,0,1:T(8,128)(2,1)S(1)}, bf16[3,4,16,512]{3,2,0,1:T(8,128)(2,1)S(1)}, u32[]{:S(2)}, u32[]{:S(2)}) collective-permute-start(bf16[3,4,16,512]{3,2,0,1:T(8,128)(2,1)S(1)} %pad_maximum_fusion.5), channel_id=1, source_target_pairs={{0,4},{1,5},{2,6},{3,7},{4,0},{5,1},{6,2},{7,3},{8,12},{9,13},{10,... | collective-permute-start | bytes 589832 | tf_op jit(solution)/shard_map/ppermute | solution.py:864
  29.3 8.6 %collective-permute-start.9 = (bf16[3,4,16,512]{3,2,0,1:T(8,128)(2,1)S(1)}, bf16[3,4,16,512]{3,2,0,1:T(8,128)(2,1)S(1)}, u32[]{:S(2)}, u32[]{:S(2)}) collective-permute-start(bf16[3,4,16,512]{3,2,0,1:T(8,128)(2,1)S(1)} %pad_maximum_fusion.5), channel_id=1, source_target_pairs={{0,2},{1,3},{2,0},{3,1},{4,6},{5,7},{6,4},{7,5},{8,10},{9,11},{10,... | collective-permute-start | bytes 589832 | tf_op jit(solution)/shard_map/ppermute | solution.py:864
  38.1 4.7 %collective-permute-start.12 = (bf16[3,4,4,16,512]{4,3,0,1,2:T(8,128)(2,1)S(1)}, bf16[3,4,4,16,512]{4,3,0,1,2:T(8,128)(2,1)S(1)}, u32[]{:S(2)}, u32[]{:S(2)}) collective-permute-start(bf16[3,4,4,16,512]{4,3,0,1,2:T(8,128)(2,1)S(1)} %pad_maximum_fusion.3), channel_id=1, source_target_pairs={{0,1},{1,0},{2,3},{3,2},{4,5},{5,4},{6,7},{7,6},{8,9},{9,8},{10,11... | collective-permute-start | bytes 2359304 | tf_op jit(solution)/shard_map/ppermute | solution.py:864
  39.3 15.0 %collective-permute-start.5 = (bf16[6,4,16,512]{3,2,1,0:T(8,128)(2,1)S(1)}, bf16[6,4,16,512]{3,2,1,0:T(8,128)(2,1)S(1)}, u32[]{:S(2)}, u32[]{:S(2)}) collective-permute-start(bf16[6,4,16,512]{3,2,1,0:T(8,128)(2,1)S(1)} %pad_maximum_fusion.4.rest_0_), channel_id=1, source_target_pairs={{0,6},{1,7},{2,4},{3,5},{4,2},{5,3},{6,0},{7,1},{8,14},{9,15},{10,... | collective-permute-start | bytes 1179656 | tf_op jit(solution)/shard_map/ppermute | solution.py:864
  41.0 21.0 %collective-permute-start.4 = (bf16[6,4,16,512]{3,2,1,0:T(8,128)(2,1)S(1)}, bf16[6,4,16,512]{3,2,1,0:T(8,128)(2,1)S(1)}, u32[]{:S(2)}, u32[]{:S(2)}) collective-permute-start(bf16[6,4,16,512]{3,2,1,0:T(8,128)(2,1)S(1)} %pad_maximum_fusion.4.rest_0_), channel_id=1, source_target_pairs={{0,4},{1,5},{2,6},{3,7},{4,0},{5,1},{6,2},{7,3},{8,12},{9,13},{10,... | collective-permute-start | bytes 1179656 | tf_op jit(solution)/shard_map/ppermute | solution.py:864
  42.3 21.6 %collective-permute-start.3 = (bf16[6,4,16,512]{3,2,1,0:T(8,128)(2,1)S(1)}, bf16[6,4,16,512]{3,2,1,0:T(8,128)(2,1)S(1)}, u32[]{:S(2)}, u32[]{:S(2)}) collective-permute-start(bf16[6,4,16,512]{3,2,1,0:T(8,128)(2,1)S(1)} %pad_maximum_fusion.4.rest_0_), channel_id=1, source_target_pairs={{0,2},{1,3},{2,0},{3,1},{4,6},{5,7},{6,4},{7,5},{8,10},{9,11},{10,... | collective-permute-start | bytes 1179656 | tf_op jit(solution)/shard_map/ppermute | solution.py:864
  64.3 10.0 %collective-permute-start.13 = (bf16[6,4,4,16,512]{4,3,2,1,0:T(8,128)(2,1)S(1)}, bf16[6,4,4,16,512]{4,3,2,1,0:T(8,128)(2,1)S(1)}, u32[]{:S(2)}, u32[]{:S(2)}) collective-permute-start(bf16[6,4,4,16,512]{4,3,2,1,0:T(8,128)(2,1)S(1)} %pad_maximum_fusion.2.rest_0_), channel_id=1, source_target_pairs={{0,1},{1,0},{2,3},{3,2},{4,5},{5,4},{6,7},{7,6},{8,9},{9,8},{10,11... | collective-permute-start | bytes 4718600 | tf_op jit(solution)/shard_map/ppermute | solution.py:864
  126.2 17.8 %collective-permute-start.14 = (bf16[16,9,16,512]{3,2,1,0:T(8,128)(2,1)}, bf16[16,9,16,512]{3,2,1,0:T(8,128)(2,1)S(1)}, u32[]{:S(2)}, u32[]{:S(2)}) collective-permute-start(bf16[16,9,16,512]{3,2,1,0:T(8,128)(2,1)} %get-tuple-element.150.rest_0_), channel_id=1, source_target_pairs={{0,1},{1,0},{2,3},{3,2},{4,5},{5,4},{6,7},{7,6},{8,9},{9,8},{10,11... | collective-permute-start | bytes 7077896 | tf_op jit(solution)/shard_map/ppermute | solution.py:864
  144.6 29.7 %collective-permute-start.15 = (bf16[4,9,16,512]{3,2,1,0:T(8,128)(2,1)S(1)}, bf16[4,9,16,512]{3,2,1,0:T(8,128)(2,1)S(1)}, u32[]{:S(2)}, u32[]{:S(2)}) collective-permute-start(bf16[4,9,16,512]{3,2,1,0:T(8,128)(2,1)S(1)} %get-tuple-element.155.rest_0_), channel_id=1, source_target_pairs={{0,2},{1,3},{2,0},{3,1},{4,6},{5,7},{6,4},{7,5},{8,10},{9,11},{10,... | collective-permute-start | bytes 1769480 | tf_op jit(solution)/shard_map/ppermute | solution.py:864
  148.6 25.7 %collective-permute-start.16 = (bf16[4,9,16,512]{3,2,1,0:T(8,128)(2,1)S(1)}, bf16[4,9,16,512]{3,2,1,0:T(8,128)(2,1)S(1)}, u32[]{:S(2)}, u32[]{:S(2)}) collective-permute-start(bf16[4,9,16,512]{3,2,1,0:T(8,128)(2,1)S(1)} %get-tuple-element.156.rest_1_), channel_id=1, source_target_pairs={{0,4},{1,5},{2,6},{3,7},{4,0},{5,1},{6,2},{7,3},{8,12},{9,13},{10,... | collective-permute-start | bytes 1769480 | tf_op jit(solution)/shard_map/ppermute | solution.py:864
  148.6 15.8 %copy-start.18 = (f32[4,512]{1,0:T(4,128)S(1)}, f32[4,512]{1,0:T(4,128)}, u32[]{:S(2)}) copy-start(f32[4,512]{1,0:T(4,128)} %get-tuple-element.159.gn23_ref) | copy-start | bytes 24580
  164.3 16.9 %collective-permute-start.17 = (bf16[4,9,16,512]{3,2,1,0:T(8,128)(2,1)S(1)}, bf16[4,9,16,512]{3,2,1,0:T(8,128)(2,1)S(1)}, u32[]{:S(2)}, u32[]{:S(2)}) collective-permute-start(bf16[4,9,16,512]{3,2,1,0:T(8,128)(2,1)S(1)} %get-tuple-element.157.rest_2_), channel_id=1, source_target_pairs={{0,6},{1,7},{2,4},{3,5},{4,2},{5,3},{6,0},{7,1},{8,14},{9,15},{10,... | collective-permute-start | bytes 1769480 | tf_op jit(solution)/shard_map/ppermute | solution.py:864
  173.2 19.7 %collective-permute-start.18 = (bf16[16,5,16,512]{3,2,1,0:T(8,128)(2,1)S(1)}, bf16[16,5,16,512]{3,2,1,0:T(8,128)(2,1)S(1)}, u32[]{:S(2)}, u32[]{:S(2)}) collective-permute-start(bf16[16,5,16,512]{3,2,1,0:T(8,128)(2,1)S(1)} %get-tuple-element.178.rest_3_), channel_id=1, source_target_pairs={{0,1},{1,0},{2,3},{3,2},{4,5},{5,4},{6,7},{7,6},{8,9},{9,8},{10,11... | collective-permute-start | bytes 3932168 | tf_op jit(solution)/shard_map/ppermute | solution.py:864
  181.5 11.3 %copy-start.1 = (bf16[1,9,16,512]{3,2,1,0:T(8,128)(2,1)}, bf16[1,9,16,512]{3,2,1,0:T(8,128)(2,1)S(1)}, u32[]{:S(2)}) copy-start(bf16[1,9,16,512]{3,2,1,0:T(8,128)(2,1)S(1)} %get-tuple-element.175.rest_0_) | copy-start | bytes 442372
  181.5 11.3 %copy-start.16 = (bf16[1,9,16,512]{3,2,1,0:T(8,128)(2,1)}, bf16[1,9,16,512]{3,2,1,0:T(8,128)(2,1)S(1)}, u32[]{:S(2)}) copy-start(bf16[1,9,16,512]{3,2,1,0:T(8,128)(2,1)S(1)} %get-tuple-element.216) | copy-start | bytes 442372
  206.8 6.4 %collective-permute-start.22 = (bf16[16,3,16,512]{3,2,1,0:T(8,128)(2,1)S(1)}, bf16[16,3,16,512]{3,2,1,0:T(8,128)(2,1)S(1)}, u32[]{:S(2)}, u32[]{:S(2)}) collective-permute-start(bf16[16,3,16,512]{3,2,1,0:T(8,128)(2,1)S(1)} %get-tuple-element.193), channel_id=1, source_target_pairs={{0,1},{1,0},{2,3},{3,2},{4,5},{5,4},{6,7},{7,6},{8,9},{9,8},{10,11... | collective-permute-start | bytes 2359304 | tf_op jit(solution)/shard_map/ppermute | solution.py:864
  206.9 11.4 %collective-permute-start.19 = (bf16[4,5,16,512]{3,2,1,0:T(8,128)(2,1)S(1)}, bf16[4,5,16,512]{3,2,1,0:T(8,128)(2,1)S(1)}, u32[]{:S(2)}, u32[]{:S(2)}) collective-permute-start(bf16[4,5,16,512]{3,2,1,0:T(8,128)(2,1)S(1)} %get-tuple-element.183.rest_2_), channel_id=1, source_target_pairs={{0,2},{1,3},{2,0},{3,1},{4,6},{5,7},{6,4},{7,5},{8,10},{9,11},{10,... | collective-permute-start | bytes 983048 | tf_op jit(solution)/shard_map/ppermute | solution.py:864
  209.8 16.1 %collective-permute-start.20 = (bf16[4,5,16,512]{3,2,1,0:T(8,128)(2,1)S(1)}, bf16[4,5,16,512]{3,2,1,0:T(8,128)(2,1)S(1)}, u32[]{:S(2)}, u32[]{:S(2)}) collective-permute-start(bf16[4,5,16,512]{3,2,1,0:T(8,128)(2,1)S(1)} %get-tuple-element.184.rest_3_), channel_id=1, source_target_pairs={{0,4},{1,5},{2,6},{3,7},{4,0},{5,1},{6,2},{7,3},{8,12},{9,13},{10,... | collective-permute-start | bytes 983048 | tf_op jit(solution)/shard_map/ppermute | solution.py:864
  211.7 16.6 %collective-permute-start.21 = (bf16[4,5,16,512]{3,2,1,0:T(8,128)(2,1)S(1)}, bf16[4,5,16,512]{3,2,1,0:T(8,128)(2,1)}, u32[]{:S(2)}, u32[]{:S(2)}) collective-permute-start(bf16[4,5,16,512]{3,2,1,0:T(8,128)(2,1)S(1)} %get-tuple-element.185.rest_4_), channel_id=1, source_target_pairs={{0,6},{1,7},{2,4},{3,5},{4,2},{5,3},{6,0},{7,1},{8,14},{9,15},{10,... | collective-permute-start | bytes 983048 | tf_op jit(solution)/shard_map/ppermute | solution.py:864
  213.2 18.1 %collective-permute-start.32 = (bf16[1,9,16,512]{3,2,1,0:T(8,128)(2,1)}, bf16[1,9,16,512]{3,2,1,0:T(8,128)(2,1)S(1)}, u32[]{:S(2)}, u32[]{:S(2)}) collective-permute-start(bf16[1,9,16,512]{3,2,1,0:T(8,128)(2,1)} %copy-done.1), channel_id=1, source_target_pairs={{0,8},{1,9},{2,10},{3,11},{4,12},{5,13},{6,14},{7,15},{8,0},{9,1},... | collective-permute-start | bytes 442376 | tf_op jit(solution)/shard_map/ppermute | solution.py:864
  213.2 24.3 %collective-permute-start.33 = (bf16[1,9,16,512]{3,2,1,0:T(8,128)(2,1)S(1)}, bf16[1,9,16,512]{3,2,1,0:T(8,128)(2,1)S(1)}, u32[]{:S(2)}, u32[]{:S(2)}) collective-permute-start(bf16[1,9,16,512]{3,2,1,0:T(8,128)(2,1)S(1)} %get-tuple-element.176.rest_1_), channel_id=1, source_target_pairs={{0,16},{1,17},{2,18},{3,19},{4,20},{5,21},{6,22},{7,23},{8,24},{9,... | collective-permute-start | bytes 442376 | tf_op jit(solution)/shard_map/ppermute | solution.py:864
  214.6 15.5 %copy-start.15 = (bf16[4,5,16,512]{3,2,1,0:T(8,128)(2,1)S(1)}, bf16[4,5,16,512]{3,2,1,0:T(8,128)(2,1)}, u32[]{:S(2)}) copy-start(bf16[4,5,16,512]{3,2,1,0:T(8,128)(2,1)} %copy-done.14) | copy-start | bytes 983044
  218.3 19.3 %collective-permute-start.34 = (bf16[1,9,16,512]{3,2,1,0:T(8,128)(2,1)S(1)}, bf16[1,9,16,512]{3,2,1,0:T(8,128)(2,1)S(1)}, u32[]{:S(2)}, u32[]{:S(2)}) collective-permute-start(bf16[1,9,16,512]{3,2,1,0:T(8,128)(2,1)S(1)} %get-tuple-element.177.rest_2_), channel_id=1, source_target_pairs={{0,24},{1,25},{2,26},{3,27},{4,28},{5,29},{6,30},{7,31},{8,16},{9,... | collective-permute-start | bytes 442376 | tf_op jit(solution)/shard_map/ppermute | solution.py:864
  225.9 16.0 %collective-permute-start.23 = (bf16[4,3,16,512]{3,2,1,0:T(8,128)(2,1)S(1)}, bf16[4,3,16,512]{3,2,1,0:T(8,128)(2,1)S(1)}, u32[]{:S(2)}, u32[]{:S(2)}) collective-permute-start(bf16[4,3,16,512]{3,2,1,0:T(8,128)(2,1)S(1)} %get-tuple-element.194), channel_id=1, source_target_pairs={{0,2},{1,3},{2,0},{3,1},{4,6},{5,7},{6,4},{7,5},{8,10},{9,11},{10,... | collective-permute-start | bytes 589832 | tf_op jit(solution)/shard_map/ppermute | solution.py:864
  228.4 11.7 %collective-permute-start.24 = (bf16[4,3,16,512]{3,2,1,0:T(8,128)(2,1)S(1)}, bf16[4,3,16,512]{3,2,1,0:T(8,128)(2,1)S(1)}, u32[]{:S(2)}, u32[]{:S(2)}) collective-permute-start(bf16[4,3,16,512]{3,2,1,0:T(8,128)(2,1)S(1)} %get-tuple-element.202), channel_id=1, source_target_pairs={{0,4},{1,5},{2,6},{3,7},{4,0},{5,1},{6,2},{7,3},{8,12},{9,13},{10,... | collective-permute-start | bytes 589832 | tf_op jit(solution)/shard_map/ppermute | solution.py:864
  231.3 10.6 %collective-permute-start.25 = (bf16[4,3,16,512]{3,2,1,0:T(8,128)(2,1)S(1)}, bf16[4,3,16,512]{3,2,1,0:T(8,128)(2,1)S(1)}, u32[]{:S(2)}, u32[]{:S(2)}) collective-permute-start(bf16[4,3,16,512]{3,2,1,0:T(8,128)(2,1)S(1)} %get-tuple-element.203), channel_id=1, source_target_pairs={{0,6},{1,7},{2,4},{3,5},{4,2},{5,3},{6,0},{7,1},{8,14},{9,15},{10,... | collective-permute-start | bytes 589832 | tf_op jit(solution)/shard_map/ppermute | solution.py:864
  231.4 8.0 %copy-start.17 = (bf16[1,9,16,512]{3,2,1,0:T(8,128)(2,1)S(1)}, bf16[1,9,16,512]{3,2,1,0:T(8,128)(2,1)}, u32[]{:S(2)}) copy-start(bf16[1,9,16,512]{3,2,1,0:T(8,128)(2,1)} %copy-done.16) | copy-start | bytes 442372
  237.5 8.3 %collective-permute-start.30 = (bf16[1,5,16,512]{3,2,1,0:T(8,128)(2,1)S(1)}, bf16[1,5,16,512]{3,2,1,0:T(8,128)(2,1)S(1)}, u32[]{:S(2)}, u32[]{:S(2)}) collective-permute-start(bf16[1,5,16,512]{3,2,1,0:T(8,128)(2,1)S(1)} %get-tuple-element.199.rest_1_), channel_id=1, source_target_pairs={{0,16},{1,17},{2,18},{3,19},{4,20},{5,21},{6,22},{7,23},{8,24},{9,... | collective-permute-start | bytes 245768 | tf_op jit(solution)/shard_map/ppermute | solution.py:864
  237.6 9.6 %collective-permute-start.31 = (bf16[1,5,16,512]{3,2,1,0:T(8,128)(2,1)S(1)}, bf16[1,5,16,512]{3,2,1,0:T(8,128)(2,1)S(1)}, u32[]{:S(2)}, u32[]{:S(2)}) collective-permute-start(bf16[1,5,16,512]{3,2,1,0:T(8,128)(2,1)S(1)} %get-tuple-element.200.rest_2_), channel_id=1, source_target_pairs={{0,24},{1,25},{2,26},{3,27},{4,28},{5,29},{6,30},{7,31},{8,16},{9,... | collective-permute-start | bytes 245768 | tf_op jit(solution)/shard_map/ppermute | solution.py:864
  240.1 7.1 %collective-permute-start.29 = (bf16[1,5,16,512]{3,2,1,0:T(8,128)(2,1)S(1)}, bf16[1,5,16,512]{3,2,1,0:T(8,128)(2,1)S(1)}, u32[]{:S(2)}, u32[]{:S(2)}) collective-permute-start(bf16[1,5,16,512]{3,2,1,0:T(8,128)(2,1)S(1)} %get-tuple-element.198.rest_0_), channel_id=1, source_target_pairs={{0,8},{1,9},{2,10},{3,11},{4,12},{5,13},{6,14},{7,15},{8,0},{9,1},... | collective-permute-start | bytes 245768 | tf_op jit(solution)/shard_map/ppermute | solution.py:864
  242.0 6.5 %collective-permute-start.26 = (bf16[1,3,16,512]{3,2,1,0:T(8,128)(2,1)S(1)}, bf16[1,3,16,512]{3,2,1,0:T(8,128)(2,1)S(1)}, u32[]{:S(2)}, u32[]{:S(2)}) collective-permute-start(bf16[1,3,16,512]{3,2,1,0:T(8,128)(2,1)S(1)} %get-tuple-element.205), channel_id=1, source_target_pairs={{0,8},{1,9},{2,10},{3,11},{4,12},{5,13},{6,14},{7,15},{8,0},{9,1},... | collective-permute-start | bytes 147464 | tf_op jit(solution)/shard_map/ppermute | solution.py:864
  242.3 6.5 %collective-permute-start.27 = (bf16[1,3,16,512]{3,2,1,0:T(8,128)(2,1)S(1)}, bf16[1,3,16,512]{3,2,1,0:T(8,128)(2,1)S(1)}, u32[]{:S(2)}, u32[]{:S(2)}) collective-permute-start(bf16[1,3,16,512]{3,2,1,0:T(8,128)(2,1)S(1)} %get-tuple-element.206), channel_id=1, source_target_pairs={{0,16},{1,17},{2,18},{3,19},{4,20},{5,21},{6,22},{7,23},{8,24},{9,... | collective-permute-start | bytes 147464 | tf_op jit(solution)/shard_map/ppermute | solution.py:864
  245.9 5.9 %collective-permute-start.28 = (bf16[1,3,16,512]{3,2,1,0:T(8,128)(2,1)S(1)}, bf16[1,3,16,512]{3,2,1,0:T(8,128)(2,1)S(1)}, u32[]{:S(2)}, u32[]{:S(2)}) collective-permute-start(bf16[1,3,16,512]{3,2,1,0:T(8,128)(2,1)S(1)} %get-tuple-element.207), channel_id=1, source_target_pairs={{0,24},{1,25},{2,26},{3,27},{4,28},{5,29},{6,30},{7,31},{8,16},{9,... | collective-permute-start | bytes 147464 | tf_op jit(solution)/shard_map/ppermute | solution.py:864
  (10 other events, 13.0 us)
Sparse Core Ops, SparseCore 0:
  20.6 66.4 all-gather.1
